TPU v7x, 32 devices: a whole 2x2x4 slice. The times are simulated.
32 devices in a mesh: row: 4 (over z), col: 8 (over y, x, core).
Axes of the slice: x: 2, y: 2, z: 4, core: 2. Of those that a mesh axis runs over, the one named last changes fastest.
Arguments:
- lensed_picture_vectors: bfloat16 [6144, 512], P(('row', 'col')), may hold values from -6 to 6
- theta_feature_vectors: bfloat16 [6144, 512], P(('row', 'col')), may hold values from -6 to 6
- prior_domain_label: int32 [6144], P(('row', 'col')), may hold values from 0 to 63, as said below
- matched_theta_index: int32 [6144], P(('row', 'col')), may hold values from 0 to 6143, each once
- affinity_gain: float32 [1], replicated, may hold values from 5 to 15
- affinity_shift: float32 [1], replicated, may hold values from -4 to -1
Outputs:
- loss: float32 [1], replicated
- grad_data: float32 [6144, 512], P(('row', 'col'))
- grad_param: float32 [6144, 512], P(('row', 'col'))
Inputs may be any that keep to these rules, and one draw needn't show every extreme that they name: `matched_theta_index`: a permutation of the pair indices. `prior_domain_label`: region 0 is shared by a share of the pairs that differs between blocks of 192 pairs.
All inputs are finite; a program needn't handle non-finite values.
Results may differ from a plain program's by a relative error of at most 0.00086.
Values may be sent and summed in bfloat16 or wider, within the bound.
No kernel may reach another device: no remote copies, remote signals or barrier semaphores. Data moves between devices by JAX's collectives and lax.ppermute only.
A program may use at most 64 MiB of HBM per device.

v0:
```python
import jax
import jax.numpy as jnp
from jax import lax
from jax.sharding import PartitionSpec as P


def normalize(embed):
    full = embed.astype(jnp.float32)
    scale = lax.rsqrt(jnp.mean(full * full, axis=-1, keepdims=True) + 1e-06)
    full = full * scale
    return (full, scale, full.astype(jnp.bfloat16))


def backward_norm(dnorm, full, scale):
    return scale * (dnorm - full * jnp.mean(dnorm * full, axis=-1, keepdims=True))


def tile_terms(
    source_count,
    source_region,
    source_subset,
    target_count,
    target_region,
    target_overall,
    sharpness_coefficient,
    shift_amount,
):
    similarity_value = jnp.dot(source_count, target_count.T, preferred_element_type=jnp.float32)
    pair_affinity = sharpness_coefficient * similarity_value + shift_amount
    positive = source_subset[:, None] == target_overall[None, :]
    retain_mask = positive | (source_region[:, None] != target_region[None, :])
    polarity_value = jnp.where(positive, 1.0, -1.0).astype(jnp.float32)
    partial_loss = jnp.sum(
        jnp.where(retain_mask, -jax.nn.log_sigmoid(polarity_value * pair_affinity), 0.0)
    )
    pairwise_slope = (
        jnp.where(
            retain_mask, -polarity_value * jax.nn.sigmoid(-polarity_value * pair_affinity), 0.0
        )
        * sharpness_coefficient
    ).astype(jnp.bfloat16)
    image_embed_gradient = jnp.dot(pairwise_slope, target_count, preferred_element_type=jnp.float32)
    param_d = lax.dot_general(
        pairwise_slope, source_count, (((0,), (0,)), ((), ())), preferred_element_type=jnp.float32
    )
    return (partial_loss, image_embed_gradient, param_d)


def on_device(
    lensed_picture_vectors,
    theta_feature_vectors,
    prior_domain_label,
    matched_theta_index,
    affinity_gain,
    affinity_shift,
):
    shard = lensed_picture_vectors.shape[0]
    hidden_size = lensed_picture_vectors.shape[1]
    col_count = lax.axis_size("col")
    row_count = lax.axis_size("row")
    col_index = lax.axis_index("col")
    sharpness_coefficient = affinity_gain[0] / hidden_size
    shift_amount = affinity_shift[0]
    data_full, data_scale, data_norm = normalize(lensed_picture_vectors)
    param_full, param_scale, param_norm = normalize(theta_feature_vectors)
    col_total = shard * row_count
    target_count, target_region = (
        lax.all_gather(param_norm, "row", axis=0, tiled=True),
        lax.all_gather(prior_domain_label, "row", axis=0, tiled=True),
    )
    place = jnp.arange(col_total, dtype=jnp.int32)
    target_overall = place // shard * (shard * col_count) + col_index * shard + place % shard
    source_count = lax.all_gather(data_norm, "col", axis=0, tiled=True)
    source_region = lax.all_gather(prior_domain_label, "col", axis=0, tiled=True)
    source_subset = lax.all_gather(matched_theta_index, "col", axis=0, tiled=True)
    partial_loss, image_embed_gradient, param_d = tile_terms(
        source_count,
        source_region,
        source_subset,
        target_count,
        target_region,
        target_overall,
        sharpness_coefficient,
        shift_amount,
    )
    data_dnorm = lax.psum_scatter(image_embed_gradient, "col", scatter_dimension=0, tiled=True)
    param_dnorm = lax.psum_scatter(param_d, "row", scatter_dimension=0, tiled=True)
    total = lax.psum(partial_loss, ("row", "col"))
    pair_total = shard * row_count * col_count
    loss = (total / (pair_total * pair_total)).reshape(1)
    grad_data = backward_norm(data_dnorm, data_full, data_scale)
    grad_param = backward_norm(param_dnorm, param_full, param_scale)
    return (loss, grad_data, grad_param)


def solution(mesh):
    placed = (
        P(("row", "col"), None),
        P(("row", "col"), None),
        P(("row", "col")),
        P(("row", "col")),
        P(),
        P(),
    )
    return jax.shard_map(
        on_device,
        mesh=mesh,
        in_specs=placed,
        out_specs=(P(), P(("row", "col"), None), P(("row", "col"), None)),
        check_vma=False,
    )
```

profile of v0, /device:TPU:0, one launch (start us, length us, event | category | flops | bytes accessed | tf_op | source)
XLA Modules:
  0.0 175.6 jit_solution(1884486491031504147)
XLA Ops:
  7.2 0.0 all-gather.2.cloned.1.call-start
  7.2 1.0 fusion.19
  8.3 1.7 fusion.15
  10.0 0.0 all-gather.2.cloned.1.call-update
  10.0 0.0 reduce-scatter.5.cloned.1.call-start
  10.1 1.2 dynamic-slice
  11.3 1.2 dynamic-slice.2
  15.1 0.9 dynamic-update-slice
  16.0 0.9 dynamic-update-slice.1
  16.9 0.9 dynamic-update-slice.2
  17.8 9.9 %all-reduce.2 = s32[768]{0:T(1024)S(1)} all-reduce(s32[768]{0:T(1024)S(1)} %dynamic-update-slice.2), channel_id=1, replica_groups=mesh['row'=4,'col'=8] {'row'}, use_global_device_ids=true, to_apply=%add.2 | all-reduce | flops 768 | bytes 6144
  27.7 22.5 %all-reduce.3 = (s32[1536]{0:T(1024)S(1)}, s32[1536]{0:T(1024)S(1)}) all-reduce(s32[1536]{0:T(1024)S(1)} %dynamic-update-slice.1, s32[1536]{0:T(1024)S(1)} %dynamic-update-slice), channel_id=1, replica_groups=mesh['row'=4,'col'=8] {'col'}, use_global_device_ids=true, to_apply=%add.1 | all-reduce | flops 3072 | bytes 24576
  50.2 1.0 fusion.23
  51.2 1.0 fusion.12
  52.3 17.6 %all_gather.19 = bf16[768,512]{1,0:T(8,128)(2,1)S(1)} all-gather(bf16[192,512]{1,0:T(8,128)(2,1)S(1)} %fusion.12), channel_id=1, replica_groups=mesh['row'=4,'col'=8] {'row'}, dimensions={0}, use_global_device_ids=true | all-gather | bytes 983040 | tf_op jit(solution)/shard_map/all_gather | solution.py:68
  69.8 0.0 all-gather.2.cloned.1.call-done
  69.8 0.0 copy-start.2
  69.8 8.5 %multiply_convert_fusion = (bf16[1536,768]{1,0:T(8,128)(2,1)S(1)}, f32[]{:T(128)}) fusion(f32[]{:T(128)} %bitcast.11, f32[]{:T(128)} %bitcast.2, s32[768]{0:T(1024)S(1)} %all-reduce.2, s32[768]{0:T(1024)S(1)} %fusion.32, s32[1536]{0:T(1024)S(1)} %get-tuple-element.3, s32[1536]{0:T(1024)S(1)} %get-tuple-element.4, ...), kind=kOutput, calls=%fused_computation.14 | convolution fusion | flops 1237450752 | bytes 4737036 | tf_op jit(solution)/shard_map/dot_general | solution.py:28
  78.4 0.0 copy-done.2
  78.4 2.5 %fusion.35 = f32[768,512]{1,0:T(8,128)} fusion(bf16[1536,768]{1,0:T(8,128)(2,1)S(1)} %get-tuple-element.5, bf16[1536,512]{1,0:T(8,128)(2,1)S(1)} %copy-done.2), kind=kOutput, calls=%fused_computation.53 | convolution fusion | flops 1207959552 | bytes 5505024 | tf_op jit(solution)/shard_map/dot_general | solution.py:43
  80.9 0.0 reduce-scatter.5.cloned.1.call-update
  81.0 0.0 reduce-scatter.3.cloned.1.call-start
  81.0 3.1 %fusion.34 = f32[1536,512]{1,0:T(8,128)} fusion(bf16[1536,768]{1,0:T(8,128)(2,1)S(1)} %get-tuple-element.5, bf16[768,512]{1,0:T(8,128)(2,1)S(1)} %all_gather.19), kind=kOutput, calls=%fused_computation.52 | convolution fusion | flops 1207959552 | bytes 6291456 | tf_op jit(solution)/shard_map/dot_general | solution.py:42
  84.1 0.0 copy-start
  84.1 0.0 copy-start.1
  84.1 0.0 reduce-scatter.3.cloned.1.call-update
  84.1 39.9 %psum.7 = f32[]{:T(128)} all-reduce(f32[]{:T(128)} %get-tuple-element.6), channel_id=1, replica_groups=mesh['row'=4,'col'=8] {'row','col'}, use_global_device_ids=true, to_apply=%region_3.4 | all-reduce | flops 1 | bytes 8 | tf_op jit(solution)/shard_map/psum | solution.py:88
  124.6 0.0 reduce-scatter.5.cloned.1.call-done
  124.6 0.0 copy-done
  124.6 1.2 fusion.20
  125.9 1.9 %fusion.22 = f32[192,512]{1,0:T(8,128)} fusion(f32[192,512]{1,0:T(8,128)} %reduce-scatter.5.cloned.1.call-done, bf16[192,512]{1,0:T(8,128)(2,1)S(1)} %copy-done, f32[192]{0:T(256)S(1)} %broadcast_multiply_fusion, f32[192]{0:T(256)S(1)} %add_rsqrt_fusion), kind=kLoop, calls=%fused_computation.32 | loop fusion | flops 491520 | bytes 984576 | tf_op jit(solution)/shard_map/mul | solution.py:15
  127.8 37.0 %reduce-scatter.3.cloned.1.call-done = f32[192,512]{1,0:T(8,128)} async-done(((f32[1536,512]{1,0:T(8,128)}), f32[192,512]{1,0:T(8,128)}) %reduce-scatter.3.cloned.1.call-update) | async-done | bytes 393232 | tf_op jit(solution)/shard_map/reduce_scatter | solution.py:86
  164.8 0.0 copy-done.1
  164.8 1.2 fusion.16
  166.0 1.9 %fusion.18 = f32[192,512]{1,0:T(8,128)} fusion(f32[192,512]{1,0:T(8,128)} %reduce-scatter.3.cloned.1.call-done, bf16[192,512]{1,0:T(8,128)(2,1)S(1)} %copy-done.1, f32[192]{0:T(256)S(1)} %broadcast_multiply_fusion.1, f32[192]{0:T(256)S(1)} %add_rsqrt_fusion.1), kind=kLoop, calls=%fused_computation.28 | loop fusion | flops 491520 | bytes 984576 | tf_op jit(solution)/shard_map/mul | solution.py:15
  (8 shorter events, 0.0 us)
Async XLA Ops:
  7.2 62.7 %all-gather.2.cloned.1.call-start = ((), (), s32[]{:S(2)}) async-start(), calls=%async_computation.2 | async-start | bytes 1769472 | tf_op jit(solution)/shard_map/all_gather | solution.py:73
  10.0 114.6 %reduce-scatter.5.cloned.1.call-start = ((), (), s32[]{:S(2)}) async-start(), calls=%async_computation.4 | async-start | bytes 1966080 | tf_op jit(solution)/shard_map/reduce_scatter | solution.py:87
  69.8 8.5 %copy-start.2 = (bf16[1536,512]{1,0:T(8,128)(2,1)S(1)}, bf16[1536,512]{1,0:T(8,128)(2,1)}, u32[]{:S(2)}) copy-start(bf16[1536,512]{1,0:T(8,128)(2,1)} %all-gather.2.cloned.1.call-done) | copy-start | bytes 4718596
  81.0 83.8 %reduce-scatter.3.cloned.1.call-start = ((), (), s32[]{:S(2)}) async-start(), calls=%async_computation.3 | async-start | bytes 3538944 | tf_op jit(solution)/shard_map/reduce_scatter | solution.py:86
  84.1 40.6 %copy-start = (bf16[192,512]{1,0:T(8,128)(2,1)S(1)}, bf16[192,512]{1,0:T(8,128)(2,1)}, u32[]{:S(2)}) copy-start(bf16[192,512]{1,0:T(8,128)(2,1)} %param.7) | copy-start | bytes 589828
  84.1 80.7 %copy-start.1 = (bf16[192,512]{1,0:T(8,128)(2,1)S(1)}, bf16[192,512]{1,0:T(8,128)(2,1)}, u32[]{:S(2)}) copy-start(bf16[192,512]{1,0:T(8,128)(2,1)} %param.6) | copy-start | bytes 589828
Sparse Core Ops, SparseCore 0:
  10.5 28.4 all-gather.1
  81.1 34.9 reduce-scatter.4
  119.5 45.2 reduce-scatter.2
where the time goes:
time: 176 us
  blocking collectives  89.8 us (51%)
  waiting for transfers between devices  37.1 us (21%)
  between operations  18.2 us (10%)
  matrix products  14.1 us (8%)
  other arithmetic  11.1 us (6%)
  local copies, waits for them, and re-layouts  5.13 us (3%)
    psum x1, blocking collectives, on_device(): total = lax.psum(partial_loss, ('row', 'col'))  39.9 us
    reduce_scatter x1, waiting for transfers between devices, on_device(): lax.psum_scatter(image_embed_gradient, 'col', scatter_dimension=0, tiled=...  37 us
    unnamed x2, blocking collectives  32.4 us
    all_gather x1, blocking collectives, on_device(): lax.all_gather(param_norm, 'row', axis=0, tiled=True)  17.6 us
    dot_general x1, matrix products, tile_terms(): jnp.dot(source_count, target_count.T, preferred_element_type=jnp.float32)  8.54 us
    unnamed x13, local copies, waits for them, and re-layouts  5.13 us
    mul x2, other arithmetic, backward_norm(): scale * (dnorm - full * jnp.mean(dnorm * full, axis=-1, keepdims=True))  3.83 us
  transfers between devices with their start and end apart: 3, of which 1 were waited for; matrix products, arithmetic and copies ran while one was open for 8% of the time, Pallas kernels for 0%

commit v1 on v0

v1 whole, which is shorter than its diff:
```python
import functools

import jax
import jax.numpy as jnp
from jax import lax
from jax.experimental import pallas as pl
from jax.experimental.pallas import tpu as pltpu
from jax.sharding import PartitionSpec as P

AUX = 16
FULL = 32000.0
LOG2E = 1.4426950408889634
LN2 = 0.6931471805599453
VMEM = pl.BlockSpec(memory_space=pltpu.VMEM)
SMEM = pl.BlockSpec(memory_space=pltpu.SMEM)
F32 = jnp.float32
BF16 = jnp.bfloat16
I16 = jnp.int16


def call(body, out_shape, in_specs, scratch=(), aliases=None, vmem=24 * 2**20):
    inner = pl.pallas_call(
        body,
        out_shape=jax.tree.map(lambda s: pltpu.VMEM(s.shape, s.dtype), out_shape),
        in_specs=in_specs,
        input_output_aliases=aliases or {},
        cost_estimate=pl.CostEstimate(flops=1, bytes_accessed=1, transcendentals=0),
        out_specs=jax.tree.map(lambda _: VMEM, out_shape),
        scratch_shapes=list(scratch),
        compiler_params=pltpu.CompilerParams(vmem_limit_bytes=vmem),
    )

    def run(*args):
        args = [
            x if s is SMEM else pltpu.with_memory_space_constraint(x, s.memory_space)
            for x, s in zip(args, in_specs)
        ]
        return inner(*args)

    return run


def normalize(embed):
    full = embed.astype(F32)
    scale = lax.rsqrt(jnp.mean(full * full, axis=-1, keepdims=True) + 1e-06)
    return full * scale, scale


def pack_kernel(data_hbm, param_hbm, region_hbm, partner_hbm, data_msg, param_msg, *scratch):
    data, param, region, partner, aux, sems = scratch
    rows = data.shape[0]
    pairs = ((param_hbm, param), (region_hbm, region), (partner_hbm, partner), (data_hbm, data))
    copies = [pltpu.make_async_copy(a, b, sems.at[i]) for i, (a, b) in enumerate(pairs)]
    for copy in copies:
        copy.start()
    aux[...] = jnp.zeros_like(aux)
    for copy in copies:
        copy.wait()
    index = partner[...]
    aux[0:1, 0:rows] = region[...].astype(F32)
    aux[1:2, 0:rows] = (index >> 8).astype(F32)
    aux[2:3, 0:rows] = (index & 255).astype(F32)
    side = aux[...].astype(BF16)
    for raw, msg in ((param, param_msg), (data, data_msg)):
        msg[pl.ds(rows, AUX), :] = side
        msg[pl.ds(0, rows), :] = normalize(raw[...])[0].astype(BF16)


def encode(value, ref, start):
    rows, width = value.shape
    parts = value.reshape(rows // AUX, AUX, width)
    top = jnp.max(jnp.abs(parts), axis=0)
    power = jnp.ceil(jnp.log2(jnp.maximum(top, 1e-30)) * 256.0)
    unit = jnp.exp2(power * (-1.0 / 256.0)) * FULL
    coded = ((parts * unit[None] + 32768.5).astype(jnp.int32) - 32768).astype(I16)
    ref[pl.ds(start, rows), :] = coded.reshape(rows, width)
    ref[pl.ds(start + rows, AUX), :] = power.astype(jnp.int32).astype(I16)


def decode(ref, start, rows):
    width = ref.shape[-1]
    coded = ref[pl.ds(start, rows), :].astype(F32).reshape(rows // AUX, AUX, width)
    power = ref[pl.ds(start + rows, AUX), :].astype(F32)
    unit = jnp.exp2(power * (1.0 / 256.0)) * (1.0 / FULL)
    return (coded * unit[None]).reshape(rows, width)


def log1p(t):
    u = 1.0 + t
    small = t * (1.0 - t * (0.5 - t * (1.0 / 3.0)))
    return jnp.where(t < 0.01, small, jnp.log(u))


LAST = (((1,), (1,)), ((), ()))
FIRST = (((0,), (0,)), ((), ()))


def load_data(msgs, data, side, rows):
    for i, msg in enumerate(msgs):
        at = pl.ds(i * rows, rows)
        data[at, :] = msg[pl.ds(0, rows), :]
        aux = msg[pl.ds(rows, AUX), :].astype(F32)[:, :rows]
        side[0:1, at] = aux[0:1]
        side[1:2, at] = aux[1:2] * 256.0 + aux[2:3]


def side_columns(msg, base, rows):
    square = (rows + 127) // 128 * 128
    lane = lax.broadcasted_iota(jnp.int32, (rows, square), 1)
    eye = (lax.broadcasted_iota(jnp.int32, (rows, square), 0) == lane).astype(F32).astype(BF16)
    aux = msg[pl.ds(rows, AUX), :][:, :square]
    region = lax.dot_general(eye, aux, LAST, preferred_element_type=F32)[:, 0:1]
    place = lax.broadcasted_iota(jnp.int32, (rows, 1), 0) + base
    return region, place.astype(F32)


def tile(block, columns, data, side, coef, shift):
    region_col, index_col = columns
    rows, cols = block.shape[0], data.shape[0]
    dots = lax.dot_general(block, data[...], LAST, preferred_element_type=F32)
    positive = index_col == side[1:2, :]
    keep = jnp.logical_or(positive, region_col != side[0:1, :])
    x = dots * (coef * LOG2E) + shift * LOG2E
    x = jnp.where(positive, -x, x)
    t = jnp.where(keep, jnp.exp2(x), 0.0)
    slope = t / (1.0 + t)
    grad = (jnp.where(positive, -slope, slope) * coef).astype(BF16)
    q = t.reshape(4, rows // 4, cols)
    t01 = q[0] + q[1] * (1.0 + q[0])
    t23 = q[2] + q[3] * (1.0 + q[2])
    terms = log1p(t01 + t23 * (1.0 + t01)).reshape(rows // 32, 8, cols)
    terms = jnp.sum(terms, axis=0)
    loss = terms[:, 0:128]
    for k in range(128, cols, 128):
        loss = loss + terms[:, k : k + 128]
    return grad, loss


def early_kernel(rows, n, p_n, *refs):
    msgs, params, (base, coef) = refs[:n], refs[n : n + p_n], refs[n + p_n : n + p_n + 2]
    data, side, acc, parts, loss_out = refs[n + p_n + 2 :]
    load_data(msgs, data, side, rows)
    loss = jnp.zeros((8, 128), F32)
    for s in range(p_n):
        block = params[s][pl.ds(0, rows), :]
        columns = side_columns(params[s], base[s], rows)
        grad, term = tile(block, columns, data, side, coef[0], coef[1])
        loss = loss + term
        parts[pl.ds(s * rows, rows), :] = jnp.dot(grad, data[...], preferred_element_type=F32)
        d_part = lax.dot_general(grad, block, FIRST, preferred_element_type=F32)
        acc[...] = d_part if s == 0 else acc[...] + d_part
    loss_out[...] = loss


def middle_kernel(rows, n, p_n, m_n, *refs):
    msgs, params = refs[:n], refs[n : n + p_n + m_n]
    data0, side0, acc0, parts_in, loss_in, base, coef = refs[n + p_n + m_n : n + p_n + m_n + 7]
    data, side, acc0_out, acc, parts, loss_out = refs[n + p_n + m_n + 7 :]
    load_data(msgs, data, side, rows)
    loss = loss_in[...]
    for s in range(p_n + m_n):
        at = pl.ds(s * rows, rows)
        block = params[s][pl.ds(0, rows), :]
        columns = side_columns(params[s], base[s], rows)
        grad, term = tile(block, columns, data, side, coef[0], coef[1])
        loss = loss + term
        part = jnp.dot(grad, data[...], preferred_element_type=F32)
        d_part = lax.dot_general(grad, block, FIRST, preferred_element_type=F32)
        acc[...] = d_part if s == 0 else acc[...] + d_part
        if s < p_n:
            parts[at, :] = parts_in[at, :] + part
            continue
        grad, term = tile(block, columns, data0, side0, coef[0], coef[1])
        loss = loss + term
        parts[at, :] = part + jnp.dot(grad, data0[...], preferred_element_type=F32)
        d_part = lax.dot_general(grad, block, FIRST, preferred_element_type=F32)
        acc0_out[...] = (acc0 if s == p_n else acc0_out)[...] + d_part
    if m_n == 0:
        acc0_out[...] = acc0[...]
    loss_out[...] = loss


def late_kernel(rows, n, l_n, ready, *refs):
    params = refs[:l_n]
    data0, side0, acc0, data1, side1, acc1, parts, loss_in, base, coef = refs[l_n : l_n + 10]
    outs = refs[l_n + 10 :]
    keep_d, send_d, loss_out = outs[:3]
    send_p = outs[3:]
    loss = loss_in[...]
    half = n // 2
    for k, s in enumerate(ready):
        encode(parts[pl.ds(s * rows, rows), :], send_p[k], 0)
    for s in range(l_n):
        block = params[s][pl.ds(0, rows), :]
        columns = side_columns(params[s], base[s], rows)
        total = None
        for h, (data, side, acc) in enumerate(((data0, side0, acc0), (data1, side1, acc1))):
            grad, term = tile(block, columns, data, side, coef[0], coef[1])
            loss = loss + term
            part = jnp.dot(grad, data[...], preferred_element_type=F32)
            total = part if total is None else total + part
            d_part = acc[...] + lax.dot_general(grad, block, FIRST, preferred_element_type=F32)
            if s < l_n - 1:
                acc[...] = d_part
                continue
            for i in range(half):
                keep_d[pl.ds((2 * i + h) * rows, rows), :] = d_part[i * rows : (i + 1) * rows]
                at = half + i
                encode(d_part[at * rows : (at + 1) * rows], send_d, (2 * i + h) * (rows + AUX))
        encode(total, send_p[len(ready) + s], 0)
    loss_out[...] = loss


def emit_kernel(rows, plan, *refs):
    n_arrays = max(max([b] + [a for a, _ in parts]) for b, _, parts in plan) + 1
    arrays, loss, got, outs = refs[:n_arrays], refs[n_arrays], refs[n_arrays + 1], refs[n_arrays + 2 :]
    outs[-1][...] = loss[...] + got[...]
    for out, (b, start, parts) in zip(outs, plan):
        total = arrays[b][pl.ds(start * rows, rows), :]
        for a, i in parts:
            total = total + decode(arrays[a], i * (rows + AUX), rows)
        encode(total, out, 0)


def finish_kernel(rows, plan, pairs, raw_ref, *refs):
    start, parts, arrays = plan
    if pairs:
        terms, out_ref, loss_ref = refs[arrays:-2], refs[-2], refs[-1]
        loss_ref[...] = jnp.sum(sum([t[...] for t in terms]), keepdims=True) / (pairs * pairs)
    else:
        out_ref = refs[-1]
    full, scale = normalize(raw_ref[...])
    dnorm = refs[0][pl.ds(start * rows, rows), :]
    for a, i in parts:
        dnorm = dnorm + decode(refs[a], i * (rows + AUX), rows)
    out_ref[...] = scale * (dnorm - full * jnp.mean(dnorm * full, axis=-1, keepdims=True))


def combine(bits):
    masks = [0]
    for bit in bits:
        masks += [m ^ bit for m in masks]
    return masks


def on_device(core, bits_data, bits_param, sizes, data, param, region, partner, gain, shift):
    rows, width = data.shape
    msg = rows + AUX
    devices = sizes["row"] * sizes["col"]
    shape = jax.ShapeDtypeStruct

    def swap(x, mask):
        return lax.ppermute(x, ("row", "col"), [(i, i ^ mask) for i in range(devices)])

    data_msg, param_msg = call(
        pack_kernel,
        [shape((msg, width), BF16)] * 2,
        [pl.BlockSpec(memory_space=pltpu.HBM)] * 4,
        [
            pltpu.VMEM((rows, width), BF16),
            pltpu.VMEM((rows, width), BF16),
            pltpu.VMEM((1, rows), jnp.int32),
            pltpu.VMEM((1, rows), jnp.int32),
            pltpu.VMEM((AUX, width), F32),
            pltpu.SemaphoreType.DMA((4,)),
        ],
    )(data, param, region.reshape(1, rows), partner.reshape(1, rows))
    held_p, masks_p = [param_msg], [0]
    held_d = [data_msg]
    for k in range(max(len(bits_data), len(bits_param))):
        if k < len(bits_param):
            held_p += [swap(x, bits_param[k]) for x in held_p]
            masks_p += [m ^ bits_param[k] for m in masks_p]
        if k < len(bits_data):
            held_d += [swap(x, bits_data[k]) for x in held_d]
    held_d = [held_d, [swap(x, core) for x in held_d]]
    me = lax.axis_index("row") * sizes["col"] + lax.axis_index("col")
    coef = jnp.stack([gain[0] / width, shift[0]])
    n_own, n_param = len(held_d[0]), len(held_p)
    halves = [[x for side in held_d for x in side[h::2]] for h in (0, 1)]
    n = n_own
    cols = n * rows
    late = [i for i in range(n_param) if i == n_param - 1]
    early = [i for i in range(n_param) if i not in late and not i & 1]
    middle = [i for i in range(n_param) if i not in late and i & 1]
    order = early + middle
    base = {i: (me ^ masks_p[i]) * rows for i in range(n_param)}
    bases = lambda group: jnp.stack([base[i] for i in group]).astype(jnp.int32)
    data0, side0, acc0, parts, loss = call(
        functools.partial(early_kernel, rows, n, len(early)),
        [
            shape((cols, width), BF16),
            shape((8, cols), F32),
            shape((cols, width), F32),
            shape((len(early) * rows, width), F32),
            shape((8, 128), F32),
        ],
        [VMEM] * (n + len(early)) + [SMEM] * 2,
    )(*halves[0], *[held_p[i] for i in early], bases(early), coef)
    data1, side1, acc0, acc1, parts, loss = call(
        functools.partial(middle_kernel, rows, n, len(early), len(middle)),
        [
            shape((cols, width), BF16),
            shape((8, cols), F32),
            shape((cols, width), F32),
            shape((cols, width), F32),
            shape((len(order) * rows, width), F32),
            shape((8, 128), F32),
        ],
        [VMEM] * (n + len(order) + 5) + [SMEM] * 2,
    )(
        *halves[1], *[held_p[i] for i in order], data0, side0, acc0, parts, loss, bases(order), coef
    )
    top = n_param // 2
    ready = [k for k, i in enumerate(order) if i >= top]
    sent = [order[k] for k in ready] + late
    keep_d, send_d, loss, *send_p = call(
        functools.partial(late_kernel, rows, n, len(late), ready),
        [
            shape((n * rows, width), F32),
            shape((n * msg, width), I16),
            shape((8, 128), F32),
            *[shape((msg, width), I16)] * len(sent),
        ],
        [VMEM] * (len(late) + 8) + [SMEM] * 2,
    )(
        *[held_p[i] for i in late],
        data0, side0, acc0, data1, side1, acc1, parts, loss, bases(late), coef,
    )
    loss_steps = [core] + bits_data[:0:-1] + bits_param[:0:-1] + bits_data[:1] + bits_param[:1]
    pending = [swap(loss, loss_steps.pop(0))]

    def emit(items):
        nonlocal loss
        arrays = []

        def slot(x):
            for i, y in enumerate(arrays):
                if x is y:
                    return i
            arrays.append(x)
            return len(arrays) - 1

        plan = [(slot(b), at, [(slot(x), i) for x, i in parts]) for b, at, parts in items]
        *msgs, loss = call(
            functools.partial(emit_kernel, rows, plan),
            [shape((msg, width), I16)] * len(items) + [shape((8, 128), F32)],
            [VMEM] * (len(arrays) + 2),
        )(*arrays, loss, pending.pop())
        if len(loss_steps) > 2 or emits[0] > 1:
            pending.append(swap(loss, loss_steps.pop(0)))
        emits[0] -= 1
        return msgs

    got = swap(send_d, core)
    items_d = [(keep_d, i, [(got, i)]) for i in range(n_own)]
    items_p = [(parts, order.index(i), []) for i in range(top)]
    got = {i: swap(x, bits_param[-1]) for i, x in zip(sent, send_p)}
    for i in range(top):
        items_p[i][2].append((got[i + top], 0))
    left_d, left_p = bits_data[::-1], bits_param[-2::-1]
    emits = [len(left_d) + len(left_p)]
    while left_d or left_p:
        for items, left in ((items_d, left_d), (items_p, left_p)):
            if left:
                step, half = left.pop(0), len(items) // 2
                for i, x in enumerate(emit(items[half:])):
                    items[i][2].append((swap(x, step), 0))
                del items[half:]
    while len(loss_steps) > 2:
        loss = loss + pending.pop()
        pending.append(swap(loss, loss_steps.pop(0)))
    if pending:
        loss = loss + pending.pop()
    terms = [loss] + [swap(loss, m) for m in combine(loss_steps)[1:]]

    def finish(raw, item, terms=(), pairs=0):
        arrays, at, parts = [item[0]], item[1], []
        for x, i in item[2]:
            arrays.append(x)
            parts.append((len(arrays) - 1, i))
        return call(
            functools.partial(finish_kernel, rows, (at, parts, len(arrays)), pairs),
            [shape((rows, width), F32)] + [shape((1, 1), F32)] * bool(pairs),
            [VMEM] * (1 + len(arrays) + len(terms)),
        )(raw, *arrays, *terms)

    (grad_param,) = finish(param, items_p[0])
    grad_data, loss = finish(data, items_d[0], terms, rows * devices)
    return loss.reshape(1), grad_data, grad_param


def solution(mesh):
    sizes = dict(mesh.shape)
    columns = sizes["col"]
    col_bits = [1 << k for k in range(columns.bit_length() - 1)]
    row_bits = [columns << k for k in range(sizes["row"].bit_length() - 1)]
    core, rest = col_bits[0], col_bits[1:]
    bits_data = row_bits[0::2] + rest[0::2]
    bits_param = row_bits[1::2] + rest[1::2]
    split = P(("row", "col"))
    rows = P(("row", "col"), None)
    return jax.shard_map(
        functools.partial(on_device, core, bits_data, bits_param, sizes),
        mesh=mesh,
        in_specs=(rows, rows, split, split, P(), P()),
        out_specs=(P(), rows, rows),
        check_vma=False,
    )
```

time: 176 us -> 62.6 us (0.36)
  blocking collectives: 89.8 us -> 0 us
  starting transfers between devices: 0.12 us -> 29 us
  waiting for transfers between devices: 37.1 us -> 15.9 us
  between operations: 18.2 us -> 3.23 us
  matrix products: 14.1 us -> 0 us
  Pallas kernels: 0 us -> 12.7 us
  other arithmetic: 11.1 us -> 0.23 us
  local copies, waits for them, and re-layouts: 5.13 us -> 1.5 us
    psum x1 -> x0, blocking collectives: 39.9 us -> none  [on_device(): total = lax.psum(partial_loss, ('row', 'col'))]
    reduce_scatter x2 -> x0, waiting for transfers between devices: 37 us -> none  [the longest x1 37 us: on_device(): lax.psum_scatter(image_embed_gradient, 'col', scatter_dimension=0, tiled=...]
    unnamed x2 -> x0, blocking collectives: 32.4 us -> none
    ppermute x0 -> x23, starting transfers between devices: none -> 29 us  [swap(): lax.ppermute(x, ('row', 'col'), [(i, i ^ mask) for i in range(devices)])]
    all_gather x1 -> x0, blocking collectives: 17.6 us -> none  [on_device(): lax.all_gather(param_norm, 'row', axis=0, tiled=True)]
    ppermute x0 -> x23, waiting for transfers between devices: none -> 15.9 us  [swap(): lax.ppermute(x, ('row', 'col'), [(i, i ^ mask) for i in range(devices)])]
    dot_general x3 -> x0, matrix products: 14.1 us -> none  [the longest x1 8.54 us: tile_terms(): jnp.dot(source_count, target_count.T, preferred_element_type=jnp.float32)]
    pallas_call x0 -> x9, Pallas kernels: none -> 12.7 us  [run(): return inner(*args)]
  transfers between devices with their start and end apart: 3 -> 23, of which waited for: 1 -> 6; matrix products, arithmetic and copies ran while one was open for 8% -> 2% of each run, Pallas kernels for 0% -> 13%
where the time goes in v1:
time: 62.6 us; the launch traced here: 62.5 us
  starting transfers between devices  29 us (46%)
  waiting for transfers between devices  15.9 us (25%)
  Pallas kernels  12.7 us (20%)
  between operations  3.23 us (5%)
  local copies, waits for them, and re-layouts  1.5 us (2%)
    ppermute x23, starting transfers between devices, swap(): lax.ppermute(x, ('row', 'col'), [(i, i ^ mask) for i in range(devices)])  29 us
    ppermute x23, waiting for transfers between devices, swap(): lax.ppermute(x, ('row', 'col'), [(i, i ^ mask) for i in range(devices)])  15.9 us
    pallas_call x9, Pallas kernels, run(): return inner(*args)  12.7 us
    unnamed x6, local copies, waits for them, and re-layouts  1.5 us
  transfers between devices with their start and end apart: 23, of which 6 were waited for; matrix products, arithmetic and copies ran while one was open for 2% of the time, Pallas kernels for 13%

profile of v1, /device:TPU:0, one launch (start us, length us, event | category | flops | bytes accessed | tf_op | source)
XLA Modules:
  0.0 62.5 jit_solution(17307738677579572698)
XLA Ops:
  0.6 1.3 %shard_map.85 = (bf16[208,512]{1,0:T(8,128)(2,1)S(1)}, bf16[208,512]{1,0:T(8,128)(2,1)S(1)}) custom-call(bf16[192,512]{1,0:T(8,128)(2,1)} %raw_ref.2, bf16[192,512]{1,0:T(8,128)(2,1)} %raw_ref.3, s32[1,192]{1,0:T(1,128)} %bitcast.7, s32[1,192]{1,0:T(1,128)} %bitcast.8), custom_call_target="tpu_custom_call" | custom-call | flops 1 | bytes 1 | tf_op jit(solution)/shard_map/pallas_call | solution.py:38
  1.9 3.1 %collective-permute-start.6 = (bf16[208,512]{1,0:T(8,128)(2,1)S(1)}, bf16[208,512]{1,0:T(8,128)(2,1)S(1)}, u32[]{:S(2)}, u32[]{:S(2)}) collective-permute-start(bf16[208,512]{1,0:T(8,128)(2,1)S(1)} %get-tuple-element.31.refs_0_), channel_id=1, source_target_pairs={{0,8},{1,9},{2,10},{3,11},{4,12},{5,13},{6,14},{7,15},{8,0},{9,1},... | collective-permute-start | bytes 638984 | tf_op jit(solution)/shard_map/ppermute | solution.py:253
  5.0 1.5 %collective-permute-start.2 = (bf16[208,512]{1,0:T(8,128)(2,1)S(1)}, bf16[208,512]{1,0:T(8,128)(2,1)S(1)}, u32[]{:S(2)}, u32[]{:S(2)}) collective-permute-start(bf16[208,512]{1,0:T(8,128)(2,1)S(1)} %get-tuple-element.31.refs_0_), channel_id=1, source_target_pairs={{0,2},{1,3},{2,0},{3,1},{4,6},{5,7},{6,4},{7,5},{8,10},{9,11},{10,... | collective-permute-start | bytes 638984 | tf_op jit(solution)/shard_map/ppermute | solution.py:253
  6.5 1.5 %collective-permute-start.5 = (bf16[208,512]{1,0:T(8,128)(2,1)S(1)}, bf16[208,512]{1,0:T(8,128)(2,1)S(1)}, u32[]{:S(2)}, u32[]{:S(2)}) collective-permute-start(bf16[208,512]{1,0:T(8,128)(2,1)S(1)} %get-tuple-element.30.refs_4_), channel_id=1, source_target_pairs={{0,4},{1,5},{2,6},{3,7},{4,0},{5,1},{6,2},{7,3},{8,12},{9,13},{10,... | collective-permute-start | bytes 638984 | tf_op jit(solution)/shard_map/ppermute | solution.py:253
  8.0 2.6 %collective-permute-start = (bf16[208,512]{1,0:T(8,128)(2,1)S(1)}, bf16[208,512]{1,0:T(8,128)(2,1)S(1)}, u32[]{:S(2)}, u32[]{:S(2)}) collective-permute-start(bf16[208,512]{1,0:T(8,128)(2,1)S(1)} %get-tuple-element.30.refs_4_), channel_id=1, source_target_pairs={{0,16},{1,17},{2,18},{3,19},{4,20},{5,21},{6,22},{7,23},{8,24},{9,... | collective-permute-start | bytes 638984 | tf_op jit(solution)/shard_map/ppermute | solution.py:253
  10.6 0.0 collective-permute-done.6.refs_0_
  10.6 3.8 %collective-permute-start.7 = (bf16[208,512]{1,0:T(8,128)(2,1)S(1)}, bf16[208,512]{1,0:T(8,128)(2,1)S(1)}, u32[]{:S(2)}, u32[]{:S(2)}) collective-permute-start(bf16[208,512]{1,0:T(8,128)(2,1)S(1)} %collective-permute-done.6.refs_0_), channel_id=1, source_target_pairs={{0,2},{1,3},{2,0},{3,1},{4,6},{5,7},{6,4},{7,5},{8,10},{9,11},{10,... | collective-permute-start | bytes 638984 | tf_op jit(solution)/shard_map/ppermute | solution.py:253
  15.7 0.1 pad_add_fusion.refs_6_
  15.8 0.0 collective-permute-done.2.refs_1_
  15.8 0.5 collective-permute-start.8
  16.3 0.1 collective-permute-start.4
  16.4 3.2 %collective-permute-done.refs_6_ = bf16[208,512]{1,0:T(8,128)(2,1)S(1)} collective-permute-done((bf16[208,512]{1,0:T(8,128)(2,1)S(1)}, bf16[208,512]{1,0:T(8,128)(2,1)S(1)}, u32[]{:S(2)}, u32[]{:S(2)}) %collective-permute-start) | collective-permute-done | bytes 213024 | tf_op jit(solution)/shard_map/ppermute | solution.py:253
  19.6 0.6 collective-permute-start.1
  20.2 0.0 collective-permute-done.7.refs_1_
  20.2 0.1 pad_add_fusion.1.refs_12_
  20.2 0.1 pad_maximum_fusion.refs_7_.refs_13_.refs_10_
  20.3 0.0 collective-permute-done.3.refs_2_
  20.3 0.0 collective-permute-done.4.refs_3_
  20.3 2.5 %shard_map.86 = (bf16[768,512]{1,0:T(8,128)(2,1)S(1)}, f32[8,768]{1,0:T(8,128)S(1)}, f32[768,512]{1,0:T(8,128)S(1)}, f32[384,512]{1,0:T(8,128)S(1)}, f32[8,128]{1,0:T(8,128)S(1)}) custom-call(bf16[208,512]{1,0:T(8,128)(2,1)S(1)} %get-tuple-element.31.refs_0_, bf16[208,512]{1,0:T(8,128)(2,1)S(1)} %collective-permute-done.2.refs_1_, ...), custom_call_target="tpu_custom_call" | custom-call | flops 1 | bytes 1 | tf_op jit(solution)/shard_map/pallas_call | solution.py:38
  22.9 4.4 %shard_map.87 = (bf16[768,512]{1,0:T(8,128)(2,1)S(1)}, f32[8,768]{1,0:T(8,128)S(1)}, f32[768,512]{1,0:T(8,128)S(1)}, f32[768,512]{1,0:T(8,128)S(1)}, f32[576,512]{1,0:T(8,128)S(1)}, /*index=5*/f32[8,128]{1,0:T(8,128)S(1)}) custom-call(bf16[208,512]{1,0:T(8,128)(2,1)S(1)} %collective-permute-done.6.refs_0_, ...), custom_call_target="tpu_custom_call" | custom-call | flops 1 | bytes 1 | tf_op jit(solution)/shard_map/pallas_call | solution.py:38
  27.3 3.0 %shard_map.88 = (f32[768,512]{1,0:T(8,128)S(1)}, s16[832,512]{1,0:T(8,128)(2,1)S(1)}, f32[8,128]{1,0:T(8,128)S(1)}, s16[208,512]{1,0:T(8,128)(2,1)S(1)}, s16[208,512]{1,0:T(8,128)(2,1)S(1)}) custom-call(bf16[208,512]{1,0:T(8,128)(2,1)S(1)} %collective-permute-done.1.refs_0_, bf16[768,512]{1,0:T(8,128)(2,1)S(1)} %get-tuple-element.32.refs_7_.refs_1_, ...), custom_call_target="tpu_custom_call" | custom-call | flops 1 | bytes 1 | tf_op jit(solution)/shard_map/pallas_call | solution.py:38
  30.4 0.6 collective-permute-start.10
  30.9 0.1 collective-permute-start.11
  31.0 1.5 %collective-permute-start.14 = (s16[208,512]{1,0:T(8,128)(2,1)S(1)}, s16[208,512]{1,0:T(8,128)(2,1)S(1)}, u32[]{:S(2)}, u32[]{:S(2)}) collective-permute-start(s16[208,512]{1,0:T(8,128)(2,1)S(1)} %get-tuple-element.48), channel_id=1, source_target_pairs={{0,4},{1,5},{2,6},{3,7},{4,0},{5,1},{6,2},{7,3},{8,12},{9,13},{10,... | collective-permute-start | bytes 638984 | tf_op jit(solution)/shard_map/ppermute | solution.py:253
  32.5 0.5 collective-permute-done.11.refs_3_
  32.9 0.3 shard_map.89
  33.3 1.2 %collective-permute-start.13 = (s16[208,512]{1,0:T(8,128)(2,1)S(1)}, s16[208,512]{1,0:T(8,128)(2,1)S(1)}, u32[]{:S(2)}, u32[]{:S(2)}) collective-permute-start(s16[208,512]{1,0:T(8,128)(2,1)S(1)} %get-tuple-element.47), channel_id=1, source_target_pairs={{0,2},{1,3},{2,0},{3,1},{4,6},{5,7},{6,4},{7,5},{8,10},{9,11},{10,... | collective-permute-start | bytes 638984 | tf_op jit(solution)/shard_map/ppermute | solution.py:253
  34.5 0.9 %collective-permute-start.15 = (f32[8,128]{1,0:T(8,128)S(1)}, f32[8,128]{1,0:T(8,128)S(1)}, u32[]{:S(2)}, u32[]{:S(2)}) collective-permute-start(f32[8,128]{1,0:T(8,128)S(1)} %get-tuple-element.49.refs_2_), channel_id=1, source_target_pairs={{0,2},{1,3},{2,0},{3,1},{4,6},{5,7},{6,4},{7,5},{8,10},{9,11},{10,... | collective-permute-start | bytes 12296 | tf_op jit(solution)/shard_map/ppermute | solution.py:253
  35.4 1.5 %collective-permute-start.21 = (s16[208,512]{1,0:T(8,128)(2,1)S(1)}, s16[208,512]{1,0:T(8,128)(2,1)S(1)}, u32[]{:S(2)}, u32[]{:S(2)}) collective-permute-start(s16[208,512]{1,0:T(8,128)(2,1)S(1)} %get-tuple-element.55), channel_id=1, source_target_pairs={{0,4},{1,5},{2,6},{3,7},{4,0},{5,1},{6,2},{7,3},{8,12},{9,13},{10,... | collective-permute-start | bytes 638984 | tf_op jit(solution)/shard_map/ppermute | solution.py:253
  36.9 2.2 %collective-permute-done.14.refs_1_ = s16[208,512]{1,0:T(8,128)(2,1)S(1)} collective-permute-done((s16[208,512]{1,0:T(8,128)(2,1)S(1)}, s16[208,512]{1,0:T(8,128)(2,1)S(1)}, u32[]{:S(2)}, u32[]{:S(2)}) %collective-permute-start.14) | collective-permute-done | bytes 213024 | tf_op jit(solution)/shard_map/ppermute | solution.py:253
  39.1 1.9 %collective-permute-done.15.refs_3_ = f32[8,128]{1,0:T(8,128)S(1)} collective-permute-done((f32[8,128]{1,0:T(8,128)S(1)}, f32[8,128]{1,0:T(8,128)S(1)}, u32[]{:S(2)}, u32[]{:S(2)}) %collective-permute-start.15) | collective-permute-done | bytes 4128 | tf_op jit(solution)/shard_map/ppermute | solution.py:253
  41.0 0.2 shard_map.90
  41.2 0.0 copy-start
  41.2 1.5 %collective-permute-start.16 = (f32[8,128]{1,0:T(8,128)S(1)}, f32[8,128]{1,0:T(8,128)S(1)}, u32[]{:S(2)}, u32[]{:S(2)}) collective-permute-start(f32[8,128]{1,0:T(8,128)S(1)} %get-tuple-element.50.refs_3_), channel_id=1, source_target_pairs={{0,4},{1,5},{2,6},{3,7},{4,0},{5,1},{6,2},{7,3},{8,12},{9,13},{10,... | collective-permute-start | bytes 12296 | tf_op jit(solution)/shard_map/ppermute | solution.py:253
  42.7 0.5 collective-permute-start.22
  43.2 1.7 %collective-permute-start.12 = (s16[208,512]{1,0:T(8,128)(2,1)S(1)}, s16[208,512]{1,0:T(8,128)(2,1)S(1)}, u32[]{:S(2)}, u32[]{:S(2)}) collective-permute-start(s16[208,512]{1,0:T(8,128)(2,1)S(1)} %get-tuple-element.46), channel_id=1, source_target_pairs={{0,2},{1,3},{2,0},{3,1},{4,6},{5,7},{6,4},{7,5},{8,10},{9,11},{10,... | collective-permute-start | bytes 638984 | tf_op jit(solution)/shard_map/ppermute | solution.py:253
  45.0 0.2 shard_map.91
  45.2 0.0 copy-start.1
  45.2 2.7 %collective-permute-start.17 = (s16[208,512]{1,0:T(8,128)(2,1)S(1)}, s16[208,512]{1,0:T(8,128)(2,1)S(1)}, u32[]{:S(2)}, u32[]{:S(2)}) collective-permute-start(s16[208,512]{1,0:T(8,128)(2,1)S(1)} %get-tuple-element.51), channel_id=1, source_target_pairs={{0,8},{1,9},{2,10},{3,11},{4,12},{5,13},{6,14},{7,15},{8,0},{9,1},... | collective-permute-start | bytes 638984 | tf_op jit(solution)/shard_map/ppermute | solution.py:253
  47.9 0.1 collective-permute-start.18
  48.0 1.6 %collective-permute-start.19 = (f32[8,128]{1,0:T(8,128)S(1)}, f32[8,128]{1,0:T(8,128)S(1)}, u32[]{:S(2)}, u32[]{:S(2)}) collective-permute-start(f32[8,128]{1,0:T(8,128)S(1)} %get-tuple-element.52.refs_4_), channel_id=1, source_target_pairs={{0,16},{1,17},{2,18},{3,19},{4,20},{5,21},{6,22},{7,23},{8,24},{9,... | collective-permute-start | bytes 12296 | tf_op jit(solution)/shard_map/ppermute | solution.py:253
  49.6 5.2 %collective-permute-done.22.refs_2_ = s16[208,512]{1,0:T(8,128)(2,1)S(1)} collective-permute-done((s16[208,512]{1,0:T(8,128)(2,1)S(1)}, s16[208,512]{1,0:T(8,128)(2,1)S(1)}, u32[]{:S(2)}, u32[]{:S(2)}) %collective-permute-start.22) | collective-permute-done | bytes 213024 | tf_op jit(solution)/shard_map/ppermute | solution.py:253
  54.8 1.5 %collective-permute-start.20 = (f32[8,128]{1,0:T(8,128)S(1)}, f32[8,128]{1,0:T(8,128)S(1)}, u32[]{:S(2)}, u32[]{:S(2)}) collective-permute-start(f32[8,128]{1,0:T(8,128)S(1)} %get-tuple-element.52.refs_4_), channel_id=1, source_target_pairs={{0,24},{1,25},{2,26},{3,27},{4,28},{5,29},{6,30},{7,31},{8,16},{9,... | collective-permute-start | bytes 12296 | tf_op jit(solution)/shard_map/ppermute | solution.py:253
  56.2 0.3 shard_map.93
  56.5 0.7 %copy.11 = f32[192,512]{1,0:T(8,128)} copy(f32[192,512]{1,0:T(8,128)S(1)} %shard_map.93) | data formatting | bytes 786432
  57.3 2.9 %collective-permute-done.20.refs_7_ = f32[8,128]{1,0:T(8,128)S(1)} collective-permute-done((f32[8,128]{1,0:T(8,128)S(1)}, f32[8,128]{1,0:T(8,128)S(1)}, u32[]{:S(2)}, u32[]{:S(2)}) %collective-permute-start.20) | collective-permute-done | bytes 4128 | tf_op jit(solution)/shard_map/ppermute | solution.py:253
  60.2 0.4 shard_map.92
  60.6 0.7 %copy.10 = f32[192,512]{1,0:T(8,128)} copy(f32[192,512]{1,0:T(8,128)S(1)} %get-tuple-element.58) | data formatting | bytes 786432
  (16 shorter events, 0.0 us)
Async XLA Ops:
  1.9 8.7 %collective-permute-start.6 = (bf16[208,512]{1,0:T(8,128)(2,1)S(1)}, bf16[208,512]{1,0:T(8,128)(2,1)S(1)}, u32[]{:S(2)}, u32[]{:S(2)}) collective-permute-start(bf16[208,512]{1,0:T(8,128)(2,1)S(1)} %get-tuple-element.31.refs_0_), channel_id=1, source_target_pairs={{0,8},{1,9},{2,10},{3,11},{4,12},{5,13},{6,14},{7,15},{8,0},{9,1},... | collective-permute-start | bytes 638984 | tf_op jit(solution)/shard_map/ppermute | solution.py:253
  5.0 10.8 %collective-permute-start.2 = (bf16[208,512]{1,0:T(8,128)(2,1)S(1)}, bf16[208,512]{1,0:T(8,128)(2,1)S(1)}, u32[]{:S(2)}, u32[]{:S(2)}) collective-permute-start(bf16[208,512]{1,0:T(8,128)(2,1)S(1)} %get-tuple-element.31.refs_0_), channel_id=1, source_target_pairs={{0,2},{1,3},{2,0},{3,1},{4,6},{5,7},{6,4},{7,5},{8,10},{9,11},{10,... | collective-permute-start | bytes 638984 | tf_op jit(solution)/shard_map/ppermute | solution.py:253
  6.5 9.9 %collective-permute-start.5 = (bf16[208,512]{1,0:T(8,128)(2,1)S(1)}, bf16[208,512]{1,0:T(8,128)(2,1)S(1)}, u32[]{:S(2)}, u32[]{:S(2)}) collective-permute-start(bf16[208,512]{1,0:T(8,128)(2,1)S(1)} %get-tuple-element.30.refs_4_), channel_id=1, source_target_pairs={{0,4},{1,5},{2,6},{3,7},{4,0},{5,1},{6,2},{7,3},{8,12},{9,13},{10,... | collective-permute-start | bytes 638984 | tf_op jit(solution)/shard_map/ppermute | solution.py:253
  8.0 11.6 %collective-permute-start = (bf16[208,512]{1,0:T(8,128)(2,1)S(1)}, bf16[208,512]{1,0:T(8,128)(2,1)S(1)}, u32[]{:S(2)}, u32[]{:S(2)}) collective-permute-start(bf16[208,512]{1,0:T(8,128)(2,1)S(1)} %get-tuple-element.30.refs_4_), channel_id=1, source_target_pairs={{0,16},{1,17},{2,18},{3,19},{4,20},{5,21},{6,22},{7,23},{8,24},{9,... | collective-permute-start | bytes 638984 | tf_op jit(solution)/shard_map/ppermute | solution.py:253
  10.6 9.6 %collective-permute-start.7 = (bf16[208,512]{1,0:T(8,128)(2,1)S(1)}, bf16[208,512]{1,0:T(8,128)(2,1)S(1)}, u32[]{:S(2)}, u32[]{:S(2)}) collective-permute-start(bf16[208,512]{1,0:T(8,128)(2,1)S(1)} %collective-permute-done.6.refs_0_), channel_id=1, source_target_pairs={{0,2},{1,3},{2,0},{3,1},{4,6},{5,7},{6,4},{7,5},{8,10},{9,11},{10,... | collective-permute-start | bytes 638984 | tf_op jit(solution)/shard_map/ppermute | solution.py:253
  14.4 5.9 %collective-permute-start.3 = (bf16[208,512]{1,0:T(8,128)(2,1)S(1)}, bf16[208,512]{1,0:T(8,128)(2,1)S(1)}, u32[]{:S(2)}, u32[]{:S(2)}) collective-permute-start(bf16[208,512]{1,0:T(8,128)(2,1)S(1)} %get-tuple-element.31.refs_0_), channel_id=1, source_target_pairs={{0,1},{1,0},{2,3},{3,2},{4,5},{5,4},{6,7},{7,6},{8,9},{9,8},{10,11... | collective-permute-start | bytes 638984 | tf_op jit(solution)/shard_map/ppermute | solution.py:253
  15.8 7.0 %collective-permute-start.8 = (bf16[208,512]{1,0:T(8,128)(2,1)S(1)}, bf16[208,512]{1,0:T(8,128)(2,1)S(1)}, u32[]{:S(2)}, u32[]{:S(2)}) collective-permute-start(bf16[208,512]{1,0:T(8,128)(2,1)S(1)} %collective-permute-done.6.refs_0_), channel_id=1, source_target_pairs={{0,1},{1,0},{2,3},{3,2},{4,5},{5,4},{6,7},{7,6},{8,9},{9,8},{10,11... | collective-permute-start | bytes 638984 | tf_op jit(solution)/shard_map/ppermute | solution.py:253
  16.3 4.0 %collective-permute-start.4 = (bf16[208,512]{1,0:T(8,128)(2,1)S(1)}, bf16[208,512]{1,0:T(8,128)(2,1)S(1)}, u32[]{:S(2)}, u32[]{:S(2)}) collective-permute-start(bf16[208,512]{1,0:T(8,128)(2,1)S(1)} %collective-permute-done.2.refs_1_), channel_id=1, source_target_pairs={{0,1},{1,0},{2,3},{3,2},{4,5},{5,4},{6,7},{7,6},{8,9},{9,8},{10,11... | collective-permute-start | bytes 638984 | tf_op jit(solution)/shard_map/ppermute | solution.py:253
  19.6 7.7 %collective-permute-start.1 = (bf16[208,512]{1,0:T(8,128)(2,1)S(1)}, bf16[208,512]{1,0:T(8,128)(2,1)S(1)}, u32[]{:S(2)}, u32[]{:S(2)}) collective-permute-start(bf16[208,512]{1,0:T(8,128)(2,1)S(1)} %collective-permute-done.refs_6_), channel_id=1, source_target_pairs={{0,4},{1,5},{2,6},{3,7},{4,0},{5,1},{6,2},{7,3},{8,12},{9,13},{10,... | collective-permute-start | bytes 638984 | tf_op jit(solution)/shard_map/ppermute | solution.py:253
  20.2 2.7 %collective-permute-start.9 = (bf16[208,512]{1,0:T(8,128)(2,1)S(1)}, bf16[208,512]{1,0:T(8,128)(2,1)S(1)}, u32[]{:S(2)}, u32[]{:S(2)}) collective-permute-start(bf16[208,512]{1,0:T(8,128)(2,1)S(1)} %collective-permute-done.7.refs_1_), channel_id=1, source_target_pairs={{0,1},{1,0},{2,3},{3,2},{4,5},{5,4},{6,7},{7,6},{8,9},{9,8},{10,11... | collective-permute-start | bytes 638984 | tf_op jit(solution)/shard_map/ppermute | solution.py:253
  30.4 2.6 %collective-permute-start.10 = (s16[832,512]{1,0:T(8,128)(2,1)S(1)}, s16[832,512]{1,0:T(8,128)(2,1)S(1)}, u32[]{:S(2)}, u32[]{:S(2)}) collective-permute-start(s16[832,512]{1,0:T(8,128)(2,1)S(1)} %get-tuple-element.44), channel_id=1, source_target_pairs={{0,1},{1,0},{2,3},{3,2},{4,5},{5,4},{6,7},{7,6},{8,9},{9,8},{10,11... | collective-permute-start | bytes 2555912 | tf_op jit(solution)/shard_map/ppermute | solution.py:253
  30.9 2.0 %collective-permute-start.11 = (f32[8,128]{1,0:T(8,128)S(1)}, f32[8,128]{1,0:T(8,128)S(1)}, u32[]{:S(2)}, u32[]{:S(2)}) collective-permute-start(f32[8,128]{1,0:T(8,128)S(1)} %get-tuple-element.45.refs_2_), channel_id=1, source_target_pairs={{0,1},{1,0},{2,3},{3,2},{4,5},{5,4},{6,7},{7,6},{8,9},{9,8},{10,11... | collective-permute-start | bytes 12296 | tf_op jit(solution)/shard_map/ppermute | solution.py:253
  31.0 8.1 %collective-permute-start.14 = (s16[208,512]{1,0:T(8,128)(2,1)S(1)}, s16[208,512]{1,0:T(8,128)(2,1)S(1)}, u32[]{:S(2)}, u32[]{:S(2)}) collective-permute-start(s16[208,512]{1,0:T(8,128)(2,1)S(1)} %get-tuple-element.48), channel_id=1, source_target_pairs={{0,4},{1,5},{2,6},{3,7},{4,0},{5,1},{6,2},{7,3},{8,12},{9,13},{10,... | collective-permute-start | bytes 638984 | tf_op jit(solution)/shard_map/ppermute | solution.py:253
  33.3 11.7 %collective-permute-start.13 = (s16[208,512]{1,0:T(8,128)(2,1)S(1)}, s16[208,512]{1,0:T(8,128)(2,1)S(1)}, u32[]{:S(2)}, u32[]{:S(2)}) collective-permute-start(s16[208,512]{1,0:T(8,128)(2,1)S(1)} %get-tuple-element.47), channel_id=1, source_target_pairs={{0,2},{1,3},{2,0},{3,1},{4,6},{5,7},{6,4},{7,5},{8,10},{9,11},{10,... | collective-permute-start | bytes 638984 | tf_op jit(solution)/shard_map/ppermute | solution.py:253
  34.5 6.5 %collective-permute-start.15 = (f32[8,128]{1,0:T(8,128)S(1)}, f32[8,128]{1,0:T(8,128)S(1)}, u32[]{:S(2)}, u32[]{:S(2)}) collective-permute-start(f32[8,128]{1,0:T(8,128)S(1)} %get-tuple-element.49.refs_2_), channel_id=1, source_target_pairs={{0,2},{1,3},{2,0},{3,1},{4,6},{5,7},{6,4},{7,5},{8,10},{9,11},{10,... | collective-permute-start | bytes 12296 | tf_op jit(solution)/shard_map/ppermute | solution.py:253
  35.4 12.6 %collective-permute-start.21 = (s16[208,512]{1,0:T(8,128)(2,1)S(1)}, s16[208,512]{1,0:T(8,128)(2,1)S(1)}, u32[]{:S(2)}, u32[]{:S(2)}) collective-permute-start(s16[208,512]{1,0:T(8,128)(2,1)S(1)} %get-tuple-element.55), channel_id=1, source_target_pairs={{0,4},{1,5},{2,6},{3,7},{4,0},{5,1},{6,2},{7,3},{8,12},{9,13},{10,... | collective-permute-start | bytes 638984 | tf_op jit(solution)/shard_map/ppermute | solution.py:253
  41.2 15.1 %copy-start = (bf16[192,512]{1,0:T(8,128)(2,1)S(1)}, bf16[192,512]{1,0:T(8,128)(2,1)}, u32[]{:S(2)}) copy-start(bf16[192,512]{1,0:T(8,128)(2,1)} %raw_ref.3) | copy-start | bytes 589828
  41.2 3.8 %collective-permute-start.16 = (f32[8,128]{1,0:T(8,128)S(1)}, f32[8,128]{1,0:T(8,128)S(1)}, u32[]{:S(2)}, u32[]{:S(2)}) collective-permute-start(f32[8,128]{1,0:T(8,128)S(1)} %get-tuple-element.50.refs_3_), channel_id=1, source_target_pairs={{0,4},{1,5},{2,6},{3,7},{4,0},{5,1},{6,2},{7,3},{8,12},{9,13},{10,... | collective-permute-start | bytes 12296 | tf_op jit(solution)/shard_map/ppermute | solution.py:253
  42.7 12.1 %collective-permute-start.22 = (s16[208,512]{1,0:T(8,128)(2,1)S(1)}, s16[208,512]{1,0:T(8,128)(2,1)S(1)}, u32[]{:S(2)}, u32[]{:S(2)}) collective-permute-start(s16[208,512]{1,0:T(8,128)(2,1)S(1)} %get-tuple-element.56), channel_id=1, source_target_pairs={{0,16},{1,17},{2,18},{3,19},{4,20},{5,21},{6,22},{7,23},{8,24},{9,... | collective-permute-start | bytes 638984 | tf_op jit(solution)/shard_map/ppermute | solution.py:253
  43.2 14.0 %collective-permute-start.12 = (s16[208,512]{1,0:T(8,128)(2,1)S(1)}, s16[208,512]{1,0:T(8,128)(2,1)S(1)}, u32[]{:S(2)}, u32[]{:S(2)}) collective-permute-start(s16[208,512]{1,0:T(8,128)(2,1)S(1)} %get-tuple-element.46), channel_id=1, source_target_pairs={{0,2},{1,3},{2,0},{3,1},{4,6},{5,7},{6,4},{7,5},{8,10},{9,11},{10,... | collective-permute-start | bytes 638984 | tf_op jit(solution)/shard_map/ppermute | solution.py:253
  45.2 14.9 %copy-start.1 = (bf16[192,512]{1,0:T(8,128)(2,1)S(1)}, bf16[192,512]{1,0:T(8,128)(2,1)}, u32[]{:S(2)}) copy-start(bf16[192,512]{1,0:T(8,128)(2,1)} %raw_ref.2) | copy-start | bytes 589828
  45.2 14.9 %collective-permute-start.17 = (s16[208,512]{1,0:T(8,128)(2,1)S(1)}, s16[208,512]{1,0:T(8,128)(2,1)S(1)}, u32[]{:S(2)}, u32[]{:S(2)}) collective-permute-start(s16[208,512]{1,0:T(8,128)(2,1)S(1)} %get-tuple-element.51), channel_id=1, source_target_pairs={{0,8},{1,9},{2,10},{3,11},{4,12},{5,13},{6,14},{7,15},{8,0},{9,1},... | collective-permute-start | bytes 638984 | tf_op jit(solution)/shard_map/ppermute | solution.py:253
  47.9 9.3 %collective-permute-start.18 = (f32[8,128]{1,0:T(8,128)S(1)}, f32[8,128]{1,0:T(8,128)S(1)}, u32[]{:S(2)}, u32[]{:S(2)}) collective-permute-start(f32[8,128]{1,0:T(8,128)S(1)} %get-tuple-element.52.refs_4_), channel_id=1, source_target_pairs={{0,8},{1,9},{2,10},{3,11},{4,12},{5,13},{6,14},{7,15},{8,0},{9,1},... | collective-permute-start | bytes 12296 | tf_op jit(solution)/shard_map/ppermute | solution.py:253
  48.0 9.3 %collective-permute-start.19 = (f32[8,128]{1,0:T(8,128)S(1)}, f32[8,128]{1,0:T(8,128)S(1)}, u32[]{:S(2)}, u32[]{:S(2)}) collective-permute-start(f32[8,128]{1,0:T(8,128)S(1)} %get-tuple-element.52.refs_4_), channel_id=1, source_target_pairs={{0,16},{1,17},{2,18},{3,19},{4,20},{5,21},{6,22},{7,23},{8,24},{9,... | collective-permute-start | bytes 12296 | tf_op jit(solution)/shard_map/ppermute | solution.py:253
  54.8 5.4 %collective-permute-start.20 = (f32[8,128]{1,0:T(8,128)S(1)}, f32[8,128]{1,0:T(8,128)S(1)}, u32[]{:S(2)}, u32[]{:S(2)}) collective-permute-start(f32[8,128]{1,0:T(8,128)S(1)} %get-tuple-element.52.refs_4_), channel_id=1, source_target_pairs={{0,24},{1,25},{2,26},{3,27},{4,28},{5,29},{6,30},{7,31},{8,16},{9,... | collective-permute-start | bytes 12296 | tf_op jit(solution)/shard_map/ppermute | solution.py:253

commit v2 on v1

--- a/solution.py
+++ b/solution.py
@@ -8,7 +8,9 @@
 from jax.sharding import PartitionSpec as P
 
 AUX = 16
+SUB = 8
 FULL = 32000.0
+LIMB = 16384.0
 LOG2E = 1.4426950408889634
 LN2 = 0.6931471805599453
 VMEM = pl.BlockSpec(memory_space=pltpu.VMEM)
@@ -18,14 +20,14 @@
 I16 = jnp.int16
 
 
-def call(body, out_shape, in_specs, scratch=(), aliases=None, vmem=24 * 2**20):
+def call(body, out_shape, in_specs, scratch=(), aliases=None, vmem=16 * 2**20, to=pltpu.VMEM):
     inner = pl.pallas_call(
         body,
-        out_shape=jax.tree.map(lambda s: pltpu.VMEM(s.shape, s.dtype), out_shape),
+        out_shape=jax.tree.map(lambda s: to(s.shape, s.dtype), out_shape),
         in_specs=in_specs,
         input_output_aliases=aliases or {},
         cost_estimate=pl.CostEstimate(flops=1, bytes_accessed=1, transcendentals=0),
-        out_specs=jax.tree.map(lambda _: VMEM, out_shape),
+        out_specs=jax.tree.map(lambda _: pl.BlockSpec(memory_space=to), out_shape),
         scratch_shapes=list(scratch),
         compiler_params=pltpu.CompilerParams(vmem_limit_bytes=vmem),
     )
@@ -46,8 +48,8 @@
     return full * scale, scale
 
 
-def pack_kernel(data_hbm, param_hbm, region_hbm, partner_hbm, data_msg, param_msg, *scratch):
-    data, param, region, partner, aux, sems = scratch
+def pack_kernel(data_hbm, param_hbm, region_hbm, partner_hbm, param_msg, data, side, *scratch):
+    param, region, partner, aux, sems = scratch
     rows = data.shape[0]
     pairs = ((param_hbm, param), (region_hbm, region), (partner_hbm, partner), (data_hbm, data))
     copies = [pltpu.make_async_copy(a, b, sems.at[i]) for i, (a, b) in enumerate(pairs)]
@@ -60,29 +62,48 @@
     aux[0:1, 0:rows] = region[...].astype(F32)
     aux[1:2, 0:rows] = (index >> 8).astype(F32)
     aux[2:3, 0:rows] = (index & 255).astype(F32)
-    side = aux[...].astype(BF16)
-    for raw, msg in ((param, param_msg), (data, data_msg)):
-        msg[pl.ds(rows, AUX), :] = side
-        msg[pl.ds(0, rows), :] = normalize(raw[...])[0].astype(BF16)
-
-
-def encode(value, ref, start):
+    side[...] = aux[...].astype(BF16)
+    param_msg[pl.ds(rows, AUX), :] = side[...]
+    param_msg[pl.ds(0, rows), :] = normalize(param[...])[0].astype(BF16)
+
+
+def pack_data_kernel(data, side, data_msg):
+    rows = data.shape[0]
+    data_msg[pl.ds(rows, AUX), :] = side[...]
+    data_msg[pl.ds(0, rows), :] = normalize(data[...])[0].astype(BF16)
+
+
+def encode(value, ref, start, loss=None):
     rows, width = value.shape
-    parts = value.reshape(rows // AUX, AUX, width)
+    parts = value.reshape(rows // SUB, SUB, width)
     top = jnp.max(jnp.abs(parts), axis=0)
     power = jnp.ceil(jnp.log2(jnp.maximum(top, 1e-30)) * 256.0)
     unit = jnp.exp2(power * (-1.0 / 256.0)) * FULL
     coded = ((parts * unit[None] + 32768.5).astype(jnp.int32) - 32768).astype(I16)
     ref[pl.ds(start, rows), :] = coded.reshape(rows, width)
-    ref[pl.ds(start + rows, AUX), :] = power.astype(jnp.int32).astype(I16)
-
-
-def decode(ref, start, rows):
-    width = ref.shape[-1]
-    coded = ref[pl.ds(start, rows), :].astype(F32).reshape(rows // AUX, AUX, width)
-    power = ref[pl.ds(start + rows, AUX), :].astype(F32)
+    below = jnp.zeros_like(power)
+    if loss is not None:
+        exponent = jnp.ceil(jnp.log2(jnp.maximum(loss, 1e-30)))
+        mantissa = loss * jnp.exp2(-exponent) * LIMB
+        high = jnp.floor(mantissa)
+        low = jnp.floor((mantissa - high) * LIMB)
+        rest = jnp.zeros((SUB, width - 3 * loss.shape[1]), F32)
+        below = jnp.concatenate([exponent, high, low, rest], axis=1)
+    aux = jnp.concatenate([power, below], axis=0)
+    ref[pl.ds(start + rows, AUX), :] = aux.astype(jnp.int32).astype(I16)
+
+
+def decode(ref, start, rows, at=0, piece=None):
+    piece, width = piece or rows, ref.shape[-1]
+    coded = ref[pl.ds(start + at, piece), :].astype(F32).reshape(piece // SUB, SUB, width)
+    power = ref[pl.ds(start + rows, AUX), :].astype(F32)[:SUB]
     unit = jnp.exp2(power * (1.0 / 256.0)) * (1.0 / FULL)
-    return (coded * unit[None]).reshape(rows, width)
+    return (coded * unit[None]).reshape(piece, width)
+
+
+def decode_loss(ref, rows):
+    exponent, high, low = jnp.split(ref[pl.ds(rows, AUX), :].astype(F32)[SUB:, :384], 3, axis=1)
+    return (high + low * (1.0 / LIMB)) * (1.0 / LIMB) * jnp.exp2(exponent)
 
 
 def log1p(t):
@@ -138,7 +159,8 @@
 
 def early_kernel(rows, n, p_n, *refs):
     msgs, params, (base, coef) = refs[:n], refs[n : n + p_n], refs[n + p_n : n + p_n + 2]
-    data, side, acc, parts, loss_out = refs[n + p_n + 2 :]
+    data, side, acc, loss_out = refs[n + p_n + 2 :]
+    cols = n * rows
     load_data(msgs, data, side, rows)
     loss = jnp.zeros((8, 128), F32)
     for s in range(p_n):
@@ -146,16 +168,19 @@
         columns = side_columns(params[s], base[s], rows)
         grad, term = tile(block, columns, data, side, coef[0], coef[1])
         loss = loss + term
-        parts[pl.ds(s * rows, rows), :] = jnp.dot(grad, data[...], preferred_element_type=F32)
+        at = pl.ds(cols + s * rows, rows)
+        acc[at, :] = jnp.dot(grad, data[...], preferred_element_type=F32)
         d_part = lax.dot_general(grad, block, FIRST, preferred_element_type=F32)
-        acc[...] = d_part if s == 0 else acc[...] + d_part
+        acc[pl.ds(0, cols), :] = d_part if s == 0 else acc[pl.ds(0, cols), :] + d_part
     loss_out[...] = loss
 
 
 def middle_kernel(rows, n, p_n, m_n, *refs):
     msgs, params = refs[:n], refs[n : n + p_n + m_n]
-    data0, side0, acc0, parts_in, loss_in, base, coef = refs[n + p_n + m_n : n + p_n + m_n + 7]
-    data, side, acc0_out, acc, parts, loss_out = refs[n + p_n + m_n + 7 :]
+    data0, side0, acc0, loss_in, base, coef = refs[n + p_n + m_n : n + p_n + m_n + 6]
+    data, side, acc0_out, acc, parts, loss_out = refs[n + p_n + m_n + 6 :]
+    cols = n * rows
+    whole = pl.ds(0, cols)
     load_data(msgs, data, side, rows)
     loss = loss_in[...]
     for s in range(p_n + m_n):
@@ -168,15 +193,15 @@
         d_part = lax.dot_general(grad, block, FIRST, preferred_element_type=F32)
         acc[...] = d_part if s == 0 else acc[...] + d_part
         if s < p_n:
-            parts[at, :] = parts_in[at, :] + part
+            parts[at, :] = acc0[pl.ds(cols + s * rows, rows), :] + part
             continue
         grad, term = tile(block, columns, data0, side0, coef[0], coef[1])
         loss = loss + term
         parts[at, :] = part + jnp.dot(grad, data0[...], preferred_element_type=F32)
         d_part = lax.dot_general(grad, block, FIRST, preferred_element_type=F32)
-        acc0_out[...] = (acc0 if s == p_n else acc0_out)[...] + d_part
+        acc0_out[...] = (acc0[whole, :] if s == p_n else acc0_out[...]) + d_part
     if m_n == 0:
-        acc0_out[...] = acc0[...]
+        acc0_out[...] = acc0[whole, :]
     loss_out[...] = loss
 
 
@@ -211,29 +236,45 @@
     loss_out[...] = loss
 
 
-def emit_kernel(rows, plan, *refs):
-    n_arrays = max(max([b] + [a for a, _ in parts]) for b, _, parts in plan) + 1
-    arrays, loss, got, outs = refs[:n_arrays], refs[n_arrays], refs[n_arrays + 1], refs[n_arrays + 2 :]
-    outs[-1][...] = loss[...] + got[...]
+def emit_kernel(rows, plan, n_arrays, carried, *refs):
+    arrays, terms, outs = refs[:n_arrays], refs[n_arrays:], None
+    loss = None
+    if carried is None:
+        outs = terms
+    else:
+        terms, outs = terms[: -len(plan) - 1], terms[-len(plan) - 1 :]
+        loss = sum([t[...] for t in terms] + [decode_loss(arrays[a], rows) for a in carried])
+        outs[-1][...] = loss
     for out, (b, start, parts) in zip(outs, plan):
         total = arrays[b][pl.ds(start * rows, rows), :]
         for a, i in parts:
             total = total + decode(arrays[a], i * (rows + AUX), rows)
-        encode(total, out, 0)
+        encode(total, out, 0, loss)
 
 
 def finish_kernel(rows, plan, pairs, raw_ref, *refs):
-    start, parts, arrays = plan
+    start, parts, arrays, carried = plan
+    out_vmem, loss_vmem, sems = refs[-3:]
+    out_ref = refs[-5] if pairs else refs[-4]
+    copies = []
     if pairs:
-        terms, out_ref, loss_ref = refs[arrays:-2], refs[-2], refs[-1]
-        loss_ref[...] = jnp.sum(sum([t[...] for t in terms]), keepdims=True) / (pairs * pairs)
-    else:
-        out_ref = refs[-1]
-    full, scale = normalize(raw_ref[...])
-    dnorm = refs[0][pl.ds(start * rows, rows), :]
-    for a, i in parts:
-        dnorm = dnorm + decode(refs[a], i * (rows + AUX), rows)
-    out_ref[...] = scale * (dnorm - full * jnp.mean(dnorm * full, axis=-1, keepdims=True))
+        terms = [t[...] for t in refs[arrays:-5]] + [decode_loss(refs[a], rows) for a in carried]
+        loss_vmem[...] = jnp.sum(sum(terms), keepdims=True) / (pairs * pairs)
+        copies.append(pltpu.make_async_copy(loss_vmem, refs[-4], sems.at[0]))
+        copies[-1].start()
+    piece = rows // 3 if rows % (3 * AUX) == 0 else rows
+    for k, at in enumerate(range(0, rows, piece)):
+        full, scale = normalize(raw_ref[pl.ds(at, piece), :])
+        dnorm = refs[0][pl.ds(start * rows + at, piece), :]
+        for a, i in parts:
+            dnorm = dnorm + decode(refs[a], i * (rows + AUX), rows, at, piece)
+        grad = scale * (dnorm - full * jnp.mean(dnorm * full, axis=-1, keepdims=True))
+        here = pl.ds(at, piece)
+        out_vmem[here, :] = grad
+        copies.append(pltpu.make_async_copy(out_vmem.at[here], out_ref.at[here], sems.at[1 + k]))
+        copies[-1].start()
+    for copy in copies:
+        copy.wait()
 
 
 def combine(bits):
@@ -252,12 +293,11 @@
     def swap(x, mask):
         return lax.ppermute(x, ("row", "col"), [(i, i ^ mask) for i in range(devices)])
 
-    data_msg, param_msg = call(
+    param_msg, raw_data, side = call(
         pack_kernel,
-        [shape((msg, width), BF16)] * 2,
+        [shape((msg, width), BF16), shape((rows, width), BF16), shape((AUX, width), BF16)],
         [pl.BlockSpec(memory_space=pltpu.HBM)] * 4,
         [
-            pltpu.VMEM((rows, width), BF16),
             pltpu.VMEM((rows, width), BF16),
             pltpu.VMEM((1, rows), jnp.int32),
             pltpu.VMEM((1, rows), jnp.int32),
@@ -265,6 +305,7 @@
             pltpu.SemaphoreType.DMA((4,)),
         ],
     )(data, param, region.reshape(1, rows), partner.reshape(1, rows))
+    (data_msg,) = call(pack_data_kernel, [shape((msg, width), BF16)], [VMEM] * 2)(raw_data, side)
     held_p, masks_p = [param_msg], [0]
     held_d = [data_msg]
     for k in range(max(len(bits_data), len(bits_param))):
@@ -273,11 +314,10 @@
             masks_p += [m ^ bits_param[k] for m in masks_p]
         if k < len(bits_data):
             held_d += [swap(x, bits_data[k]) for x in held_d]
-    held_d = [held_d, [swap(x, core) for x in held_d]]
+    n_own, n_param = len(held_d), len(held_p)
+    other_d = [swap(x, core) for x in held_d]
     me = lax.axis_index("row") * sizes["col"] + lax.axis_index("col")
     coef = jnp.stack([gain[0] / width, shift[0]])
-    n_own, n_param = len(held_d[0]), len(held_p)
-    halves = [[x for side in held_d for x in side[h::2]] for h in (0, 1)]
     n = n_own
     cols = n * rows
     late = [i for i in range(n_param) if i == n_param - 1]
@@ -286,17 +326,16 @@
     order = early + middle
     base = {i: (me ^ masks_p[i]) * rows for i in range(n_param)}
     bases = lambda group: jnp.stack([base[i] for i in group]).astype(jnp.int32)
-    data0, side0, acc0, parts, loss = call(
+    data0, side0, acc0, loss = call(
         functools.partial(early_kernel, rows, n, len(early)),
         [
             shape((cols, width), BF16),
             shape((8, cols), F32),
-            shape((cols, width), F32),
-            shape((len(early) * rows, width), F32),
+            shape((cols + len(early) * rows, width), F32),
             shape((8, 128), F32),
         ],
         [VMEM] * (n + len(early)) + [SMEM] * 2,
-    )(*halves[0], *[held_p[i] for i in early], bases(early), coef)
+    )(*held_d[0::2], *other_d[0::2], *[held_p[i] for i in early], bases(early), coef)
     data1, side1, acc0, acc1, parts, loss = call(
         functools.partial(middle_kernel, rows, n, len(early), len(middle)),
         [
@@ -307,9 +346,9 @@
             shape((len(order) * rows, width), F32),
             shape((8, 128), F32),
         ],
-        [VMEM] * (n + len(order) + 5) + [SMEM] * 2,
+        [VMEM] * (n + len(order) + 4) + [SMEM] * 2,
     )(
-        *halves[1], *[held_p[i] for i in order], data0, side0, acc0, parts, loss, bases(order), coef
+        *held_d[1::2], *other_d[1::2], *[held_p[i] for i in order], data0, side0, acc0, loss, bases(order), coef
     )
     top = n_param // 2
     ready = [k for k, i in enumerate(order) if i >= top]
@@ -327,11 +366,14 @@
         *[held_p[i] for i in late],
         data0, side0, acc0, data1, side1, acc1, parts, loss, bases(late), coef,
     )
-    loss_steps = [core] + bits_data[:0:-1] + bits_param[:0:-1] + bits_data[:1] + bits_param[:1]
-    pending = [swap(loss, loss_steps.pop(0))]
-
-    def emit(items):
-        nonlocal loss
+    columns = sizes["col"]
+    inner = [b for b in bits_data + bits_param if b < columns]
+    outer = [b for b in bits_data + bits_param if b >= columns]
+    rounds = [inner, outer]
+    terms, carriers = [loss, swap(loss, core)], []
+
+    def emit(items, step, with_loss):
+        nonlocal terms, carriers
         arrays = []
 
         def slot(x):
@@ -342,15 +384,24 @@
             return len(arrays) - 1
 
         plan = [(slot(b), at, [(slot(x), i) for x, i in parts]) for b, at, parts in items]
-        *msgs, loss = call(
-            functools.partial(emit_kernel, rows, plan),
-            [shape((msg, width), I16)] * len(items) + [shape((8, 128), F32)],
-            [VMEM] * (len(arrays) + 2),
-        )(*arrays, loss, pending.pop())
-        if len(loss_steps) > 2 or emits[0] > 1:
-            pending.append(swap(loss, loss_steps.pop(0)))
-        emits[0] -= 1
-        return msgs
+        carried, outs = None, [shape((msg, width), I16)] * len(items)
+        n_arrays = len(arrays)
+        if with_loss and rounds:
+            carried = [slot(x) for x in carriers]
+            n_arrays = len(arrays)
+            outs.append(shape((8, 128), F32))
+            arrays = arrays + terms
+        msgs = call(
+            functools.partial(emit_kernel, rows, plan, n_arrays, carried),
+            outs,
+            [VMEM] * len(arrays),
+        )(*arrays)
+        got = [swap(x, step) for x in msgs[: len(items)]]
+        if carried is not None:
+            bits = rounds.pop(0)
+            terms = [msgs[-1]] + [swap(msgs[-1], m) for m in combine(bits)[1:] if m != step]
+            carriers = got[-1:] if step in bits else []
+        return got
 
     got = swap(send_d, core)
     items_d = [(keep_d, i, [(got, i)]) for i in range(n_own)]
@@ -359,34 +410,38 @@
     for i in range(top):
         items_p[i][2].append((got[i + top], 0))
     left_d, left_p = bits_data[::-1], bits_param[-2::-1]
-    emits = [len(left_d) + len(left_p)]
     while left_d or left_p:
         for items, left in ((items_d, left_d), (items_p, left_p)):
             if left:
                 step, half = left.pop(0), len(items) // 2
-                for i, x in enumerate(emit(items[half:])):
-                    items[i][2].append((swap(x, step), 0))
+                for i, x in enumerate(emit(items[half:], step, items is items_d)):
+                    items[i][2].append((x, 0))
                 del items[half:]
-    while len(loss_steps) > 2:
-        loss = loss + pending.pop()
-        pending.append(swap(loss, loss_steps.pop(0)))
-    if pending:
-        loss = loss + pending.pop()
-    terms = [loss] + [swap(loss, m) for m in combine(loss_steps)[1:]]
-
-    def finish(raw, item, terms=(), pairs=0):
+    def finish(raw, item, terms=(), carriers=(), pairs=0):
         arrays, at, parts = [item[0]], item[1], []
         for x, i in item[2]:
             arrays.append(x)
             parts.append((len(arrays) - 1, i))
+        carried = []
+        for x in carriers:
+            places = [a for a, y in enumerate(arrays) if y is x]
+            if not places:
+                arrays.append(x)
+            carried.append(places[0] if places else len(arrays) - 1)
         return call(
-            functools.partial(finish_kernel, rows, (at, parts, len(arrays)), pairs),
+            functools.partial(finish_kernel, rows, (at, parts, len(arrays), carried), pairs),
             [shape((rows, width), F32)] + [shape((1, 1), F32)] * bool(pairs),
             [VMEM] * (1 + len(arrays) + len(terms)),
+            [
+                pltpu.VMEM((rows, width), F32),
+                pltpu.VMEM((1, 1), F32),
+                pltpu.SemaphoreType.DMA((4,)),
+            ],
+            to=pltpu.HBM,
         )(raw, *arrays, *terms)
 
     (grad_param,) = finish(param, items_p[0])
-    grad_data, loss = finish(data, items_d[0], terms, rows * devices)
+    grad_data, loss = finish(data, items_d[0], terms, carriers, rows * devices)
     return loss.reshape(1), grad_data, grad_param
 
 
@@ -396,8 +451,9 @@
     col_bits = [1 << k for k in range(columns.bit_length() - 1)]
     row_bits = [columns << k for k in range(sizes["row"].bit_length() - 1)]
     core, rest = col_bits[0], col_bits[1:]
-    bits_data = row_bits[0::2] + rest[0::2]
-    bits_param = row_bits[1::2] + rest[1::2]
+    odd = len(row_bits) & 1
+    bits_data = row_bits[0::2] + rest[odd::2]
+    bits_param = row_bits[1::2] + rest[1 - odd :: 2]
     split = P(("row", "col"))
     rows = P(("row", "col"), None)
     return jax.shard_map(

time: 62.6 us -> 54.9 us (0.88)
  waiting for transfers between devices: 15.9 us -> 12.5 us
  starting transfers between devices: 29 us -> 25.7 us
  Pallas kernels: 12.7 us -> 14.2 us
  local copies, waits for them, and re-layouts: 1.5 us -> 0.01 us
  between operations: 3.23 us -> 2.11 us
    ppermute x23 -> x22, waiting for transfers between devices: 15.9 us -> 12.5 us  [swap(): lax.ppermute(x, ('row', 'col'), [(i, i ^ mask) for i in range(devices)])]
    ppermute x23 -> x22, starting transfers between devices: 29 us -> 25.7 us  [swap(): lax.ppermute(x, ('row', 'col'), [(i, i ^ mask) for i in range(devices)])]
    pallas_call x9 -> x10, Pallas kernels: 12.7 us -> 14.2 us  [run(): return inner(*args)]
    unnamed x6 -> x4, local copies, waits for them, and re-layouts: 1.5 us -> 0.01 us
  transfers between devices with their start and end apart: 23 -> 22, of which waited for: 6 -> 7; matrix products, arithmetic and copies ran while one was open for 2% -> 0% of each run, Pallas kernels for 13% -> 16%
where the time goes in v2:
time: 54.9 us; the launch traced here: 54.7 us
  starting transfers between devices  25.7 us (47%)
  Pallas kernels  14.2 us (26%)
  waiting for transfers between devices  12.5 us (23%)
  between operations  2.11 us (4%)
    ppermute x22, starting transfers between devices, swap(): lax.ppermute(x, ('row', 'col'), [(i, i ^ mask) for i in range(devices)])  25.7 us
    pallas_call x10, Pallas kernels, run(): return inner(*args)  14.2 us
    ppermute x22, waiting for transfers between devices, swap(): lax.ppermute(x, ('row', 'col'), [(i, i ^ mask) for i in range(devices)])  12.5 us
  transfers between devices with their start and end apart: 22, of which 7 were waited for; matrix products, arithmetic and copies ran while one was open for 0% of the time, Pallas kernels for 16%

profile of v2, /device:TPU:0, one launch (start us, length us, event | category | flops | bytes accessed | tf_op | source)
XLA Modules:
  0.0 54.7 jit_solution(11911000731412944052)
XLA Ops:
  0.6 1.2 %shard_map.85 = (bf16[208,512]{1,0:T(8,128)(2,1)S(1)}, bf16[192,512]{1,0:T(8,128)(2,1)S(1)}, bf16[16,512]{1,0:T(8,128)(2,1)S(1)}) custom-call(bf16[192,512]{1,0:T(8,128)(2,1)} %raw_ref.2, bf16[192,512]{1,0:T(8,128)(2,1)} %raw_ref.3, s32[1,192]{1,0:T(1,128)} %bitcast.7, s32[1,192]{1,0:T(1,128)} %bitcast.8), custom_call_target="tpu_custom_call" | custom-call | flops 1 | bytes 1 | tf_op jit(solution)/shard_map/pallas_call | solution.py:40
  1.9 0.1 shard_map.86.refs_0_
  2.0 3.1 %collective-permute-start.6 = (bf16[208,512]{1,0:T(8,128)(2,1)S(1)}, bf16[208,512]{1,0:T(8,128)(2,1)S(1)}, u32[]{:S(2)}, u32[]{:S(2)}) collective-permute-start(bf16[208,512]{1,0:T(8,128)(2,1)S(1)} %shard_map.86.refs_0_), channel_id=1, source_target_pairs={{0,8},{1,9},{2,10},{3,11},{4,12},{5,13},{6,14},{7,15},{8,0},{9,1},... | collective-permute-start | bytes 638984 | tf_op jit(solution)/shard_map/ppermute | solution.py:294
  5.1 1.5 %collective-permute-start.2 = (bf16[208,512]{1,0:T(8,128)(2,1)S(1)}, bf16[208,512]{1,0:T(8,128)(2,1)S(1)}, u32[]{:S(2)}, u32[]{:S(2)}) collective-permute-start(bf16[208,512]{1,0:T(8,128)(2,1)S(1)} %shard_map.86.refs_0_), channel_id=1, source_target_pairs={{0,2},{1,3},{2,0},{3,1},{4,6},{5,7},{6,4},{7,5},{8,10},{9,11},{10,... | collective-permute-start | bytes 638984 | tf_op jit(solution)/shard_map/ppermute | solution.py:294
  6.6 2.6 %collective-permute-start = (bf16[208,512]{1,0:T(8,128)(2,1)S(1)}, bf16[208,512]{1,0:T(8,128)(2,1)S(1)}, u32[]{:S(2)}, u32[]{:S(2)}) collective-permute-start(bf16[208,512]{1,0:T(8,128)(2,1)S(1)} %get-tuple-element.28.refs_4_), channel_id=1, source_target_pairs={{0,16},{1,17},{2,18},{3,19},{4,20},{5,21},{6,22},{7,23},{8,24},{9,... | collective-permute-start | bytes 638984 | tf_op jit(solution)/shard_map/ppermute | solution.py:294
  9.2 1.2 %collective-permute-done.6.refs_0_ = bf16[208,512]{1,0:T(8,128)(2,1)S(1)} collective-permute-done((bf16[208,512]{1,0:T(8,128)(2,1)S(1)}, bf16[208,512]{1,0:T(8,128)(2,1)S(1)}, u32[]{:S(2)}, u32[]{:S(2)}) %collective-permute-start.6) | collective-permute-done | bytes 213024 | tf_op jit(solution)/shard_map/ppermute | solution.py:294
  10.3 4.2 %collective-permute-start.7 = (bf16[208,512]{1,0:T(8,128)(2,1)S(1)}, bf16[208,512]{1,0:T(8,128)(2,1)S(1)}, u32[]{:S(2)}, u32[]{:S(2)}) collective-permute-start(bf16[208,512]{1,0:T(8,128)(2,1)S(1)} %collective-permute-done.6.refs_0_), channel_id=1, source_target_pairs={{0,2},{1,3},{2,0},{3,1},{4,6},{5,7},{6,4},{7,5},{8,10},{9,11},{10,... | collective-permute-start | bytes 638984 | tf_op jit(solution)/shard_map/ppermute | solution.py:294
  14.5 1.5 %collective-permute-start.5 = (bf16[208,512]{1,0:T(8,128)(2,1)S(1)}, bf16[208,512]{1,0:T(8,128)(2,1)S(1)}, u32[]{:S(2)}, u32[]{:S(2)}) collective-permute-start(bf16[208,512]{1,0:T(8,128)(2,1)S(1)} %get-tuple-element.28.refs_4_), channel_id=1, source_target_pairs={{0,4},{1,5},{2,6},{3,7},{4,0},{5,1},{6,2},{7,3},{8,12},{9,13},{10,... | collective-permute-start | bytes 638984 | tf_op jit(solution)/shard_map/ppermute | solution.py:294
  17.3 0.1 pad_add_fusion.refs_6_
  17.4 0.0 collective-permute-done.2.refs_1_
  17.4 0.0 collective-permute-start.8
  17.5 0.0 collective-permute-done.3.refs_2_
  17.5 0.5 collective-permute-start.4
  18.0 1.7 %collective-permute-done.refs_6_ = bf16[208,512]{1,0:T(8,128)(2,1)S(1)} collective-permute-done((bf16[208,512]{1,0:T(8,128)(2,1)S(1)}, bf16[208,512]{1,0:T(8,128)(2,1)S(1)}, u32[]{:S(2)}, u32[]{:S(2)}) %collective-permute-start) | collective-permute-done | bytes 213024 | tf_op jit(solution)/shard_map/ppermute | solution.py:294
  19.7 1.5 %collective-permute-start.1 = (bf16[208,512]{1,0:T(8,128)(2,1)S(1)}, bf16[208,512]{1,0:T(8,128)(2,1)S(1)}, u32[]{:S(2)}, u32[]{:S(2)}) collective-permute-start(bf16[208,512]{1,0:T(8,128)(2,1)S(1)} %collective-permute-done.refs_6_), channel_id=1, source_target_pairs={{0,4},{1,5},{2,6},{3,7},{4,0},{5,1},{6,2},{7,3},{8,12},{9,13},{10,... | collective-permute-start | bytes 638984 | tf_op jit(solution)/shard_map/ppermute | solution.py:294
  21.2 0.0 collective-permute-done.7.refs_1_
  21.2 0.0 collective-permute-start.9
  21.2 0.1 pad_add_fusion.1.refs_11_
  21.3 0.1 pad_maximum_fusion.refs_7_.refs_12_.refs_10_
  21.4 0.0 collective-permute-done.4.refs_3_
  21.4 2.5 %shard_map.87 = (bf16[768,512]{1,0:T(8,128)(2,1)S(1)}, f32[8,768]{1,0:T(8,128)S(1)}, f32[1152,512]{1,0:T(8,128)S(1)}, f32[8,128]{1,0:T(8,128)S(1)}) custom-call(bf16[208,512]{1,0:T(8,128)(2,1)S(1)} %shard_map.86.refs_0_, bf16[208,512]{1,0:T(8,128)(2,1)S(1)} %collective-permute-done.2.refs_1_, bf16[208,512]{1,0:T(8,128)(2,1)S(1)} %collective-permute-done.3.refs_2_, ...), custom_call_target="tpu_custom_call" | custom-call | flops 1 | bytes 1 | tf_op jit(solution)/shard_map/pallas_call | solution.py:40
  23.9 0.0 collective-permute-done.8.refs_2_
  23.9 4.4 %shard_map.88 = (bf16[768,512]{1,0:T(8,128)(2,1)S(1)}, f32[8,768]{1,0:T(8,128)S(1)}, f32[768,512]{1,0:T(8,128)S(1)}, f32[768,512]{1,0:T(8,128)S(1)}, f32[576,512]{1,0:T(8,128)S(1)}, /*index=5*/f32[8,128]{1,0:T(8,128)S(1)}) custom-call(bf16[208,512]{1,0:T(8,128)(2,1)S(1)} %collective-permute-done.6.refs_0_, ...), custom_call_target="tpu_custom_call" | custom-call | flops 1 | bytes 1 | tf_op jit(solution)/shard_map/pallas_call | solution.py:40
  28.4 3.1 %shard_map.89 = (f32[768,512]{1,0:T(8,128)S(1)}, s16[832,512]{1,0:T(8,128)(2,1)S(1)}, f32[8,128]{1,0:T(8,128)S(1)}, s16[208,512]{1,0:T(8,128)(2,1)S(1)}, s16[208,512]{1,0:T(8,128)(2,1)S(1)}) custom-call(bf16[208,512]{1,0:T(8,128)(2,1)S(1)} %collective-permute-done.1.refs_0_, bf16[768,512]{1,0:T(8,128)(2,1)S(1)} %get-tuple-element.31.refs_7_.refs_1_, ...), custom_call_target="tpu_custom_call" | custom-call | flops 1 | bytes 1 | tf_op jit(solution)/shard_map/pallas_call | solution.py:40
  31.4 0.6 %collective-permute-start.10 = (s16[832,512]{1,0:T(8,128)(2,1)S(1)}, s16[832,512]{1,0:T(8,128)(2,1)S(1)}, u32[]{:S(2)}, u32[]{:S(2)}) collective-permute-start(s16[832,512]{1,0:T(8,128)(2,1)S(1)} %get-tuple-element.42), channel_id=1, source_target_pairs={{0,1},{1,0},{2,3},{3,2},{4,5},{5,4},{6,7},{7,6},{8,9},{9,8},{10,11... | collective-permute-start | bytes 2555912 | tf_op jit(solution)/shard_map/ppermute | solution.py:294
  32.0 0.1 collective-permute-start.11
  32.1 0.5 collective-permute-start.20
  32.6 1.4 %collective-permute-done.11.refs_3_ = f32[8,128]{1,0:T(8,128)S(1)} collective-permute-done((f32[8,128]{1,0:T(8,128)S(1)}, f32[8,128]{1,0:T(8,128)S(1)}, u32[]{:S(2)}, u32[]{:S(2)}) %collective-permute-start.11) | collective-permute-done | bytes 4128 | tf_op jit(solution)/shard_map/ppermute | solution.py:294
  34.0 0.3 shard_map.90
  34.4 0.7 %collective-permute-start.13 = (s16[208,512]{1,0:T(8,128)(2,1)S(1)}, s16[208,512]{1,0:T(8,128)(2,1)S(1)}, u32[]{:S(2)}, u32[]{:S(2)}) collective-permute-start(s16[208,512]{1,0:T(8,128)(2,1)S(1)} %get-tuple-element.45), channel_id=1, source_target_pairs={{0,2},{1,3},{2,0},{3,1},{4,6},{5,7},{6,4},{7,5},{8,10},{9,11},{10,... | collective-permute-start | bytes 638984 | tf_op jit(solution)/shard_map/ppermute | solution.py:294
  35.0 0.5 collective-permute-start.14
  35.5 2.4 %collective-permute-start.15 = (f32[8,128]{1,0:T(8,128)S(1)}, f32[8,128]{1,0:T(8,128)S(1)}, u32[]{:S(2)}, u32[]{:S(2)}) collective-permute-start(f32[8,128]{1,0:T(8,128)S(1)} %get-tuple-element.46.refs_3_), channel_id=1, source_target_pairs={{0,6},{1,7},{2,4},{3,5},{4,2},{5,3},{6,0},{7,1},{8,14},{9,15},{10,... | collective-permute-start | bytes 12296 | tf_op jit(solution)/shard_map/ppermute | solution.py:294
  37.9 0.5 collective-permute-start.19
  38.4 1.3 %collective-permute-done.20.refs_1_ = s16[208,512]{1,0:T(8,128)(2,1)S(1)} collective-permute-done((s16[208,512]{1,0:T(8,128)(2,1)S(1)}, s16[208,512]{1,0:T(8,128)(2,1)S(1)}, u32[]{:S(2)}, u32[]{:S(2)}) %collective-permute-start.20) | collective-permute-done | bytes 213024 | tf_op jit(solution)/shard_map/ppermute | solution.py:294
  39.7 0.2 shard_map.93
  39.9 0.0 copy-start
  39.9 0.1 collective-permute-start.21
  40.0 0.6 %collective-permute-start.12 = (s16[208,512]{1,0:T(8,128)(2,1)S(1)}, s16[208,512]{1,0:T(8,128)(2,1)S(1)}, u32[]{:S(2)}, u32[]{:S(2)}) collective-permute-start(s16[208,512]{1,0:T(8,128)(2,1)S(1)} %get-tuple-element.44), channel_id=1, source_target_pairs={{0,2},{1,3},{2,0},{3,1},{4,6},{5,7},{6,4},{7,5},{8,10},{9,11},{10,... | collective-permute-start | bytes 638984 | tf_op jit(solution)/shard_map/ppermute | solution.py:294
  40.6 1.4 %collective-permute-done.15.refs_5_ = f32[8,128]{1,0:T(8,128)S(1)} collective-permute-done((f32[8,128]{1,0:T(8,128)S(1)}, f32[8,128]{1,0:T(8,128)S(1)}, u32[]{:S(2)}, u32[]{:S(2)}) %collective-permute-start.15) | collective-permute-done | bytes 4128 | tf_op jit(solution)/shard_map/ppermute | solution.py:294
  42.1 0.2 shard_map.91
  42.3 0.0 copy-start.1
  42.3 1.6 %collective-permute-start.16 = (s16[208,512]{1,0:T(8,128)(2,1)S(1)}, s16[208,512]{1,0:T(8,128)(2,1)S(1)}, u32[]{:S(2)}, u32[]{:S(2)}) collective-permute-start(s16[208,512]{1,0:T(8,128)(2,1)S(1)} %get-tuple-element.47), channel_id=1, source_target_pairs={{0,8},{1,9},{2,10},{3,11},{4,12},{5,13},{6,14},{7,15},{8,0},{9,1},... | collective-permute-start | bytes 638984 | tf_op jit(solution)/shard_map/ppermute | solution.py:294
  43.9 1.5 %collective-permute-start.17 = (f32[8,128]{1,0:T(8,128)S(1)}, f32[8,128]{1,0:T(8,128)S(1)}, u32[]{:S(2)}, u32[]{:S(2)}) collective-permute-start(f32[8,128]{1,0:T(8,128)S(1)} %get-tuple-element.48.refs_4_), channel_id=1, source_target_pairs={{0,16},{1,17},{2,18},{3,19},{4,20},{5,21},{6,22},{7,23},{8,24},{9,... | collective-permute-start | bytes 12296 | tf_op jit(solution)/shard_map/ppermute | solution.py:294
  45.5 1.7 %collective-permute-start.18 = (f32[8,128]{1,0:T(8,128)S(1)}, f32[8,128]{1,0:T(8,128)S(1)}, u32[]{:S(2)}, u32[]{:S(2)}) collective-permute-start(f32[8,128]{1,0:T(8,128)S(1)} %get-tuple-element.48.refs_4_), channel_id=1, source_target_pairs={{0,24},{1,25},{2,26},{3,27},{4,28},{5,29},{6,30},{7,31},{8,16},{9,... | collective-permute-start | bytes 12296 | tf_op jit(solution)/shard_map/ppermute | solution.py:294
  47.2 5.1 %collective-permute-done.21.refs_2_ = s16[208,512]{1,0:T(8,128)(2,1)S(1)} collective-permute-done((s16[208,512]{1,0:T(8,128)(2,1)S(1)}, s16[208,512]{1,0:T(8,128)(2,1)S(1)}, u32[]{:S(2)}, u32[]{:S(2)}) %collective-permute-start.21) | collective-permute-done | bytes 213024 | tf_op jit(solution)/shard_map/ppermute | solution.py:294
  52.3 1.0 %shard_map.94 = f32[192,512]{1,0:T(8,128)} custom-call(bf16[192,512]{1,0:T(8,128)(2,1)S(1)} %copy-done, f32[576,512]{1,0:T(8,128)S(1)} %get-tuple-element.39.refs_7_.refs_0_, s16[208,512]{1,0:T(8,128)(2,1)S(1)} %collective-permute-done.19.refs_1_, s16[208,512]{1,0:T(8,128)(2,1)S(1)} %collective-permute-done.21.refs_2_), custom_call_target="tpu_custom_call" | custom-call | flops 1 | bytes 1 | tf_op jit(solution)/shard_map/pallas_call | solution.py:40
  53.4 0.2 collective-permute-done.16.refs_3_
  53.6 1.1 %shard_map.92 = (f32[192,512]{1,0:T(8,128)}, f32[1,1]{1,0:T(1,128)}) custom-call(bf16[192,512]{1,0:T(8,128)(2,1)S(1)} %copy-done.1, f32[768,512]{1,0:T(8,128)S(1)} %get-tuple-element.41.refs_0_, s16[832,512]{1,0:T(8,128)(2,1)S(1)} %collective-permute-done.10.refs_1_, s16[208,512]{1,0:T(8,128)(2,1)S(1)} %collective-permute-done.12.refs_2_, ...), custom_call_target="tpu_custom_call" | custom-call | flops 1 | bytes 1 | tf_op jit(solution)/shard_map/pallas_call | solution.py:40
  (13 shorter events, 0.0 us)
Async XLA Ops:
  2.0 8.3 %collective-permute-start.6 = (bf16[208,512]{1,0:T(8,128)(2,1)S(1)}, bf16[208,512]{1,0:T(8,128)(2,1)S(1)}, u32[]{:S(2)}, u32[]{:S(2)}) collective-permute-start(bf16[208,512]{1,0:T(8,128)(2,1)S(1)} %shard_map.86.refs_0_), channel_id=1, source_target_pairs={{0,8},{1,9},{2,10},{3,11},{4,12},{5,13},{6,14},{7,15},{8,0},{9,1},... | collective-permute-start | bytes 638984 | tf_op jit(solution)/shard_map/ppermute | solution.py:294
  5.1 12.3 %collective-permute-start.2 = (bf16[208,512]{1,0:T(8,128)(2,1)S(1)}, bf16[208,512]{1,0:T(8,128)(2,1)S(1)}, u32[]{:S(2)}, u32[]{:S(2)}) collective-permute-start(bf16[208,512]{1,0:T(8,128)(2,1)S(1)} %shard_map.86.refs_0_), channel_id=1, source_target_pairs={{0,2},{1,3},{2,0},{3,1},{4,6},{5,7},{6,4},{7,5},{8,10},{9,11},{10,... | collective-permute-start | bytes 638984 | tf_op jit(solution)/shard_map/ppermute | solution.py:294
  6.6 10.9 %collective-permute-start.3 = (bf16[208,512]{1,0:T(8,128)(2,1)S(1)}, bf16[208,512]{1,0:T(8,128)(2,1)S(1)}, u32[]{:S(2)}, u32[]{:S(2)}) collective-permute-start(bf16[208,512]{1,0:T(8,128)(2,1)S(1)} %shard_map.86.refs_0_), channel_id=1, source_target_pairs={{0,1},{1,0},{2,3},{3,2},{4,5},{5,4},{6,7},{7,6},{8,9},{9,8},{10,11... | collective-permute-start | bytes 638984 | tf_op jit(solution)/shard_map/ppermute | solution.py:294
  6.6 13.1 %collective-permute-start = (bf16[208,512]{1,0:T(8,128)(2,1)S(1)}, bf16[208,512]{1,0:T(8,128)(2,1)S(1)}, u32[]{:S(2)}, u32[]{:S(2)}) collective-permute-start(bf16[208,512]{1,0:T(8,128)(2,1)S(1)} %get-tuple-element.28.refs_4_), channel_id=1, source_target_pairs={{0,16},{1,17},{2,18},{3,19},{4,20},{5,21},{6,22},{7,23},{8,24},{9,... | collective-permute-start | bytes 638984 | tf_op jit(solution)/shard_map/ppermute | solution.py:294
  10.3 10.9 %collective-permute-start.7 = (bf16[208,512]{1,0:T(8,128)(2,1)S(1)}, bf16[208,512]{1,0:T(8,128)(2,1)S(1)}, u32[]{:S(2)}, u32[]{:S(2)}) collective-permute-start(bf16[208,512]{1,0:T(8,128)(2,1)S(1)} %collective-permute-done.6.refs_0_), channel_id=1, source_target_pairs={{0,2},{1,3},{2,0},{3,1},{4,6},{5,7},{6,4},{7,5},{8,10},{9,11},{10,... | collective-permute-start | bytes 638984 | tf_op jit(solution)/shard_map/ppermute | solution.py:294
  14.5 6.9 %collective-permute-start.5 = (bf16[208,512]{1,0:T(8,128)(2,1)S(1)}, bf16[208,512]{1,0:T(8,128)(2,1)S(1)}, u32[]{:S(2)}, u32[]{:S(2)}) collective-permute-start(bf16[208,512]{1,0:T(8,128)(2,1)S(1)} %get-tuple-element.28.refs_4_), channel_id=1, source_target_pairs={{0,4},{1,5},{2,6},{3,7},{4,0},{5,1},{6,2},{7,3},{8,12},{9,13},{10,... | collective-permute-start | bytes 638984 | tf_op jit(solution)/shard_map/ppermute | solution.py:294
  17.4 6.5 %collective-permute-start.8 = (bf16[208,512]{1,0:T(8,128)(2,1)S(1)}, bf16[208,512]{1,0:T(8,128)(2,1)S(1)}, u32[]{:S(2)}, u32[]{:S(2)}) collective-permute-start(bf16[208,512]{1,0:T(8,128)(2,1)S(1)} %collective-permute-done.6.refs_0_), channel_id=1, source_target_pairs={{0,1},{1,0},{2,3},{3,2},{4,5},{5,4},{6,7},{7,6},{8,9},{9,8},{10,11... | collective-permute-start | bytes 638984 | tf_op jit(solution)/shard_map/ppermute | solution.py:294
  17.5 3.9 %collective-permute-start.4 = (bf16[208,512]{1,0:T(8,128)(2,1)S(1)}, bf16[208,512]{1,0:T(8,128)(2,1)S(1)}, u32[]{:S(2)}, u32[]{:S(2)}) collective-permute-start(bf16[208,512]{1,0:T(8,128)(2,1)S(1)} %collective-permute-done.2.refs_1_), channel_id=1, source_target_pairs={{0,1},{1,0},{2,3},{3,2},{4,5},{5,4},{6,7},{7,6},{8,9},{9,8},{10,11... | collective-permute-start | bytes 638984 | tf_op jit(solution)/shard_map/ppermute | solution.py:294
  19.7 8.7 %collective-permute-start.1 = (bf16[208,512]{1,0:T(8,128)(2,1)S(1)}, bf16[208,512]{1,0:T(8,128)(2,1)S(1)}, u32[]{:S(2)}, u32[]{:S(2)}) collective-permute-start(bf16[208,512]{1,0:T(8,128)(2,1)S(1)} %collective-permute-done.refs_6_), channel_id=1, source_target_pairs={{0,4},{1,5},{2,6},{3,7},{4,0},{5,1},{6,2},{7,3},{8,12},{9,13},{10,... | collective-permute-start | bytes 638984 | tf_op jit(solution)/shard_map/ppermute | solution.py:294
  21.2 2.7 %collective-permute-start.9 = (bf16[208,512]{1,0:T(8,128)(2,1)S(1)}, bf16[208,512]{1,0:T(8,128)(2,1)S(1)}, u32[]{:S(2)}, u32[]{:S(2)}) collective-permute-start(bf16[208,512]{1,0:T(8,128)(2,1)S(1)} %collective-permute-done.7.refs_1_), channel_id=1, source_target_pairs={{0,1},{1,0},{2,3},{3,2},{4,5},{5,4},{6,7},{7,6},{8,9},{9,8},{10,11... | collective-permute-start | bytes 638984 | tf_op jit(solution)/shard_map/ppermute | solution.py:294
  31.4 2.6 %collective-permute-start.10 = (s16[832,512]{1,0:T(8,128)(2,1)S(1)}, s16[832,512]{1,0:T(8,128)(2,1)S(1)}, u32[]{:S(2)}, u32[]{:S(2)}) collective-permute-start(s16[832,512]{1,0:T(8,128)(2,1)S(1)} %get-tuple-element.42), channel_id=1, source_target_pairs={{0,1},{1,0},{2,3},{3,2},{4,5},{5,4},{6,7},{7,6},{8,9},{9,8},{10,11... | collective-permute-start | bytes 2555912 | tf_op jit(solution)/shard_map/ppermute | solution.py:294
  32.0 2.0 %collective-permute-start.11 = (f32[8,128]{1,0:T(8,128)S(1)}, f32[8,128]{1,0:T(8,128)S(1)}, u32[]{:S(2)}, u32[]{:S(2)}) collective-permute-start(f32[8,128]{1,0:T(8,128)S(1)} %get-tuple-element.43.refs_2_), channel_id=1, source_target_pairs={{0,1},{1,0},{2,3},{3,2},{4,5},{5,4},{6,7},{7,6},{8,9},{9,8},{10,11... | collective-permute-start | bytes 12296 | tf_op jit(solution)/shard_map/ppermute | solution.py:294
  32.1 7.6 %collective-permute-start.20 = (s16[208,512]{1,0:T(8,128)(2,1)S(1)}, s16[208,512]{1,0:T(8,128)(2,1)S(1)}, u32[]{:S(2)}, u32[]{:S(2)}) collective-permute-start(s16[208,512]{1,0:T(8,128)(2,1)S(1)} %get-tuple-element.52), channel_id=1, source_target_pairs={{0,4},{1,5},{2,6},{3,7},{4,0},{5,1},{6,2},{7,3},{8,12},{9,13},{10,... | collective-permute-start | bytes 638984 | tf_op jit(solution)/shard_map/ppermute | solution.py:294
  34.4 7.7 %collective-permute-start.13 = (s16[208,512]{1,0:T(8,128)(2,1)S(1)}, s16[208,512]{1,0:T(8,128)(2,1)S(1)}, u32[]{:S(2)}, u32[]{:S(2)}) collective-permute-start(s16[208,512]{1,0:T(8,128)(2,1)S(1)} %get-tuple-element.45), channel_id=1, source_target_pairs={{0,2},{1,3},{2,0},{3,1},{4,6},{5,7},{6,4},{7,5},{8,10},{9,11},{10,... | collective-permute-start | bytes 638984 | tf_op jit(solution)/shard_map/ppermute | solution.py:294
  35.0 5.0 %collective-permute-start.14 = (f32[8,128]{1,0:T(8,128)S(1)}, f32[8,128]{1,0:T(8,128)S(1)}, u32[]{:S(2)}, u32[]{:S(2)}) collective-permute-start(f32[8,128]{1,0:T(8,128)S(1)} %get-tuple-element.46.refs_3_), channel_id=1, source_target_pairs={{0,4},{1,5},{2,6},{3,7},{4,0},{5,1},{6,2},{7,3},{8,12},{9,13},{10,... | collective-permute-start | bytes 12296 | tf_op jit(solution)/shard_map/ppermute | solution.py:294
  35.5 6.6 %collective-permute-start.15 = (f32[8,128]{1,0:T(8,128)S(1)}, f32[8,128]{1,0:T(8,128)S(1)}, u32[]{:S(2)}, u32[]{:S(2)}) collective-permute-start(f32[8,128]{1,0:T(8,128)S(1)} %get-tuple-element.46.refs_3_), channel_id=1, source_target_pairs={{0,6},{1,7},{2,4},{3,5},{4,2},{5,3},{6,0},{7,1},{8,14},{9,15},{10,... | collective-permute-start | bytes 12296 | tf_op jit(solution)/shard_map/ppermute | solution.py:294
  37.9 7.5 %collective-permute-start.19 = (s16[208,512]{1,0:T(8,128)(2,1)S(1)}, s16[208,512]{1,0:T(8,128)(2,1)S(1)}, u32[]{:S(2)}, u32[]{:S(2)}) collective-permute-start(s16[208,512]{1,0:T(8,128)(2,1)S(1)} %get-tuple-element.51), channel_id=1, source_target_pairs={{0,4},{1,5},{2,6},{3,7},{4,0},{5,1},{6,2},{7,3},{8,12},{9,13},{10,... | collective-permute-start | bytes 638984 | tf_op jit(solution)/shard_map/ppermute | solution.py:294
  39.9 12.4 %copy-start = (bf16[192,512]{1,0:T(8,128)(2,1)S(1)}, bf16[192,512]{1,0:T(8,128)(2,1)}, u32[]{:S(2)}) copy-start(bf16[192,512]{1,0:T(8,128)(2,1)} %raw_ref.3) | copy-start | bytes 589828
  39.9 12.4 %collective-permute-start.21 = (s16[208,512]{1,0:T(8,128)(2,1)S(1)}, s16[208,512]{1,0:T(8,128)(2,1)S(1)}, u32[]{:S(2)}, u32[]{:S(2)}) collective-permute-start(s16[208,512]{1,0:T(8,128)(2,1)S(1)} %shard_map.93), channel_id=1, source_target_pairs={{0,16},{1,17},{2,18},{3,19},{4,20},{5,21},{6,22},{7,23},{8,24},{9,... | collective-permute-start | bytes 638984 | tf_op jit(solution)/shard_map/ppermute | solution.py:294
  40.0 13.3 %collective-permute-start.12 = (s16[208,512]{1,0:T(8,128)(2,1)S(1)}, s16[208,512]{1,0:T(8,128)(2,1)S(1)}, u32[]{:S(2)}, u32[]{:S(2)}) collective-permute-start(s16[208,512]{1,0:T(8,128)(2,1)S(1)} %get-tuple-element.44), channel_id=1, source_target_pairs={{0,2},{1,3},{2,0},{3,1},{4,6},{5,7},{6,4},{7,5},{8,10},{9,11},{10,... | collective-permute-start | bytes 638984 | tf_op jit(solution)/shard_map/ppermute | solution.py:294
  42.3 11.3 %copy-start.1 = (bf16[192,512]{1,0:T(8,128)(2,1)S(1)}, bf16[192,512]{1,0:T(8,128)(2,1)}, u32[]{:S(2)}) copy-start(bf16[192,512]{1,0:T(8,128)(2,1)} %raw_ref.2) | copy-start | bytes 589828
  42.3 11.3 %collective-permute-start.16 = (s16[208,512]{1,0:T(8,128)(2,1)S(1)}, s16[208,512]{1,0:T(8,128)(2,1)S(1)}, u32[]{:S(2)}, u32[]{:S(2)}) collective-permute-start(s16[208,512]{1,0:T(8,128)(2,1)S(1)} %get-tuple-element.47), channel_id=1, source_target_pairs={{0,8},{1,9},{2,10},{3,11},{4,12},{5,13},{6,14},{7,15},{8,0},{9,1},... | collective-permute-start | bytes 638984 | tf_op jit(solution)/shard_map/ppermute | solution.py:294
  43.9 9.4 %collective-permute-start.17 = (f32[8,128]{1,0:T(8,128)S(1)}, f32[8,128]{1,0:T(8,128)S(1)}, u32[]{:S(2)}, u32[]{:S(2)}) collective-permute-start(f32[8,128]{1,0:T(8,128)S(1)} %get-tuple-element.48.refs_4_), channel_id=1, source_target_pairs={{0,16},{1,17},{2,18},{3,19},{4,20},{5,21},{6,22},{7,23},{8,24},{9,... | collective-permute-start | bytes 12296 | tf_op jit(solution)/shard_map/ppermute | solution.py:294
  45.5 7.9 %collective-permute-start.18 = (f32[8,128]{1,0:T(8,128)S(1)}, f32[8,128]{1,0:T(8,128)S(1)}, u32[]{:S(2)}, u32[]{:S(2)}) collective-permute-start(f32[8,128]{1,0:T(8,128)S(1)} %get-tuple-element.48.refs_4_), channel_id=1, source_target_pairs={{0,24},{1,25},{2,26},{3,27},{4,28},{5,29},{6,30},{7,31},{8,16},{9,... | collective-permute-start | bytes 12296 | tf_op jit(solution)/shard_map/ppermute | solution.py:294

commit v3 on v2

--- a/solution.py
+++ b/solution.py
@@ -101,8 +101,9 @@
     return (coded * unit[None]).reshape(piece, width)
 
 
-def decode_loss(ref, rows):
-    exponent, high, low = jnp.split(ref[pl.ds(rows, AUX), :].astype(F32)[SUB:, :384], 3, axis=1)
+def decode_loss(ref):
+    aux = pl.ds(ref.shape[0] - AUX, AUX)
+    exponent, high, low = jnp.split(ref[aux, :].astype(F32)[SUB:, :384], 3, axis=1)
     return (high + low * (1.0 / LIMB)) * (1.0 / LIMB) * jnp.exp2(exponent)
 
 
@@ -157,8 +158,20 @@
     return grad, loss
 
 
-def early_kernel(rows, n, p_n, *refs):
-    msgs, params, (base, coef) = refs[:n], refs[n : n + p_n], refs[n + p_n : n + p_n + 2]
+def scalars(refs, masks, columns_n, rows, width):
+    me = lax.axis_index("row") * columns_n + lax.axis_index("col")
+    return [(me ^ m) * rows for m in masks], (refs[0][0] * (1.0 / width), refs[1][0])
+
+
+def tables(refs, masks, columns_n, rows, width):
+    return [refs[0][i] for i in range(len(masks))], (refs[1][0], refs[1][1])
+
+
+def early_kernel(rows, n, masks, columns_n, *refs):
+    p_n = len(masks)
+    msgs, params = refs[:n], refs[n : n + p_n]
+    width = msgs[0].shape[1]
+    base, coef = tables(refs[n + p_n : n + p_n + 2], masks, columns_n, rows, width)
     data, side, acc, loss_out = refs[n + p_n + 2 :]
     cols = n * rows
     load_data(msgs, data, side, rows)
@@ -175,9 +188,12 @@
     loss_out[...] = loss
 
 
-def middle_kernel(rows, n, p_n, m_n, *refs):
+def middle_kernel(rows, n, p_n, masks, columns_n, *refs):
+    m_n = len(masks) - p_n
     msgs, params = refs[:n], refs[n : n + p_n + m_n]
-    data0, side0, acc0, loss_in, base, coef = refs[n + p_n + m_n : n + p_n + m_n + 6]
+    data0, side0, acc0, loss_in = refs[n + p_n + m_n : n + p_n + m_n + 4]
+    width = msgs[0].shape[1]
+    base, coef = scalars(refs[n + p_n + m_n + 4 : n + p_n + m_n + 6], masks, columns_n, rows, width)
     data, side, acc0_out, acc, parts, loss_out = refs[n + p_n + m_n + 6 :]
     cols = n * rows
     whole = pl.ds(0, cols)
@@ -205,12 +221,15 @@
     loss_out[...] = loss
 
 
-def late_kernel(rows, n, l_n, ready, *refs):
+def late_kernel(rows, n, masks, columns_n, ready, *refs):
+    l_n = len(masks)
     params = refs[:l_n]
-    data0, side0, acc0, data1, side1, acc1, parts, loss_in, base, coef = refs[l_n : l_n + 10]
+    data0, side0, acc0, data1, side1, acc1, parts, loss_in = refs[l_n : l_n + 8]
+    width = params[0].shape[1]
+    base, coef = scalars(refs[l_n + 8 : l_n + 10], masks, columns_n, rows, width)
     outs = refs[l_n + 10 :]
-    keep_d, send_d, loss_out = outs[:3]
-    send_p = outs[3:]
+    keep_d, low_d, top_d, loss_out = outs[:4]
+    send_p = outs[4:]
     loss = loss_in[...]
     half = n // 2
     for k, s in enumerate(ready):
@@ -229,9 +248,13 @@
                 acc[...] = d_part
                 continue
             for i in range(half):
-                keep_d[pl.ds((2 * i + h) * rows, rows), :] = d_part[i * rows : (i + 1) * rows]
+                place = 2 * i + h
+                keep_d[pl.ds(place * rows, rows), :] = d_part[i * rows : (i + 1) * rows]
+                send_d = top_d if place >= half else low_d
                 at = half + i
-                encode(d_part[at * rows : (at + 1) * rows], send_d, (2 * i + h) * (rows + AUX))
+                part = d_part[at * rows : (at + 1) * rows]
+                with_loss = loss if place == n - 1 else None
+                encode(part, send_d, place % half * (rows + AUX), with_loss)
         encode(total, send_p[len(ready) + s], 0)
     loss_out[...] = loss
 
@@ -243,7 +266,7 @@
         outs = terms
     else:
         terms, outs = terms[: -len(plan) - 1], terms[-len(plan) - 1 :]
-        loss = sum([t[...] for t in terms] + [decode_loss(arrays[a], rows) for a in carried])
+        loss = sum([t[...] for t in terms] + [decode_loss(arrays[a]) for a in carried])
         outs[-1][...] = loss
     for out, (b, start, parts) in zip(outs, plan):
         total = arrays[b][pl.ds(start * rows, rows), :]
@@ -252,27 +275,30 @@
         encode(total, out, 0, loss)
 
 
-def finish_kernel(rows, plan, pairs, raw_ref, *refs):
-    start, parts, arrays, carried = plan
-    out_vmem, loss_vmem, sems = refs[-3:]
-    out_ref = refs[-5] if pairs else refs[-4]
+def finish_kernel(rows, plans, n_arrays, carried, pairs, *refs):
+    arrays, terms, outs = refs[:n_arrays], refs[n_arrays:-7], refs[-7:-4]
+    buffers, loss_vmem, sems = refs[-4:-2], refs[-2], refs[-1]
     copies = []
-    if pairs:
-        terms = [t[...] for t in refs[arrays:-5]] + [decode_loss(refs[a], rows) for a in carried]
-        loss_vmem[...] = jnp.sum(sum(terms), keepdims=True) / (pairs * pairs)
-        copies.append(pltpu.make_async_copy(loss_vmem, refs[-4], sems.at[0]))
+
+    def send(a, b):
+        copies.append(pltpu.make_async_copy(a, b, sems.at[len(copies)]))
         copies[-1].start()
+
     piece = rows // 3 if rows % (3 * AUX) == 0 else rows
-    for k, at in enumerate(range(0, rows, piece)):
-        full, scale = normalize(raw_ref[pl.ds(at, piece), :])
-        dnorm = refs[0][pl.ds(start * rows + at, piece), :]
-        for a, i in parts:
-            dnorm = dnorm + decode(refs[a], i * (rows + AUX), rows, at, piece)
-        grad = scale * (dnorm - full * jnp.mean(dnorm * full, axis=-1, keepdims=True))
-        here = pl.ds(at, piece)
-        out_vmem[here, :] = grad
-        copies.append(pltpu.make_async_copy(out_vmem.at[here], out_ref.at[here], sems.at[1 + k]))
-        copies[-1].start()
+    for k, (raw, base, start, parts) in enumerate(plans):
+        for at in range(0, rows, piece):
+            full, scale = normalize(arrays[raw][pl.ds(at, piece), :])
+            dnorm = arrays[base][pl.ds(start * rows + at, piece), :]
+            for a, i in parts:
+                dnorm = dnorm + decode(arrays[a], i * (rows + AUX), rows, at, piece)
+            here = pl.ds(at, piece)
+            mean = jnp.mean(dnorm * full, axis=-1, keepdims=True)
+            buffers[k][here, :] = scale * (dnorm - full * mean)
+            send(buffers[k].at[here], outs[k].at[here])
+        if k == 0:
+            values = [t[...] for t in terms] + [decode_loss(arrays[a]) for a in carried]
+            loss_vmem[...] = jnp.sum(sum(values), keepdims=True) / (pairs * pairs)
+            send(loss_vmem, outs[2])
     for copy in copies:
         copy.wait()
 
@@ -316,18 +342,20 @@
             held_d += [swap(x, bits_data[k]) for x in held_d]
     n_own, n_param = len(held_d), len(held_p)
     other_d = [swap(x, core) for x in held_d]
-    me = lax.axis_index("row") * sizes["col"] + lax.axis_index("col")
-    coef = jnp.stack([gain[0] / width, shift[0]])
+    columns = sizes["col"]
+    coef = (gain, shift)
+    me = lax.axis_index("row") * columns + lax.axis_index("col")
+    both = jnp.stack([gain[0] / width, shift[0]])
+    where = lambda g: (jnp.stack([(me ^ masks_p[i]) * rows for i in g]).astype(jnp.int32), both)
     n = n_own
     cols = n * rows
     late = [i for i in range(n_param) if i == n_param - 1]
     early = [i for i in range(n_param) if i not in late and not i & 1]
     middle = [i for i in range(n_param) if i not in late and i & 1]
     order = early + middle
-    base = {i: (me ^ masks_p[i]) * rows for i in range(n_param)}
-    bases = lambda group: jnp.stack([base[i] for i in group]).astype(jnp.int32)
+    pick = lambda group: [masks_p[i] for i in group]
     data0, side0, acc0, loss = call(
-        functools.partial(early_kernel, rows, n, len(early)),
+        functools.partial(early_kernel, rows, n, pick(early), columns),
         [
             shape((cols, width), BF16),
             shape((8, cols), F32),
@@ -335,9 +363,9 @@
             shape((8, 128), F32),
         ],
         [VMEM] * (n + len(early)) + [SMEM] * 2,
-    )(*held_d[0::2], *other_d[0::2], *[held_p[i] for i in early], bases(early), coef)
+    )(*held_d[0::2], *other_d[0::2], *[held_p[i] for i in early], *where(early))
     data1, side1, acc0, acc1, parts, loss = call(
-        functools.partial(middle_kernel, rows, n, len(early), len(middle)),
+        functools.partial(middle_kernel, rows, n, len(early), pick(order), columns),
         [
             shape((cols, width), BF16),
             shape((8, cols), F32),
@@ -348,29 +376,30 @@
         ],
         [VMEM] * (n + len(order) + 4) + [SMEM] * 2,
     )(
-        *held_d[1::2], *other_d[1::2], *[held_p[i] for i in order], data0, side0, acc0, loss, bases(order), coef
+        *held_d[1::2], *other_d[1::2], *[held_p[i] for i in order], data0, side0, acc0, loss, *coef
     )
     top = n_param // 2
     ready = [k for k, i in enumerate(order) if i >= top]
     sent = [order[k] for k in ready] + late
-    keep_d, send_d, loss, *send_p = call(
-        functools.partial(late_kernel, rows, n, len(late), ready),
+    keep_d, low_d, top_d, loss, *send_p = call(
+        functools.partial(late_kernel, rows, n, pick(late), columns, ready),
         [
             shape((n * rows, width), F32),
-            shape((n * msg, width), I16),
+            *[shape((n // 2 * msg, width), I16)] * 2,
             shape((8, 128), F32),
             *[shape((msg, width), I16)] * len(sent),
         ],
         [VMEM] * (len(late) + 8) + [SMEM] * 2,
     )(
         *[held_p[i] for i in late],
-        data0, side0, acc0, data1, side1, acc1, parts, loss, bases(late), coef,
+        data0, side0, acc0, data1, side1, acc1, parts, loss, *coef,
     )
     columns = sizes["col"]
     inner = [b for b in bits_data + bits_param if b < columns]
     outer = [b for b in bits_data + bits_param if b >= columns]
     rounds = [inner, outer]
-    terms, carriers = [loss, swap(loss, core)], []
+    got_top, got_low = swap(top_d, core), swap(low_d, core)
+    terms, carriers = [loss], [got_top]
 
     def emit(items, step, with_loss):
         nonlocal terms, carriers
@@ -403,8 +432,8 @@
             carriers = got[-1:] if step in bits else []
         return got
 
-    got = swap(send_d, core)
-    items_d = [(keep_d, i, [(got, i)]) for i in range(n_own)]
+    half = n_own // 2
+    items_d = [(keep_d, i, [(got_top if i >= half else got_low, i % half)]) for i in range(n_own)]
     items_p = [(parts, order.index(i), []) for i in range(top)]
     got = {i: swap(x, bits_param[-1]) for i, x in zip(sent, send_p)}
     for i in range(top):
@@ -417,31 +446,30 @@
                 for i, x in enumerate(emit(items[half:], step, items is items_d)):
                     items[i][2].append((x, 0))
                 del items[half:]
-    def finish(raw, item, terms=(), carriers=(), pairs=0):
-        arrays, at, parts = [item[0]], item[1], []
-        for x, i in item[2]:
+    arrays = []
+
+    def slot(x):
+        places = [i for i, y in enumerate(arrays) if y is x]
+        if not places:
             arrays.append(x)
-            parts.append((len(arrays) - 1, i))
-        carried = []
-        for x in carriers:
-            places = [a for a, y in enumerate(arrays) if y is x]
-            if not places:
-                arrays.append(x)
-            carried.append(places[0] if places else len(arrays) - 1)
-        return call(
-            functools.partial(finish_kernel, rows, (at, parts, len(arrays), carried), pairs),
-            [shape((rows, width), F32)] + [shape((1, 1), F32)] * bool(pairs),
-            [VMEM] * (1 + len(arrays) + len(terms)),
-            [
-                pltpu.VMEM((rows, width), F32),
-                pltpu.VMEM((1, 1), F32),
-                pltpu.SemaphoreType.DMA((4,)),
-            ],
-            to=pltpu.HBM,
-        )(raw, *arrays, *terms)
-
-    (grad_param,) = finish(param, items_p[0])
-    grad_data, loss = finish(data, items_d[0], terms, carriers, rows * devices)
+        return places[0] if places else len(arrays) - 1
+
+    plans = [
+        (slot(raw), slot(item[0]), item[1], [(slot(x), i) for x, i in item[2]])
+        for raw, item in ((param, items_p[0]), (data, items_d[0]))
+    ]
+    carried = [slot(x) for x in carriers]
+    grad_param, grad_data, loss = call(
+        functools.partial(finish_kernel, rows, plans, len(arrays), carried, rows * devices),
+        [shape((rows, width), F32)] * 2 + [shape((1, 1), F32)],
+        [VMEM] * (len(arrays) + len(terms)),
+        [
+            *[pltpu.VMEM((rows, width), F32)] * 2,
+            pltpu.VMEM((1, 1), F32),
+            pltpu.SemaphoreType.DMA((7,)),
+        ],
+        to=pltpu.HBM,
+    )(*arrays, *terms)
     return loss.reshape(1), grad_data, grad_param
 
 

time: 54.9 us -> 54 us (0.984)
  Pallas kernels: 14.2 us -> 12.3 us
  starting transfers between devices: 25.7 us -> 26.8 us
    pallas_call x10 -> x9, Pallas kernels: 14.2 us -> 12.3 us  [run(): return inner(*args)]
    ppermute x22, starting transfers between devices: 25.7 us -> 26.8 us  [swap(): lax.ppermute(x, ('row', 'col'), [(i, i ^ mask) for i in range(devices)])]
  transfers between devices with their start and end apart: 22 -> 22, of which waited for: 7 -> 8; matrix products, arithmetic and copies ran while one was open for 0% -> 0% of each run, Pallas kernels for 16% -> 13%
where the time goes in v3:
time: 54 us; the launch traced here: 53.8 us
  starting transfers between devices  26.8 us (50%)
  waiting for transfers between devices  12.4 us (23%)
  Pallas kernels  12.3 us (23%)
  between operations  2.05 us (4%)
    ppermute x22, starting transfers between devices, swap(): lax.ppermute(x, ('row', 'col'), [(i, i ^ mask) for i in range(devices)])  26.8 us
    ppermute x22, waiting for transfers between devices, swap(): lax.ppermute(x, ('row', 'col'), [(i, i ^ mask) for i in range(devices)])  12.4 us
    pallas_call x9, Pallas kernels, run(): return inner(*args)  12.3 us
  transfers between devices with their start and end apart: 22, of which 8 were waited for; matrix products, arithmetic and copies ran while one was open for 0% of the time, Pallas kernels for 13%

profile of v3, /device:TPU:0, one launch (start us, length us, event | category | flops | bytes accessed | tf_op | source)
XLA Modules:
  0.0 53.8 jit_solution(5069915174129248442)
XLA Ops:
  0.6 1.2 %shard_map.85 = (bf16[208,512]{1,0:T(8,128)(2,1)S(1)}, bf16[192,512]{1,0:T(8,128)(2,1)S(1)}, bf16[16,512]{1,0:T(8,128)(2,1)S(1)}) custom-call(bf16[192,512]{1,0:T(8,128)(2,1)} %refs_4_.1, bf16[192,512]{1,0:T(8,128)(2,1)} %refs_0_.1, s32[1,192]{1,0:T(1,128)} %bitcast.5, s32[1,192]{1,0:T(1,128)} %bitcast.6), custom_call_target="tpu_custom_call" | custom-call | flops 1 | bytes 1 | tf_op jit(solution)/shard_map/pallas_call | solution.py:40
  1.9 0.1 shard_map.86.refs_0_
  2.0 3.1 %collective-permute-start = (bf16[208,512]{1,0:T(8,128)(2,1)S(1)}, bf16[208,512]{1,0:T(8,128)(2,1)S(1)}, u32[]{:S(2)}, u32[]{:S(2)}) collective-permute-start(bf16[208,512]{1,0:T(8,128)(2,1)S(1)} %shard_map.86.refs_0_), channel_id=1, source_target_pairs={{0,8},{1,9},{2,10},{3,11},{4,12},{5,13},{6,14},{7,15},{8,0},{9,1},... | collective-permute-start | bytes 638984 | tf_op jit(solution)/shard_map/ppermute | solution.py:320
  5.1 1.5 %collective-permute-start.6 = (bf16[208,512]{1,0:T(8,128)(2,1)S(1)}, bf16[208,512]{1,0:T(8,128)(2,1)S(1)}, u32[]{:S(2)}, u32[]{:S(2)}) collective-permute-start(bf16[208,512]{1,0:T(8,128)(2,1)S(1)} %shard_map.86.refs_0_), channel_id=1, source_target_pairs={{0,2},{1,3},{2,0},{3,1},{4,6},{5,7},{6,4},{7,5},{8,10},{9,11},{10,... | collective-permute-start | bytes 638984 | tf_op jit(solution)/shard_map/ppermute | solution.py:320
  6.6 2.6 %collective-permute-start.5 = (bf16[208,512]{1,0:T(8,128)(2,1)S(1)}, bf16[208,512]{1,0:T(8,128)(2,1)S(1)}, u32[]{:S(2)}, u32[]{:S(2)}) collective-permute-start(bf16[208,512]{1,0:T(8,128)(2,1)S(1)} %get-tuple-element.32.refs_4_), channel_id=1, source_target_pairs={{0,16},{1,17},{2,18},{3,19},{4,20},{5,21},{6,22},{7,23},{8,24},{9,... | collective-permute-start | bytes 638984 | tf_op jit(solution)/shard_map/ppermute | solution.py:320
  9.2 1.2 %collective-permute-done.refs_0_ = bf16[208,512]{1,0:T(8,128)(2,1)S(1)} collective-permute-done((bf16[208,512]{1,0:T(8,128)(2,1)S(1)}, bf16[208,512]{1,0:T(8,128)(2,1)S(1)}, u32[]{:S(2)}, u32[]{:S(2)}) %collective-permute-start) | collective-permute-done | bytes 213024 | tf_op jit(solution)/shard_map/ppermute | solution.py:320
  10.3 4.2 %collective-permute-start.1 = (bf16[208,512]{1,0:T(8,128)(2,1)S(1)}, bf16[208,512]{1,0:T(8,128)(2,1)S(1)}, u32[]{:S(2)}, u32[]{:S(2)}) collective-permute-start(bf16[208,512]{1,0:T(8,128)(2,1)S(1)} %collective-permute-done.refs_0_), channel_id=1, source_target_pairs={{0,2},{1,3},{2,0},{3,1},{4,6},{5,7},{6,4},{7,5},{8,10},{9,11},{10,... | collective-permute-start | bytes 638984 | tf_op jit(solution)/shard_map/ppermute | solution.py:320
  14.5 1.5 %collective-permute-start.4 = (bf16[208,512]{1,0:T(8,128)(2,1)S(1)}, bf16[208,512]{1,0:T(8,128)(2,1)S(1)}, u32[]{:S(2)}, u32[]{:S(2)}) collective-permute-start(bf16[208,512]{1,0:T(8,128)(2,1)S(1)} %get-tuple-element.32.refs_4_), channel_id=1, source_target_pairs={{0,4},{1,5},{2,6},{3,7},{4,0},{5,1},{6,2},{7,3},{8,12},{9,13},{10,... | collective-permute-start | bytes 638984 | tf_op jit(solution)/shard_map/ppermute | solution.py:320
  17.3 0.0 collective-permute-done.6.refs_1_
  17.3 0.1 collective-permute-start.2
  17.4 0.0 collective-permute-done.7.refs_2_
  17.4 0.5 collective-permute-start.8
  17.9 1.8 %collective-permute-done.5.refs_6_ = bf16[208,512]{1,0:T(8,128)(2,1)S(1)} collective-permute-done((bf16[208,512]{1,0:T(8,128)(2,1)S(1)}, bf16[208,512]{1,0:T(8,128)(2,1)S(1)}, u32[]{:S(2)}, u32[]{:S(2)}) %collective-permute-start.5) | collective-permute-done | bytes 213024 | tf_op jit(solution)/shard_map/ppermute | solution.py:320
  19.7 1.5 %collective-permute-start.9 = (bf16[208,512]{1,0:T(8,128)(2,1)S(1)}, bf16[208,512]{1,0:T(8,128)(2,1)S(1)}, u32[]{:S(2)}, u32[]{:S(2)}) collective-permute-start(bf16[208,512]{1,0:T(8,128)(2,1)S(1)} %collective-permute-done.5.refs_6_), channel_id=1, source_target_pairs={{0,4},{1,5},{2,6},{3,7},{4,0},{5,1},{6,2},{7,3},{8,12},{9,13},{10,... | collective-permute-start | bytes 638984 | tf_op jit(solution)/shard_map/ppermute | solution.py:320
  21.2 0.1 pad_add_fusion.refs_6_
  21.3 0.1 pad_maximum_fusion.refs_7_
  21.4 0.0 collective-permute-done.4.refs_5_
  21.4 2.5 %shard_map.87 = (bf16[768,512]{1,0:T(8,128)(2,1)S(1)}, f32[8,768]{1,0:T(8,128)S(1)}, f32[1152,512]{1,0:T(8,128)S(1)}, f32[8,128]{1,0:T(8,128)S(1)}) custom-call(bf16[208,512]{1,0:T(8,128)(2,1)S(1)} %shard_map.86.refs_0_, bf16[208,512]{1,0:T(8,128)(2,1)S(1)} %collective-permute-done.6.refs_1_, bf16[208,512]{1,0:T(8,128)(2,1)S(1)} %collective-permute-done.7.refs_2_, ...), custom_call_target="tpu_custom_call" | custom-call | flops 1 | bytes 1 | tf_op jit(solution)/shard_map/pallas_call | solution.py:40
  23.9 0.0 collective-permute-done.2.refs_2_
  23.9 0.0 collective-permute-done.3.refs_3_
  23.9 3.8 %shard_map.88 = (bf16[768,512]{1,0:T(8,128)(2,1)S(1)}, f32[8,768]{1,0:T(8,128)S(1)}, f32[768,512]{1,0:T(8,128)S(1)}, f32[768,512]{1,0:T(8,128)S(1)}, f32[576,512]{1,0:T(8,128)S(1)}, /*index=5*/f32[8,128]{1,0:T(8,128)S(1)}) custom-call(bf16[208,512]{1,0:T(8,128)(2,1)S(1)} %collective-permute-done.refs_0_, ...), custom_call_target="tpu_custom_call" | custom-call | flops 1 | bytes 1 | tf_op jit(solution)/shard_map/pallas_call | solution.py:40
  27.8 2.4 %shard_map.89 = (f32[768,512]{1,0:T(8,128)S(1)}, s16[416,512]{1,0:T(8,128)(2,1)S(1)}, s16[416,512]{1,0:T(8,128)(2,1)S(1)}, f32[8,128]{1,0:T(8,128)S(1)}, s16[208...) custom-call(bf16[208,512]{1,0:T(8,128)(2,1)S(1)} %collective-permute-done.9.refs_0_, ...), custom_call_target="tpu_custom_call" | custom-call | flops 1 | bytes 1 | tf_op jit(solution)/shard_map/pallas_call | solution.py:40
  30.2 0.6 %collective-permute-start.14 = (s16[416,512]{1,0:T(8,128)(2,1)S(1)}, s16[416,512]{1,0:T(8,128)(2,1)S(1)}, u32[]{:S(2)}, u32[]{:S(2)}) collective-permute-start(s16[416,512]{1,0:T(8,128)(2,1)S(1)} %get-tuple-element.47), channel_id=1, source_target_pairs={{0,1},{1,0},{2,3},{3,2},{4,5},{5,4},{6,7},{7,6},{8,9},{9,8},{10,11... | collective-permute-start | bytes 1277960 | tf_op jit(solution)/shard_map/ppermute | solution.py:320
  30.8 0.1 collective-permute-start.13
  30.9 0.5 collective-permute-start.11
  31.4 0.8 %collective-permute-done.14.refs_1_ = s16[416,512]{1,0:T(8,128)(2,1)S(1)} collective-permute-done((s16[416,512]{1,0:T(8,128)(2,1)S(1)}, s16[416,512]{1,0:T(8,128)(2,1)S(1)}, u32[]{:S(2)}, u32[]{:S(2)}) %collective-permute-start.14) | collective-permute-done | bytes 426016 | tf_op jit(solution)/shard_map/ppermute | solution.py:320
  32.2 0.3 shard_map.91
  32.5 0.7 %collective-permute-start.16 = (s16[208,512]{1,0:T(8,128)(2,1)S(1)}, s16[208,512]{1,0:T(8,128)(2,1)S(1)}, u32[]{:S(2)}, u32[]{:S(2)}) collective-permute-start(s16[208,512]{1,0:T(8,128)(2,1)S(1)} %get-tuple-element.50), channel_id=1, source_target_pairs={{0,2},{1,3},{2,0},{3,1},{4,6},{5,7},{6,4},{7,5},{8,10},{9,11},{10,... | collective-permute-start | bytes 638984 | tf_op jit(solution)/shard_map/ppermute | solution.py:320
  33.2 0.7 %collective-permute-start.17 = (f32[8,128]{1,0:T(8,128)S(1)}, f32[8,128]{1,0:T(8,128)S(1)}, u32[]{:S(2)}, u32[]{:S(2)}) collective-permute-start(f32[8,128]{1,0:T(8,128)S(1)} %get-tuple-element.51.refs_3_), channel_id=1, source_target_pairs={{0,4},{1,5},{2,6},{3,7},{4,0},{5,1},{6,2},{7,3},{8,12},{9,13},{10,... | collective-permute-start | bytes 12296 | tf_op jit(solution)/shard_map/ppermute | solution.py:320
  33.9 2.2 %collective-permute-start.18 = (f32[8,128]{1,0:T(8,128)S(1)}, f32[8,128]{1,0:T(8,128)S(1)}, u32[]{:S(2)}, u32[]{:S(2)}) collective-permute-start(f32[8,128]{1,0:T(8,128)S(1)} %get-tuple-element.51.refs_3_), channel_id=1, source_target_pairs={{0,6},{1,7},{2,4},{3,5},{4,2},{5,3},{6,0},{7,1},{8,14},{9,15},{10,... | collective-permute-start | bytes 12296 | tf_op jit(solution)/shard_map/ppermute | solution.py:320
  36.1 2.4 %collective-permute-done.11.refs_1_ = s16[208,512]{1,0:T(8,128)(2,1)S(1)} collective-permute-done((s16[208,512]{1,0:T(8,128)(2,1)S(1)}, s16[208,512]{1,0:T(8,128)(2,1)S(1)}, u32[]{:S(2)}, u32[]{:S(2)}) %collective-permute-start.11) | collective-permute-done | bytes 213024 | tf_op jit(solution)/shard_map/ppermute | solution.py:320
  38.5 0.5 collective-permute-start.10
  39.0 0.2 shard_map.90
  39.2 0.0 collective-permute-done.13.refs_1_.refs_6_
  39.2 0.8 %collective-permute-start.12 = (s16[208,512]{1,0:T(8,128)(2,1)S(1)}, s16[208,512]{1,0:T(8,128)(2,1)S(1)}, u32[]{:S(2)}, u32[]{:S(2)}) collective-permute-start(s16[208,512]{1,0:T(8,128)(2,1)S(1)} %shard_map.90), channel_id=1, source_target_pairs={{0,16},{1,17},{2,18},{3,19},{4,20},{5,21},{6,22},{7,23},{8,24},{9,... | collective-permute-start | bytes 638984 | tf_op jit(solution)/shard_map/ppermute | solution.py:320
  40.1 0.6 %collective-permute-start.15 = (s16[208,512]{1,0:T(8,128)(2,1)S(1)}, s16[208,512]{1,0:T(8,128)(2,1)S(1)}, u32[]{:S(2)}, u32[]{:S(2)}) collective-permute-start(s16[208,512]{1,0:T(8,128)(2,1)S(1)} %get-tuple-element.49), channel_id=1, source_target_pairs={{0,2},{1,3},{2,0},{3,1},{4,6},{5,7},{6,4},{7,5},{8,10},{9,11},{10,... | collective-permute-start | bytes 638984 | tf_op jit(solution)/shard_map/ppermute | solution.py:320
  40.6 0.0 collective-permute-done.18.refs_5_
  40.6 0.0 collective-permute-done.16.refs_2_
  40.7 0.2 shard_map.92
  40.9 2.6 %collective-permute-start.19 = (s16[208,512]{1,0:T(8,128)(2,1)S(1)}, s16[208,512]{1,0:T(8,128)(2,1)S(1)}, u32[]{:S(2)}, u32[]{:S(2)}) collective-permute-start(s16[208,512]{1,0:T(8,128)(2,1)S(1)} %get-tuple-element.52), channel_id=1, source_target_pairs={{0,8},{1,9},{2,10},{3,11},{4,12},{5,13},{6,14},{7,15},{8,0},{9,1},... | collective-permute-start | bytes 638984 | tf_op jit(solution)/shard_map/ppermute | solution.py:320
  43.5 0.1 collective-permute-start.20
  43.6 1.7 %collective-permute-done.10.refs_2_ = s16[208,512]{1,0:T(8,128)(2,1)S(1)} collective-permute-done((s16[208,512]{1,0:T(8,128)(2,1)S(1)}, s16[208,512]{1,0:T(8,128)(2,1)S(1)}, u32[]{:S(2)}, u32[]{:S(2)}) %collective-permute-start.10) | collective-permute-done | bytes 213024 | tf_op jit(solution)/shard_map/ppermute | solution.py:320
  45.3 2.5 %collective-permute-start.21 = (f32[8,128]{1,0:T(8,128)S(1)}, f32[8,128]{1,0:T(8,128)S(1)}, u32[]{:S(2)}, u32[]{:S(2)}) collective-permute-start(f32[8,128]{1,0:T(8,128)S(1)} %get-tuple-element.53.refs_9_), channel_id=1, source_target_pairs={{0,24},{1,25},{2,26},{3,27},{4,28},{5,29},{6,30},{7,31},{8,16},{9,... | collective-permute-start | bytes 12296 | tf_op jit(solution)/shard_map/ppermute | solution.py:320
  47.8 3.3 %collective-permute-done.12.refs_3_ = s16[208,512]{1,0:T(8,128)(2,1)S(1)} collective-permute-done((s16[208,512]{1,0:T(8,128)(2,1)S(1)}, s16[208,512]{1,0:T(8,128)(2,1)S(1)}, u32[]{:S(2)}, u32[]{:S(2)}) %collective-permute-start.12) | collective-permute-done | bytes 213024 | tf_op jit(solution)/shard_map/ppermute | solution.py:320
  51.2 0.0 collective-permute-done.15.refs_7_
  51.2 0.1 collective-permute-done.20.refs_10_
  51.3 1.1 %collective-permute-done.19.refs_8_ = s16[208,512]{1,0:T(8,128)(2,1)S(1)} collective-permute-done((s16[208,512]{1,0:T(8,128)(2,1)S(1)}, s16[208,512]{1,0:T(8,128)(2,1)S(1)}, u32[]{:S(2)}, u32[]{:S(2)}) %collective-permute-start.19) | collective-permute-done | bytes 213024 | tf_op jit(solution)/shard_map/ppermute | solution.py:320
  52.4 1.5 %shard_map.93 = (f32[192,512]{1,0:T(8,128)}, f32[192,512]{1,0:T(8,128)}, f32[1,1]{1,0:T(1,128)}) custom-call(bf16[192,512]{1,0:T(8,128)(2,1)S(1)} %copy-done, f32[576,512]{1,0:T(8,128)S(1)} %get-tuple-element.37.refs_7_.refs_0_.refs_1_, s16[208,512]{1,0:T(8,128)(2,1)S(1)} %collective-permute-done.10.refs_2_, ...), custom_call_target="tpu_custom_call" | custom-call | flops 1 | bytes 1 | tf_op jit(solution)/shard_map/pallas_call | solution.py:40
  (11 shorter events, 0.0 us)
Async XLA Ops:
  2.0 8.3 %collective-permute-start = (bf16[208,512]{1,0:T(8,128)(2,1)S(1)}, bf16[208,512]{1,0:T(8,128)(2,1)S(1)}, u32[]{:S(2)}, u32[]{:S(2)}) collective-permute-start(bf16[208,512]{1,0:T(8,128)(2,1)S(1)} %shard_map.86.refs_0_), channel_id=1, source_target_pairs={{0,8},{1,9},{2,10},{3,11},{4,12},{5,13},{6,14},{7,15},{8,0},{9,1},... | collective-permute-start | bytes 638984 | tf_op jit(solution)/shard_map/ppermute | solution.py:320
  5.1 12.3 %collective-permute-start.6 = (bf16[208,512]{1,0:T(8,128)(2,1)S(1)}, bf16[208,512]{1,0:T(8,128)(2,1)S(1)}, u32[]{:S(2)}, u32[]{:S(2)}) collective-permute-start(bf16[208,512]{1,0:T(8,128)(2,1)S(1)} %shard_map.86.refs_0_), channel_id=1, source_target_pairs={{0,2},{1,3},{2,0},{3,1},{4,6},{5,7},{6,4},{7,5},{8,10},{9,11},{10,... | collective-permute-start | bytes 638984 | tf_op jit(solution)/shard_map/ppermute | solution.py:320
  6.6 10.9 %collective-permute-start.7 = (bf16[208,512]{1,0:T(8,128)(2,1)S(1)}, bf16[208,512]{1,0:T(8,128)(2,1)S(1)}, u32[]{:S(2)}, u32[]{:S(2)}) collective-permute-start(bf16[208,512]{1,0:T(8,128)(2,1)S(1)} %shard_map.86.refs_0_), channel_id=1, source_target_pairs={{0,1},{1,0},{2,3},{3,2},{4,5},{5,4},{6,7},{7,6},{8,9},{9,8},{10,11... | collective-permute-start | bytes 638984 | tf_op jit(solution)/shard_map/ppermute | solution.py:320
  6.6 13.1 %collective-permute-start.5 = (bf16[208,512]{1,0:T(8,128)(2,1)S(1)}, bf16[208,512]{1,0:T(8,128)(2,1)S(1)}, u32[]{:S(2)}, u32[]{:S(2)}) collective-permute-start(bf16[208,512]{1,0:T(8,128)(2,1)S(1)} %get-tuple-element.32.refs_4_), channel_id=1, source_target_pairs={{0,16},{1,17},{2,18},{3,19},{4,20},{5,21},{6,22},{7,23},{8,24},{9,... | collective-permute-start | bytes 638984 | tf_op jit(solution)/shard_map/ppermute | solution.py:320
  10.3 10.9 %collective-permute-start.1 = (bf16[208,512]{1,0:T(8,128)(2,1)S(1)}, bf16[208,512]{1,0:T(8,128)(2,1)S(1)}, u32[]{:S(2)}, u32[]{:S(2)}) collective-permute-start(bf16[208,512]{1,0:T(8,128)(2,1)S(1)} %collective-permute-done.refs_0_), channel_id=1, source_target_pairs={{0,2},{1,3},{2,0},{3,1},{4,6},{5,7},{6,4},{7,5},{8,10},{9,11},{10,... | collective-permute-start | bytes 638984 | tf_op jit(solution)/shard_map/ppermute | solution.py:320
  14.5 6.9 %collective-permute-start.4 = (bf16[208,512]{1,0:T(8,128)(2,1)S(1)}, bf16[208,512]{1,0:T(8,128)(2,1)S(1)}, u32[]{:S(2)}, u32[]{:S(2)}) collective-permute-start(bf16[208,512]{1,0:T(8,128)(2,1)S(1)} %get-tuple-element.32.refs_4_), channel_id=1, source_target_pairs={{0,4},{1,5},{2,6},{3,7},{4,0},{5,1},{6,2},{7,3},{8,12},{9,13},{10,... | collective-permute-start | bytes 638984 | tf_op jit(solution)/shard_map/ppermute | solution.py:320
  17.3 6.6 %collective-permute-start.2 = (bf16[208,512]{1,0:T(8,128)(2,1)S(1)}, bf16[208,512]{1,0:T(8,128)(2,1)S(1)}, u32[]{:S(2)}, u32[]{:S(2)}) collective-permute-start(bf16[208,512]{1,0:T(8,128)(2,1)S(1)} %collective-permute-done.refs_0_), channel_id=1, source_target_pairs={{0,1},{1,0},{2,3},{3,2},{4,5},{5,4},{6,7},{7,6},{8,9},{9,8},{10,11... | collective-permute-start | bytes 638984 | tf_op jit(solution)/shard_map/ppermute | solution.py:320
  17.4 3.9 %collective-permute-start.8 = (bf16[208,512]{1,0:T(8,128)(2,1)S(1)}, bf16[208,512]{1,0:T(8,128)(2,1)S(1)}, u32[]{:S(2)}, u32[]{:S(2)}) collective-permute-start(bf16[208,512]{1,0:T(8,128)(2,1)S(1)} %collective-permute-done.6.refs_1_), channel_id=1, source_target_pairs={{0,1},{1,0},{2,3},{3,2},{4,5},{5,4},{6,7},{7,6},{8,9},{9,8},{10,11... | collective-permute-start | bytes 638984 | tf_op jit(solution)/shard_map/ppermute | solution.py:320
  19.7 8.1 %collective-permute-start.9 = (bf16[208,512]{1,0:T(8,128)(2,1)S(1)}, bf16[208,512]{1,0:T(8,128)(2,1)S(1)}, u32[]{:S(2)}, u32[]{:S(2)}) collective-permute-start(bf16[208,512]{1,0:T(8,128)(2,1)S(1)} %collective-permute-done.5.refs_6_), channel_id=1, source_target_pairs={{0,4},{1,5},{2,6},{3,7},{4,0},{5,1},{6,2},{7,3},{8,12},{9,13},{10,... | collective-permute-start | bytes 638984 | tf_op jit(solution)/shard_map/ppermute | solution.py:320
  21.2 2.7 %collective-permute-start.3 = (bf16[208,512]{1,0:T(8,128)(2,1)S(1)}, bf16[208,512]{1,0:T(8,128)(2,1)S(1)}, u32[]{:S(2)}, u32[]{:S(2)}) collective-permute-start(bf16[208,512]{1,0:T(8,128)(2,1)S(1)} %collective-permute-done.1.refs_1_), channel_id=1, source_target_pairs={{0,1},{1,0},{2,3},{3,2},{4,5},{5,4},{6,7},{7,6},{8,9},{9,8},{10,11... | collective-permute-start | bytes 638984 | tf_op jit(solution)/shard_map/ppermute | solution.py:320
  30.2 2.0 %collective-permute-start.14 = (s16[416,512]{1,0:T(8,128)(2,1)S(1)}, s16[416,512]{1,0:T(8,128)(2,1)S(1)}, u32[]{:S(2)}, u32[]{:S(2)}) collective-permute-start(s16[416,512]{1,0:T(8,128)(2,1)S(1)} %get-tuple-element.47), channel_id=1, source_target_pairs={{0,1},{1,0},{2,3},{3,2},{4,5},{5,4},{6,7},{7,6},{8,9},{9,8},{10,11... | collective-permute-start | bytes 1277960 | tf_op jit(solution)/shard_map/ppermute | solution.py:320
  30.8 8.4 %collective-permute-start.13 = (s16[416,512]{1,0:T(8,128)(2,1)S(1)}, s16[416,512]{1,0:T(8,128)(2,1)S(1)}, u32[]{:S(2)}, u32[]{:S(2)}) collective-permute-start(s16[416,512]{1,0:T(8,128)(2,1)S(1)} %get-tuple-element.46), channel_id=1, source_target_pairs={{0,1},{1,0},{2,3},{3,2},{4,5},{5,4},{6,7},{7,6},{8,9},{9,8},{10,11... | collective-permute-start | bytes 1277960 | tf_op jit(solution)/shard_map/ppermute | solution.py:320
  30.9 7.6 %collective-permute-start.11 = (s16[208,512]{1,0:T(8,128)(2,1)S(1)}, s16[208,512]{1,0:T(8,128)(2,1)S(1)}, u32[]{:S(2)}, u32[]{:S(2)}) collective-permute-start(s16[208,512]{1,0:T(8,128)(2,1)S(1)} %get-tuple-element.44), channel_id=1, source_target_pairs={{0,4},{1,5},{2,6},{3,7},{4,0},{5,1},{6,2},{7,3},{8,12},{9,13},{10,... | collective-permute-start | bytes 638984 | tf_op jit(solution)/shard_map/ppermute | solution.py:320
  32.5 8.1 %collective-permute-start.16 = (s16[208,512]{1,0:T(8,128)(2,1)S(1)}, s16[208,512]{1,0:T(8,128)(2,1)S(1)}, u32[]{:S(2)}, u32[]{:S(2)}) collective-permute-start(s16[208,512]{1,0:T(8,128)(2,1)S(1)} %get-tuple-element.50), channel_id=1, source_target_pairs={{0,2},{1,3},{2,0},{3,1},{4,6},{5,7},{6,4},{7,5},{8,10},{9,11},{10,... | collective-permute-start | bytes 638984 | tf_op jit(solution)/shard_map/ppermute | solution.py:320
  33.2 6.9 %collective-permute-start.17 = (f32[8,128]{1,0:T(8,128)S(1)}, f32[8,128]{1,0:T(8,128)S(1)}, u32[]{:S(2)}, u32[]{:S(2)}) collective-permute-start(f32[8,128]{1,0:T(8,128)S(1)} %get-tuple-element.51.refs_3_), channel_id=1, source_target_pairs={{0,4},{1,5},{2,6},{3,7},{4,0},{5,1},{6,2},{7,3},{8,12},{9,13},{10,... | collective-permute-start | bytes 12296 | tf_op jit(solution)/shard_map/ppermute | solution.py:320
  33.9 6.8 %collective-permute-start.18 = (f32[8,128]{1,0:T(8,128)S(1)}, f32[8,128]{1,0:T(8,128)S(1)}, u32[]{:S(2)}, u32[]{:S(2)}) collective-permute-start(f32[8,128]{1,0:T(8,128)S(1)} %get-tuple-element.51.refs_3_), channel_id=1, source_target_pairs={{0,6},{1,7},{2,4},{3,5},{4,2},{5,3},{6,0},{7,1},{8,14},{9,15},{10,... | collective-permute-start | bytes 12296 | tf_op jit(solution)/shard_map/ppermute | solution.py:320
  38.5 13.8 %copy-start = (bf16[192,512]{1,0:T(8,128)(2,1)S(1)}, bf16[192,512]{1,0:T(8,128)(2,1)}, u32[]{:S(2)}) copy-start(bf16[192,512]{1,0:T(8,128)(2,1)} %refs_0_.1) | copy-start | bytes 589828
  38.5 13.8 %copy-start.1 = (bf16[192,512]{1,0:T(8,128)(2,1)S(1)}, bf16[192,512]{1,0:T(8,128)(2,1)}, u32[]{:S(2)}) copy-start(bf16[192,512]{1,0:T(8,128)(2,1)} %refs_4_.1) | copy-start | bytes 589828
  38.5 6.8 %collective-permute-start.10 = (s16[208,512]{1,0:T(8,128)(2,1)S(1)}, s16[208,512]{1,0:T(8,128)(2,1)S(1)}, u32[]{:S(2)}, u32[]{:S(2)}) collective-permute-start(s16[208,512]{1,0:T(8,128)(2,1)S(1)} %get-tuple-element.43), channel_id=1, source_target_pairs={{0,4},{1,5},{2,6},{3,7},{4,0},{5,1},{6,2},{7,3},{8,12},{9,13},{10,... | collective-permute-start | bytes 638984 | tf_op jit(solution)/shard_map/ppermute | solution.py:320
  39.2 11.9 %collective-permute-start.12 = (s16[208,512]{1,0:T(8,128)(2,1)S(1)}, s16[208,512]{1,0:T(8,128)(2,1)S(1)}, u32[]{:S(2)}, u32[]{:S(2)}) collective-permute-start(s16[208,512]{1,0:T(8,128)(2,1)S(1)} %shard_map.90), channel_id=1, source_target_pairs={{0,16},{1,17},{2,18},{3,19},{4,20},{5,21},{6,22},{7,23},{8,24},{9,... | collective-permute-start | bytes 638984 | tf_op jit(solution)/shard_map/ppermute | solution.py:320
  40.1 11.1 %collective-permute-start.15 = (s16[208,512]{1,0:T(8,128)(2,1)S(1)}, s16[208,512]{1,0:T(8,128)(2,1)S(1)}, u32[]{:S(2)}, u32[]{:S(2)}) collective-permute-start(s16[208,512]{1,0:T(8,128)(2,1)S(1)} %get-tuple-element.49), channel_id=1, source_target_pairs={{0,2},{1,3},{2,0},{3,1},{4,6},{5,7},{6,4},{7,5},{8,10},{9,11},{10,... | collective-permute-start | bytes 638984 | tf_op jit(solution)/shard_map/ppermute | solution.py:320
  40.9 11.5 %collective-permute-start.19 = (s16[208,512]{1,0:T(8,128)(2,1)S(1)}, s16[208,512]{1,0:T(8,128)(2,1)S(1)}, u32[]{:S(2)}, u32[]{:S(2)}) collective-permute-start(s16[208,512]{1,0:T(8,128)(2,1)S(1)} %get-tuple-element.52), channel_id=1, source_target_pairs={{0,8},{1,9},{2,10},{3,11},{4,12},{5,13},{6,14},{7,15},{8,0},{9,1},... | collective-permute-start | bytes 638984 | tf_op jit(solution)/shard_map/ppermute | solution.py:320
  43.5 7.8 %collective-permute-start.20 = (f32[8,128]{1,0:T(8,128)S(1)}, f32[8,128]{1,0:T(8,128)S(1)}, u32[]{:S(2)}, u32[]{:S(2)}) collective-permute-start(f32[8,128]{1,0:T(8,128)S(1)} %get-tuple-element.53.refs_9_), channel_id=1, source_target_pairs={{0,16},{1,17},{2,18},{3,19},{4,20},{5,21},{6,22},{7,23},{8,24},{9,... | collective-permute-start | bytes 12296 | tf_op jit(solution)/shard_map/ppermute | solution.py:320
  45.3 6.0 %collective-permute-start.21 = (f32[8,128]{1,0:T(8,128)S(1)}, f32[8,128]{1,0:T(8,128)S(1)}, u32[]{:S(2)}, u32[]{:S(2)}) collective-permute-start(f32[8,128]{1,0:T(8,128)S(1)} %get-tuple-element.53.refs_9_), channel_id=1, source_target_pairs={{0,24},{1,25},{2,26},{3,27},{4,28},{5,29},{6,30},{7,31},{8,16},{9,... | collective-permute-start | bytes 12296 | tf_op jit(solution)/shard_map/ppermute | solution.py:320

commit v4 on v3

--- a/solution.py
+++ b/solution.py
@@ -275,30 +275,37 @@
         encode(total, out, 0, loss)
 
 
-def finish_kernel(rows, plans, n_arrays, carried, pairs, *refs):
-    arrays, terms, outs = refs[:n_arrays], refs[n_arrays:-7], refs[-7:-4]
-    buffers, loss_vmem, sems = refs[-4:-2], refs[-2], refs[-1]
+def backward(refs, plan, rows, at, piece):
+    raw, base, start, parts = plan
+    full, scale = normalize(refs[raw][pl.ds(at, piece), :])
+    dnorm = refs[base][pl.ds(start * rows + at, piece), :]
+    for a, i in parts:
+        dnorm = dnorm + decode(refs[a], i * (rows + AUX), rows, at, piece)
+    return scale * (dnorm - full * jnp.mean(dnorm * full, axis=-1, keepdims=True))
+
+
+def param_kernel(rows, plan, *refs):
+    refs[-1][...] = backward(refs, plan, rows, 0, rows)
+
+
+def finish_kernel(rows, plan, n_arrays, carried, pairs, ready, *refs):
+    arrays, terms, outs = refs[:n_arrays], refs[n_arrays:-6], refs[-6:-3]
+    buffer, loss_vmem, sems = refs[-3:]
     copies = []
 
     def send(a, b):
         copies.append(pltpu.make_async_copy(a, b, sems.at[len(copies)]))
         copies[-1].start()
 
+    send(ready, outs[0])
+    values = [t[...] for t in terms] + [decode_loss(arrays[a]) for a in carried]
+    loss_vmem[...] = jnp.sum(sum(values), keepdims=True) / (pairs * pairs)
+    send(loss_vmem, outs[2])
     piece = rows // 3 if rows % (3 * AUX) == 0 else rows
-    for k, (raw, base, start, parts) in enumerate(plans):
-        for at in range(0, rows, piece):
-            full, scale = normalize(arrays[raw][pl.ds(at, piece), :])
-            dnorm = arrays[base][pl.ds(start * rows + at, piece), :]
-            for a, i in parts:
-                dnorm = dnorm + decode(arrays[a], i * (rows + AUX), rows, at, piece)
-            here = pl.ds(at, piece)
-            mean = jnp.mean(dnorm * full, axis=-1, keepdims=True)
-            buffers[k][here, :] = scale * (dnorm - full * mean)
-            send(buffers[k].at[here], outs[k].at[here])
-        if k == 0:
-            values = [t[...] for t in terms] + [decode_loss(arrays[a]) for a in carried]
-            loss_vmem[...] = jnp.sum(sum(values), keepdims=True) / (pairs * pairs)
-            send(loss_vmem, outs[2])
+    for at in range(0, rows, piece):
+        here = pl.ds(at, piece)
+        buffer[here, :] = backward(arrays, plan, rows, at, piece)
+        send(buffer.at[here], outs[1].at[here])
     for copy in copies:
         copy.wait()
 
@@ -446,30 +453,34 @@
                 for i, x in enumerate(emit(items[half:], step, items is items_d)):
                     items[i][2].append((x, 0))
                 del items[half:]
-    arrays = []
-
-    def slot(x):
-        places = [i for i, y in enumerate(arrays) if y is x]
-        if not places:
-            arrays.append(x)
-        return places[0] if places else len(arrays) - 1
-
-    plans = [
-        (slot(raw), slot(item[0]), item[1], [(slot(x), i) for x, i in item[2]])
-        for raw, item in ((param, items_p[0]), (data, items_d[0]))
-    ]
-    carried = [slot(x) for x in carriers]
+    def plan_of(raw, item, more=()):
+        arrays = []
+
+        def slot(x):
+            places = [i for i, y in enumerate(arrays) if y is x]
+            if not places:
+                arrays.append(x)
+            return places[0] if places else len(arrays) - 1
+
+        plan = (slot(raw), slot(item[0]), item[1], [(slot(x), i) for x, i in item[2]])
+        return plan, [slot(x) for x in more], arrays
+
+    plan, _, arrays = plan_of(param, items_p[0])
+    (ready_p,) = call(
+        functools.partial(param_kernel, rows, plan), [shape((rows, width), F32)], [VMEM] * len(arrays)
+    )(*arrays)
+    plan, carried, arrays = plan_of(data, items_d[0], carriers)
     grad_param, grad_data, loss = call(
-        functools.partial(finish_kernel, rows, plans, len(arrays), carried, rows * devices),
+        functools.partial(finish_kernel, rows, plan, len(arrays), carried, rows * devices),
         [shape((rows, width), F32)] * 2 + [shape((1, 1), F32)],
-        [VMEM] * (len(arrays) + len(terms)),
+        [VMEM] * (1 + len(arrays) + len(terms)),
         [
-            *[pltpu.VMEM((rows, width), F32)] * 2,
+            pltpu.VMEM((rows, width), F32),
             pltpu.VMEM((1, 1), F32),
-            pltpu.SemaphoreType.DMA((7,)),
+            pltpu.SemaphoreType.DMA((5,)),
         ],
         to=pltpu.HBM,
-    )(*arrays, *terms)
+    )(ready_p, *arrays, *terms)
     return loss.reshape(1), grad_data, grad_param
 
 

time: 54 us -> 53.6 us (level)
    pallas_call x9 -> x10, Pallas kernels: 12.3 us -> 12.3 us  [run(): return inner(*args)]
  transfers between devices with their start and end apart: 22 -> 22, of which waited for: 8 -> 7; matrix products, arithmetic and copies ran while one was open for 0% -> 0% of each run, Pallas kernels for 13% -> 14%
where the time goes in v4:
time: 53.6 us; the launch traced here: 53.5 us
  starting transfers between devices  26.8 us (50%)
  Pallas kernels  12.3 us (23%)
  waiting for transfers between devices  12.1 us (23%)
  between operations  2.08 us (4%)
    ppermute x22, starting transfers between devices, swap(): lax.ppermute(x, ('row', 'col'), [(i, i ^ mask) for i in range(devices)])  26.8 us
    pallas_call x10, Pallas kernels, run(): return inner(*args)  12.3 us
    ppermute x22, waiting for transfers between devices, swap(): lax.ppermute(x, ('row', 'col'), [(i, i ^ mask) for i in range(devices)])  12.1 us
  transfers between devices with their start and end apart: 22, of which 7 were waited for; matrix products, arithmetic and copies ran while one was open for 0% of the time, Pallas kernels for 14%

profile of v4, /device:TPU:0, one launch (start us, length us, event | category | flops | bytes accessed | tf_op | source)
XLA Modules:
  0.0 53.5 jit_solution(13624265635804326153)
XLA Ops:
  0.6 1.2 %shard_map.85 = (bf16[208,512]{1,0:T(8,128)(2,1)S(1)}, bf16[192,512]{1,0:T(8,128)(2,1)S(1)}, bf16[16,512]{1,0:T(8,128)(2,1)S(1)}) custom-call(bf16[192,512]{1,0:T(8,128)(2,1)} %refs_0_.3, bf16[192,512]{1,0:T(8,128)(2,1)} %refs_0_.2, s32[1,192]{1,0:T(1,128)} %bitcast.5, s32[1,192]{1,0:T(1,128)} %bitcast.6), custom_call_target="tpu_custom_call" | custom-call | flops 1 | bytes 1 | tf_op jit(solution)/shard_map/pallas_call | solution.py:40
  1.9 0.1 shard_map.86.refs_0_
  2.0 3.1 %collective-permute-start = (bf16[208,512]{1,0:T(8,128)(2,1)S(1)}, bf16[208,512]{1,0:T(8,128)(2,1)S(1)}, u32[]{:S(2)}, u32[]{:S(2)}) collective-permute-start(bf16[208,512]{1,0:T(8,128)(2,1)S(1)} %shard_map.86.refs_0_), channel_id=1, source_target_pairs={{0,8},{1,9},{2,10},{3,11},{4,12},{5,13},{6,14},{7,15},{8,0},{9,1},... | collective-permute-start | bytes 638984 | tf_op jit(solution)/shard_map/ppermute | solution.py:327
  5.1 1.5 %collective-permute-start.6 = (bf16[208,512]{1,0:T(8,128)(2,1)S(1)}, bf16[208,512]{1,0:T(8,128)(2,1)S(1)}, u32[]{:S(2)}, u32[]{:S(2)}) collective-permute-start(bf16[208,512]{1,0:T(8,128)(2,1)S(1)} %shard_map.86.refs_0_), channel_id=1, source_target_pairs={{0,2},{1,3},{2,0},{3,1},{4,6},{5,7},{6,4},{7,5},{8,10},{9,11},{10,... | collective-permute-start | bytes 638984 | tf_op jit(solution)/shard_map/ppermute | solution.py:327
  6.6 2.6 %collective-permute-start.5 = (bf16[208,512]{1,0:T(8,128)(2,1)S(1)}, bf16[208,512]{1,0:T(8,128)(2,1)S(1)}, u32[]{:S(2)}, u32[]{:S(2)}) collective-permute-start(bf16[208,512]{1,0:T(8,128)(2,1)S(1)} %get-tuple-element.32.refs_4_), channel_id=1, source_target_pairs={{0,16},{1,17},{2,18},{3,19},{4,20},{5,21},{6,22},{7,23},{8,24},{9,... | collective-permute-start | bytes 638984 | tf_op jit(solution)/shard_map/ppermute | solution.py:327
  9.2 1.2 %collective-permute-done.refs_0_ = bf16[208,512]{1,0:T(8,128)(2,1)S(1)} collective-permute-done((bf16[208,512]{1,0:T(8,128)(2,1)S(1)}, bf16[208,512]{1,0:T(8,128)(2,1)S(1)}, u32[]{:S(2)}, u32[]{:S(2)}) %collective-permute-start) | collective-permute-done | bytes 213024 | tf_op jit(solution)/shard_map/ppermute | solution.py:327
  10.3 4.2 %collective-permute-start.1 = (bf16[208,512]{1,0:T(8,128)(2,1)S(1)}, bf16[208,512]{1,0:T(8,128)(2,1)S(1)}, u32[]{:S(2)}, u32[]{:S(2)}) collective-permute-start(bf16[208,512]{1,0:T(8,128)(2,1)S(1)} %collective-permute-done.refs_0_), channel_id=1, source_target_pairs={{0,2},{1,3},{2,0},{3,1},{4,6},{5,7},{6,4},{7,5},{8,10},{9,11},{10,... | collective-permute-start | bytes 638984 | tf_op jit(solution)/shard_map/ppermute | solution.py:327
  14.5 1.5 %collective-permute-start.4 = (bf16[208,512]{1,0:T(8,128)(2,1)S(1)}, bf16[208,512]{1,0:T(8,128)(2,1)S(1)}, u32[]{:S(2)}, u32[]{:S(2)}) collective-permute-start(bf16[208,512]{1,0:T(8,128)(2,1)S(1)} %get-tuple-element.32.refs_4_), channel_id=1, source_target_pairs={{0,4},{1,5},{2,6},{3,7},{4,0},{5,1},{6,2},{7,3},{8,12},{9,13},{10,... | collective-permute-start | bytes 638984 | tf_op jit(solution)/shard_map/ppermute | solution.py:327
  17.3 0.0 collective-permute-done.6.refs_1_
  17.3 0.1 collective-permute-start.2
  17.4 0.0 collective-permute-done.7.refs_2_
  17.4 0.5 collective-permute-start.8
  17.9 1.8 %collective-permute-done.5.refs_6_ = bf16[208,512]{1,0:T(8,128)(2,1)S(1)} collective-permute-done((bf16[208,512]{1,0:T(8,128)(2,1)S(1)}, bf16[208,512]{1,0:T(8,128)(2,1)S(1)}, u32[]{:S(2)}, u32[]{:S(2)}) %collective-permute-start.5) | collective-permute-done | bytes 213024 | tf_op jit(solution)/shard_map/ppermute | solution.py:327
  19.7 1.5 %collective-permute-start.9 = (bf16[208,512]{1,0:T(8,128)(2,1)S(1)}, bf16[208,512]{1,0:T(8,128)(2,1)S(1)}, u32[]{:S(2)}, u32[]{:S(2)}) collective-permute-start(bf16[208,512]{1,0:T(8,128)(2,1)S(1)} %collective-permute-done.5.refs_6_), channel_id=1, source_target_pairs={{0,4},{1,5},{2,6},{3,7},{4,0},{5,1},{6,2},{7,3},{8,12},{9,13},{10,... | collective-permute-start | bytes 638984 | tf_op jit(solution)/shard_map/ppermute | solution.py:327
  21.2 0.1 pad_add_fusion.refs_6_
  21.3 0.1 pad_maximum_fusion.refs_7_
  21.4 0.0 collective-permute-done.4.refs_5_
  21.4 2.5 %shard_map.87 = (bf16[768,512]{1,0:T(8,128)(2,1)S(1)}, f32[8,768]{1,0:T(8,128)S(1)}, f32[1152,512]{1,0:T(8,128)S(1)}, f32[8,128]{1,0:T(8,128)S(1)}) custom-call(bf16[208,512]{1,0:T(8,128)(2,1)S(1)} %shard_map.86.refs_0_, bf16[208,512]{1,0:T(8,128)(2,1)S(1)} %collective-permute-done.6.refs_1_, bf16[208,512]{1,0:T(8,128)(2,1)S(1)} %collective-permute-done.7.refs_2_, ...), custom_call_target="tpu_custom_call" | custom-call | flops 1 | bytes 1 | tf_op jit(solution)/shard_map/pallas_call | solution.py:40
  23.9 0.0 collective-permute-done.2.refs_2_
  23.9 0.0 collective-permute-done.3.refs_3_
  23.9 3.8 %shard_map.88 = (bf16[768,512]{1,0:T(8,128)(2,1)S(1)}, f32[8,768]{1,0:T(8,128)S(1)}, f32[768,512]{1,0:T(8,128)S(1)}, f32[768,512]{1,0:T(8,128)S(1)}, f32[576,512]{1,0:T(8,128)S(1)}, /*index=5*/f32[8,128]{1,0:T(8,128)S(1)}) custom-call(bf16[208,512]{1,0:T(8,128)(2,1)S(1)} %collective-permute-done.refs_0_, ...), custom_call_target="tpu_custom_call" | custom-call | flops 1 | bytes 1 | tf_op jit(solution)/shard_map/pallas_call | solution.py:40
  27.8 2.4 %shard_map.89 = (f32[768,512]{1,0:T(8,128)S(1)}, s16[416,512]{1,0:T(8,128)(2,1)S(1)}, s16[416,512]{1,0:T(8,128)(2,1)S(1)}, f32[8,128]{1,0:T(8,128)S(1)}, s16[208...) custom-call(bf16[208,512]{1,0:T(8,128)(2,1)S(1)} %collective-permute-done.9.refs_0_, ...), custom_call_target="tpu_custom_call" | custom-call | flops 1 | bytes 1 | tf_op jit(solution)/shard_map/pallas_call | solution.py:40
  30.2 0.6 %collective-permute-start.14 = (s16[416,512]{1,0:T(8,128)(2,1)S(1)}, s16[416,512]{1,0:T(8,128)(2,1)S(1)}, u32[]{:S(2)}, u32[]{:S(2)}) collective-permute-start(s16[416,512]{1,0:T(8,128)(2,1)S(1)} %get-tuple-element.47), channel_id=1, source_target_pairs={{0,1},{1,0},{2,3},{3,2},{4,5},{5,4},{6,7},{7,6},{8,9},{9,8},{10,11... | collective-permute-start | bytes 1277960 | tf_op jit(solution)/shard_map/ppermute | solution.py:327
  30.8 0.1 collective-permute-start.13
  30.9 0.5 collective-permute-start.11
  31.4 0.8 %collective-permute-done.14.refs_1_ = s16[416,512]{1,0:T(8,128)(2,1)S(1)} collective-permute-done((s16[416,512]{1,0:T(8,128)(2,1)S(1)}, s16[416,512]{1,0:T(8,128)(2,1)S(1)}, u32[]{:S(2)}, u32[]{:S(2)}) %collective-permute-start.14) | collective-permute-done | bytes 426016 | tf_op jit(solution)/shard_map/ppermute | solution.py:327
  32.2 0.3 shard_map.92
  32.5 0.7 %collective-permute-start.16 = (s16[208,512]{1,0:T(8,128)(2,1)S(1)}, s16[208,512]{1,0:T(8,128)(2,1)S(1)}, u32[]{:S(2)}, u32[]{:S(2)}) collective-permute-start(s16[208,512]{1,0:T(8,128)(2,1)S(1)} %get-tuple-element.50), channel_id=1, source_target_pairs={{0,2},{1,3},{2,0},{3,1},{4,6},{5,7},{6,4},{7,5},{8,10},{9,11},{10,... | collective-permute-start | bytes 638984 | tf_op jit(solution)/shard_map/ppermute | solution.py:327
  33.2 0.7 %collective-permute-start.17 = (f32[8,128]{1,0:T(8,128)S(1)}, f32[8,128]{1,0:T(8,128)S(1)}, u32[]{:S(2)}, u32[]{:S(2)}) collective-permute-start(f32[8,128]{1,0:T(8,128)S(1)} %get-tuple-element.51.refs_3_), channel_id=1, source_target_pairs={{0,4},{1,5},{2,6},{3,7},{4,0},{5,1},{6,2},{7,3},{8,12},{9,13},{10,... | collective-permute-start | bytes 12296 | tf_op jit(solution)/shard_map/ppermute | solution.py:327
  33.9 2.2 %collective-permute-start.18 = (f32[8,128]{1,0:T(8,128)S(1)}, f32[8,128]{1,0:T(8,128)S(1)}, u32[]{:S(2)}, u32[]{:S(2)}) collective-permute-start(f32[8,128]{1,0:T(8,128)S(1)} %get-tuple-element.51.refs_3_), channel_id=1, source_target_pairs={{0,6},{1,7},{2,4},{3,5},{4,2},{5,3},{6,0},{7,1},{8,14},{9,15},{10,... | collective-permute-start | bytes 12296 | tf_op jit(solution)/shard_map/ppermute | solution.py:327
  36.1 2.4 %collective-permute-done.11.refs_1_ = s16[208,512]{1,0:T(8,128)(2,1)S(1)} collective-permute-done((s16[208,512]{1,0:T(8,128)(2,1)S(1)}, s16[208,512]{1,0:T(8,128)(2,1)S(1)}, u32[]{:S(2)}, u32[]{:S(2)}) %collective-permute-start.11) | collective-permute-done | bytes 213024 | tf_op jit(solution)/shard_map/ppermute | solution.py:327
  38.5 0.5 collective-permute-start.10
  39.0 0.2 shard_map.90
  39.2 0.0 collective-permute-done.13.refs_1_.refs_2_
  39.2 0.8 %collective-permute-start.12 = (s16[208,512]{1,0:T(8,128)(2,1)S(1)}, s16[208,512]{1,0:T(8,128)(2,1)S(1)}, u32[]{:S(2)}, u32[]{:S(2)}) collective-permute-start(s16[208,512]{1,0:T(8,128)(2,1)S(1)} %shard_map.90), channel_id=1, source_target_pairs={{0,16},{1,17},{2,18},{3,19},{4,20},{5,21},{6,22},{7,23},{8,24},{9,... | collective-permute-start | bytes 638984 | tf_op jit(solution)/shard_map/ppermute | solution.py:327
  40.0 0.0 collective-permute-done.17.refs_4_
  40.0 0.6 %collective-permute-start.15 = (s16[208,512]{1,0:T(8,128)(2,1)S(1)}, s16[208,512]{1,0:T(8,128)(2,1)S(1)}, u32[]{:S(2)}, u32[]{:S(2)}) collective-permute-start(s16[208,512]{1,0:T(8,128)(2,1)S(1)} %get-tuple-element.49), channel_id=1, source_target_pairs={{0,2},{1,3},{2,0},{3,1},{4,6},{5,7},{6,4},{7,5},{8,10},{9,11},{10,... | collective-permute-start | bytes 638984 | tf_op jit(solution)/shard_map/ppermute | solution.py:327
  40.6 0.2 shard_map.93
  40.9 0.0 copy-start.1
  40.9 2.6 %collective-permute-start.19 = (s16[208,512]{1,0:T(8,128)(2,1)S(1)}, s16[208,512]{1,0:T(8,128)(2,1)S(1)}, u32[]{:S(2)}, u32[]{:S(2)}) collective-permute-start(s16[208,512]{1,0:T(8,128)(2,1)S(1)} %get-tuple-element.52), channel_id=1, source_target_pairs={{0,8},{1,9},{2,10},{3,11},{4,12},{5,13},{6,14},{7,15},{8,0},{9,1},... | collective-permute-start | bytes 638984 | tf_op jit(solution)/shard_map/ppermute | solution.py:327
  43.5 0.1 collective-permute-start.20
  43.6 1.7 %collective-permute-done.10.refs_2_ = s16[208,512]{1,0:T(8,128)(2,1)S(1)} collective-permute-done((s16[208,512]{1,0:T(8,128)(2,1)S(1)}, s16[208,512]{1,0:T(8,128)(2,1)S(1)}, u32[]{:S(2)}, u32[]{:S(2)}) %collective-permute-start.10) | collective-permute-done | bytes 213024 | tf_op jit(solution)/shard_map/ppermute | solution.py:327
  45.3 2.5 %collective-permute-start.21 = (f32[8,128]{1,0:T(8,128)S(1)}, f32[8,128]{1,0:T(8,128)S(1)}, u32[]{:S(2)}, u32[]{:S(2)}) collective-permute-start(f32[8,128]{1,0:T(8,128)S(1)} %get-tuple-element.53.refs_5_), channel_id=1, source_target_pairs={{0,24},{1,25},{2,26},{3,27},{4,28},{5,29},{6,30},{7,31},{8,16},{9,... | collective-permute-start | bytes 12296 | tf_op jit(solution)/shard_map/ppermute | solution.py:327
  47.8 3.3 %collective-permute-done.12.refs_3_ = s16[208,512]{1,0:T(8,128)(2,1)S(1)} collective-permute-done((s16[208,512]{1,0:T(8,128)(2,1)S(1)}, s16[208,512]{1,0:T(8,128)(2,1)S(1)}, u32[]{:S(2)}, u32[]{:S(2)}) %collective-permute-start.12) | collective-permute-done | bytes 213024 | tf_op jit(solution)/shard_map/ppermute | solution.py:327
  51.2 0.3 shard_map.91.ready
  51.5 0.0 collective-permute-done.15.refs_3_
  51.5 0.9 %collective-permute-done.19.refs_4_ = s16[208,512]{1,0:T(8,128)(2,1)S(1)} collective-permute-done((s16[208,512]{1,0:T(8,128)(2,1)S(1)}, s16[208,512]{1,0:T(8,128)(2,1)S(1)}, u32[]{:S(2)}, u32[]{:S(2)}) %collective-permute-start.19) | collective-permute-done | bytes 213024 | tf_op jit(solution)/shard_map/ppermute | solution.py:327
  52.4 1.1 %shard_map.94 = (f32[192,512]{1,0:T(8,128)}, f32[192,512]{1,0:T(8,128)}, f32[1,1]{1,0:T(1,128)}) custom-call(f32[192,512]{1,0:T(8,128)S(1)} %shard_map.91.ready, bf16[192,512]{1,0:T(8,128)(2,1)S(1)} %copy-done.1, f32[768,512]{1,0:T(8,128)S(1)} %get-tuple-element.45.refs_0_.refs_1_, s16[416,512]{1,0:T(8,128)(2,1)S(1)} %collective-permute-done.13.refs_1_.refs_2_, ...), custom_call_target="tpu_custom_call" | custom-call | flops 1 | bytes 1 | tf_op jit(solution)/shard_map/pallas_call | solution.py:40
  (12 shorter events, 0.0 us)
Async XLA Ops:
  2.0 8.3 %collective-permute-start = (bf16[208,512]{1,0:T(8,128)(2,1)S(1)}, bf16[208,512]{1,0:T(8,128)(2,1)S(1)}, u32[]{:S(2)}, u32[]{:S(2)}) collective-permute-start(bf16[208,512]{1,0:T(8,128)(2,1)S(1)} %shard_map.86.refs_0_), channel_id=1, source_target_pairs={{0,8},{1,9},{2,10},{3,11},{4,12},{5,13},{6,14},{7,15},{8,0},{9,1},... | collective-permute-start | bytes 638984 | tf_op jit(solution)/shard_map/ppermute | solution.py:327
  5.1 12.3 %collective-permute-start.6 = (bf16[208,512]{1,0:T(8,128)(2,1)S(1)}, bf16[208,512]{1,0:T(8,128)(2,1)S(1)}, u32[]{:S(2)}, u32[]{:S(2)}) collective-permute-start(bf16[208,512]{1,0:T(8,128)(2,1)S(1)} %shard_map.86.refs_0_), channel_id=1, source_target_pairs={{0,2},{1,3},{2,0},{3,1},{4,6},{5,7},{6,4},{7,5},{8,10},{9,11},{10,... | collective-permute-start | bytes 638984 | tf_op jit(solution)/shard_map/ppermute | solution.py:327
  6.6 10.9 %collective-permute-start.7 = (bf16[208,512]{1,0:T(8,128)(2,1)S(1)}, bf16[208,512]{1,0:T(8,128)(2,1)S(1)}, u32[]{:S(2)}, u32[]{:S(2)}) collective-permute-start(bf16[208,512]{1,0:T(8,128)(2,1)S(1)} %shard_map.86.refs_0_), channel_id=1, source_target_pairs={{0,1},{1,0},{2,3},{3,2},{4,5},{5,4},{6,7},{7,6},{8,9},{9,8},{10,11... | collective-permute-start | bytes 638984 | tf_op jit(solution)/shard_map/ppermute | solution.py:327
  6.6 13.1 %collective-permute-start.5 = (bf16[208,512]{1,0:T(8,128)(2,1)S(1)}, bf16[208,512]{1,0:T(8,128)(2,1)S(1)}, u32[]{:S(2)}, u32[]{:S(2)}) collective-permute-start(bf16[208,512]{1,0:T(8,128)(2,1)S(1)} %get-tuple-element.32.refs_4_), channel_id=1, source_target_pairs={{0,16},{1,17},{2,18},{3,19},{4,20},{5,21},{6,22},{7,23},{8,24},{9,... | collective-permute-start | bytes 638984 | tf_op jit(solution)/shard_map/ppermute | solution.py:327
  10.3 10.9 %collective-permute-start.1 = (bf16[208,512]{1,0:T(8,128)(2,1)S(1)}, bf16[208,512]{1,0:T(8,128)(2,1)S(1)}, u32[]{:S(2)}, u32[]{:S(2)}) collective-permute-start(bf16[208,512]{1,0:T(8,128)(2,1)S(1)} %collective-permute-done.refs_0_), channel_id=1, source_target_pairs={{0,2},{1,3},{2,0},{3,1},{4,6},{5,7},{6,4},{7,5},{8,10},{9,11},{10,... | collective-permute-start | bytes 638984 | tf_op jit(solution)/shard_map/ppermute | solution.py:327
  14.5 6.9 %collective-permute-start.4 = (bf16[208,512]{1,0:T(8,128)(2,1)S(1)}, bf16[208,512]{1,0:T(8,128)(2,1)S(1)}, u32[]{:S(2)}, u32[]{:S(2)}) collective-permute-start(bf16[208,512]{1,0:T(8,128)(2,1)S(1)} %get-tuple-element.32.refs_4_), channel_id=1, source_target_pairs={{0,4},{1,5},{2,6},{3,7},{4,0},{5,1},{6,2},{7,3},{8,12},{9,13},{10,... | collective-permute-start | bytes 638984 | tf_op jit(solution)/shard_map/ppermute | solution.py:327
  17.3 6.6 %collective-permute-start.2 = (bf16[208,512]{1,0:T(8,128)(2,1)S(1)}, bf16[208,512]{1,0:T(8,128)(2,1)S(1)}, u32[]{:S(2)}, u32[]{:S(2)}) collective-permute-start(bf16[208,512]{1,0:T(8,128)(2,1)S(1)} %collective-permute-done.refs_0_), channel_id=1, source_target_pairs={{0,1},{1,0},{2,3},{3,2},{4,5},{5,4},{6,7},{7,6},{8,9},{9,8},{10,11... | collective-permute-start | bytes 638984 | tf_op jit(solution)/shard_map/ppermute | solution.py:327
  17.4 3.9 %collective-permute-start.8 = (bf16[208,512]{1,0:T(8,128)(2,1)S(1)}, bf16[208,512]{1,0:T(8,128)(2,1)S(1)}, u32[]{:S(2)}, u32[]{:S(2)}) collective-permute-start(bf16[208,512]{1,0:T(8,128)(2,1)S(1)} %collective-permute-done.6.refs_1_), channel_id=1, source_target_pairs={{0,1},{1,0},{2,3},{3,2},{4,5},{5,4},{6,7},{7,6},{8,9},{9,8},{10,11... | collective-permute-start | bytes 638984 | tf_op jit(solution)/shard_map/ppermute | solution.py:327
  19.7 8.1 %collective-permute-start.9 = (bf16[208,512]{1,0:T(8,128)(2,1)S(1)}, bf16[208,512]{1,0:T(8,128)(2,1)S(1)}, u32[]{:S(2)}, u32[]{:S(2)}) collective-permute-start(bf16[208,512]{1,0:T(8,128)(2,1)S(1)} %collective-permute-done.5.refs_6_), channel_id=1, source_target_pairs={{0,4},{1,5},{2,6},{3,7},{4,0},{5,1},{6,2},{7,3},{8,12},{9,13},{10,... | collective-permute-start | bytes 638984 | tf_op jit(solution)/shard_map/ppermute | solution.py:327
  21.2 2.7 %collective-permute-start.3 = (bf16[208,512]{1,0:T(8,128)(2,1)S(1)}, bf16[208,512]{1,0:T(8,128)(2,1)S(1)}, u32[]{:S(2)}, u32[]{:S(2)}) collective-permute-start(bf16[208,512]{1,0:T(8,128)(2,1)S(1)} %collective-permute-done.1.refs_1_), channel_id=1, source_target_pairs={{0,1},{1,0},{2,3},{3,2},{4,5},{5,4},{6,7},{7,6},{8,9},{9,8},{10,11... | collective-permute-start | bytes 638984 | tf_op jit(solution)/shard_map/ppermute | solution.py:327
  30.2 2.0 %collective-permute-start.14 = (s16[416,512]{1,0:T(8,128)(2,1)S(1)}, s16[416,512]{1,0:T(8,128)(2,1)S(1)}, u32[]{:S(2)}, u32[]{:S(2)}) collective-permute-start(s16[416,512]{1,0:T(8,128)(2,1)S(1)} %get-tuple-element.47), channel_id=1, source_target_pairs={{0,1},{1,0},{2,3},{3,2},{4,5},{5,4},{6,7},{7,6},{8,9},{9,8},{10,11... | collective-permute-start | bytes 1277960 | tf_op jit(solution)/shard_map/ppermute | solution.py:327
  30.8 8.4 %collective-permute-start.13 = (s16[416,512]{1,0:T(8,128)(2,1)S(1)}, s16[416,512]{1,0:T(8,128)(2,1)S(1)}, u32[]{:S(2)}, u32[]{:S(2)}) collective-permute-start(s16[416,512]{1,0:T(8,128)(2,1)S(1)} %get-tuple-element.46), channel_id=1, source_target_pairs={{0,1},{1,0},{2,3},{3,2},{4,5},{5,4},{6,7},{7,6},{8,9},{9,8},{10,11... | collective-permute-start | bytes 1277960 | tf_op jit(solution)/shard_map/ppermute | solution.py:327
  30.9 7.6 %collective-permute-start.11 = (s16[208,512]{1,0:T(8,128)(2,1)S(1)}, s16[208,512]{1,0:T(8,128)(2,1)S(1)}, u32[]{:S(2)}, u32[]{:S(2)}) collective-permute-start(s16[208,512]{1,0:T(8,128)(2,1)S(1)} %get-tuple-element.44), channel_id=1, source_target_pairs={{0,4},{1,5},{2,6},{3,7},{4,0},{5,1},{6,2},{7,3},{8,12},{9,13},{10,... | collective-permute-start | bytes 638984 | tf_op jit(solution)/shard_map/ppermute | solution.py:327
  32.5 8.1 %collective-permute-start.16 = (s16[208,512]{1,0:T(8,128)(2,1)S(1)}, s16[208,512]{1,0:T(8,128)(2,1)S(1)}, u32[]{:S(2)}, u32[]{:S(2)}) collective-permute-start(s16[208,512]{1,0:T(8,128)(2,1)S(1)} %get-tuple-element.50), channel_id=1, source_target_pairs={{0,2},{1,3},{2,0},{3,1},{4,6},{5,7},{6,4},{7,5},{8,10},{9,11},{10,... | collective-permute-start | bytes 638984 | tf_op jit(solution)/shard_map/ppermute | solution.py:327
  33.2 6.9 %collective-permute-start.17 = (f32[8,128]{1,0:T(8,128)S(1)}, f32[8,128]{1,0:T(8,128)S(1)}, u32[]{:S(2)}, u32[]{:S(2)}) collective-permute-start(f32[8,128]{1,0:T(8,128)S(1)} %get-tuple-element.51.refs_3_), channel_id=1, source_target_pairs={{0,4},{1,5},{2,6},{3,7},{4,0},{5,1},{6,2},{7,3},{8,12},{9,13},{10,... | collective-permute-start | bytes 12296 | tf_op jit(solution)/shard_map/ppermute | solution.py:327
  33.9 6.7 %collective-permute-start.18 = (f32[8,128]{1,0:T(8,128)S(1)}, f32[8,128]{1,0:T(8,128)S(1)}, u32[]{:S(2)}, u32[]{:S(2)}) collective-permute-start(f32[8,128]{1,0:T(8,128)S(1)} %get-tuple-element.51.refs_3_), channel_id=1, source_target_pairs={{0,6},{1,7},{2,4},{3,5},{4,2},{5,3},{6,0},{7,1},{8,14},{9,15},{10,... | collective-permute-start | bytes 12296 | tf_op jit(solution)/shard_map/ppermute | solution.py:327
  38.5 12.6 %copy-start = (bf16[192,512]{1,0:T(8,128)(2,1)S(1)}, bf16[192,512]{1,0:T(8,128)(2,1)}, u32[]{:S(2)}) copy-start(bf16[192,512]{1,0:T(8,128)(2,1)} %refs_0_.2) | copy-start | bytes 589828
  38.5 6.8 %collective-permute-start.10 = (s16[208,512]{1,0:T(8,128)(2,1)S(1)}, s16[208,512]{1,0:T(8,128)(2,1)S(1)}, u32[]{:S(2)}, u32[]{:S(2)}) collective-permute-start(s16[208,512]{1,0:T(8,128)(2,1)S(1)} %get-tuple-element.43), channel_id=1, source_target_pairs={{0,4},{1,5},{2,6},{3,7},{4,0},{5,1},{6,2},{7,3},{8,12},{9,13},{10,... | collective-permute-start | bytes 638984 | tf_op jit(solution)/shard_map/ppermute | solution.py:327
  39.2 11.9 %collective-permute-start.12 = (s16[208,512]{1,0:T(8,128)(2,1)S(1)}, s16[208,512]{1,0:T(8,128)(2,1)S(1)}, u32[]{:S(2)}, u32[]{:S(2)}) collective-permute-start(s16[208,512]{1,0:T(8,128)(2,1)S(1)} %shard_map.90), channel_id=1, source_target_pairs={{0,16},{1,17},{2,18},{3,19},{4,20},{5,21},{6,22},{7,23},{8,24},{9,... | collective-permute-start | bytes 638984 | tf_op jit(solution)/shard_map/ppermute | solution.py:327
  40.0 11.4 %collective-permute-start.15 = (s16[208,512]{1,0:T(8,128)(2,1)S(1)}, s16[208,512]{1,0:T(8,128)(2,1)S(1)}, u32[]{:S(2)}, u32[]{:S(2)}) collective-permute-start(s16[208,512]{1,0:T(8,128)(2,1)S(1)} %get-tuple-element.49), channel_id=1, source_target_pairs={{0,2},{1,3},{2,0},{3,1},{4,6},{5,7},{6,4},{7,5},{8,10},{9,11},{10,... | collective-permute-start | bytes 638984 | tf_op jit(solution)/shard_map/ppermute | solution.py:327
  40.9 11.5 %copy-start.1 = (bf16[192,512]{1,0:T(8,128)(2,1)S(1)}, bf16[192,512]{1,0:T(8,128)(2,1)}, u32[]{:S(2)}) copy-start(bf16[192,512]{1,0:T(8,128)(2,1)} %refs_0_.3) | copy-start | bytes 589828
  40.9 11.5 %collective-permute-start.19 = (s16[208,512]{1,0:T(8,128)(2,1)S(1)}, s16[208,512]{1,0:T(8,128)(2,1)S(1)}, u32[]{:S(2)}, u32[]{:S(2)}) collective-permute-start(s16[208,512]{1,0:T(8,128)(2,1)S(1)} %get-tuple-element.52), channel_id=1, source_target_pairs={{0,8},{1,9},{2,10},{3,11},{4,12},{5,13},{6,14},{7,15},{8,0},{9,1},... | collective-permute-start | bytes 638984 | tf_op jit(solution)/shard_map/ppermute | solution.py:327
  43.5 7.9 %collective-permute-start.20 = (f32[8,128]{1,0:T(8,128)S(1)}, f32[8,128]{1,0:T(8,128)S(1)}, u32[]{:S(2)}, u32[]{:S(2)}) collective-permute-start(f32[8,128]{1,0:T(8,128)S(1)} %get-tuple-element.53.refs_5_), channel_id=1, source_target_pairs={{0,16},{1,17},{2,18},{3,19},{4,20},{5,21},{6,22},{7,23},{8,24},{9,... | collective-permute-start | bytes 12296 | tf_op jit(solution)/shard_map/ppermute | solution.py:327
  45.3 6.2 %collective-permute-start.21 = (f32[8,128]{1,0:T(8,128)S(1)}, f32[8,128]{1,0:T(8,128)S(1)}, u32[]{:S(2)}, u32[]{:S(2)}) collective-permute-start(f32[8,128]{1,0:T(8,128)S(1)} %get-tuple-element.53.refs_5_), channel_id=1, source_target_pairs={{0,24},{1,25},{2,26},{3,27},{4,28},{5,29},{6,30},{7,31},{8,16},{9,... | collective-permute-start | bytes 12296 | tf_op jit(solution)/shard_map/ppermute | solution.py:327
